TPU v7x, 32 devices: a whole 2x2x4 slice. The times are simulated.
32 devices in a mesh: dp: 4 (over y, x), ctx: 8 (over z, core).
Axes of the slice: x: 2, y: 2, z: 4, core: 2. Of those that a mesh axis runs over, the one named last changes fastest.
Arguments:
- queries: bfloat16 [8, 512, 2560], P('ctx', 'dp'), may hold values from -20 to 20
- key_states: bfloat16 [8, 512, 2560], P('ctx', 'dp'), may hold values from -20 to 20
- values: bfloat16 [8, 512, 2560], P('ctx', 'dp'), may hold values from -6 to 6
- out_grad: bfloat16 [8, 512, 2560], P('ctx', 'dp'), may hold values from -6 to 6
- block_links: int32 [2, 4], P(None, 'dp'), may hold values from -1 to 2, as said below
- sink_logit: float32 [20], replicated, may hold values from 4 to 8
Outputs:
- query_grad: bfloat16 [8, 512, 2560], P('ctx', 'dp')
- key_grad: bfloat16 [8, 512, 2560], P('ctx', 'dp')
- value_grad: bfloat16 [8, 512, 2560], P('ctx', 'dp')
- sink_grad: float32 [20], replicated
Inputs may be any that keep to these rules, and one draw needn't show every extreme that they name: block_links[j, b] is either -1 or b - 2**j; it is -1 wherever b - 2**j < 0; block_links[0, 3] is 2.
All inputs are finite; a program needn't handle non-finite values.
Results may differ from a plain program's by a relative error of at most 0.023.
Values may be sent and summed in bfloat16 or wider, within the bound.
No kernel may reach another device: no remote copies, remote signals or barrier semaphores. Data moves between devices by JAX's collectives and lax.ppermute only.
A program may use at most 64 MiB of HBM per device.

v0:
```python
import jax
import jax.numpy as jnp
from jax import lax
from jax.sharding import PartitionSpec as P

BLOCK = 128
LEVELS = 2


NEG_FILL = -1e30


def from_behind(value, axis, steps):
    count = lax.axis_size(axis)
    initial, last = (max(0, -steps), min(count, count - steps))
    return lax.ppermute(value, axis, [(source, source + steps) for source in range(initial, last)])


def causal_table(block_len):
    rows_iota = lax.broadcasted_iota(jnp.int32, (block_len, block_len), 0)
    cols_iota = lax.broadcasted_iota(jnp.int32, (block_len, block_len), 1)
    return rows_iota >= cols_iota


def attend_forward(q_blocks, key_all, val_all, allowed, sink_logit, score_scale):
    scores = (
        jnp.einsum("bqhd,bkhd->bhqk", q_blocks, key_all, preferred_element_type=jnp.float32)
        * score_scale
    )
    scores = jnp.where(allowed[:, None], scores, NEG_FILL)
    row_max = jnp.maximum(jnp.max(scores, axis=-1), sink_logit[None, :, None])
    exp_scores = jnp.exp(scores - row_max[..., None])
    sink_exp = jnp.exp(sink_logit[None, :, None] - row_max)
    denominator = jnp.sum(exp_scores, axis=-1) + sink_exp
    soft_prob = exp_scores / denominator[..., None]
    sink_prob = sink_exp / denominator
    weights = soft_prob.astype(jnp.bfloat16)
    output = jnp.einsum(
        "bhqk,bkhd->bqhd", weights, val_all, preferred_element_type=jnp.float32
    ).astype(jnp.bfloat16)
    return (soft_prob, weights, sink_prob, output)


def attend_backward(
    q_blocks, key_all, val_all, grad_blocks, soft_prob, weights, sink_prob, output, score_scale
):
    row_delta = jnp.sum(grad_blocks.astype(jnp.float32) * output.astype(jnp.float32), axis=-1)
    row_delta = jnp.transpose(row_delta, (0, 2, 1))
    prob_grad = jnp.einsum(
        "bqhd,bkhd->bhqk", grad_blocks, val_all, preferred_element_type=jnp.float32
    )
    score_grad = (soft_prob * (prob_grad - row_delta[..., None])).astype(jnp.bfloat16)
    query_grad = (
        jnp.einsum("bhqk,bkhd->bqhd", score_grad, key_all, preferred_element_type=jnp.float32)
        * score_scale
    ).astype(jnp.bfloat16)
    key_terms = (
        jnp.einsum("bhqk,bqhd->bkhd", score_grad, q_blocks, preferred_element_type=jnp.float32)
        * score_scale
    )
    value_terms = jnp.einsum(
        "bhqk,bqhd->bkhd", weights, grad_blocks, preferred_element_type=jnp.float32
    )
    sink_term = -jnp.sum(sink_prob * row_delta, axis=(0, 2))
    return (query_grad, key_terms, value_terms, sink_term)


def body(queries, key_states, values, out_grad, block_links, sink_logit):
    tokens = queries.shape[1]
    width = queries.shape[2]
    blocks = tokens // BLOCK
    heads = sink_logit.shape[0]
    head_size = width // heads
    score_scale = head_size ** (-0.5)

    def to_blocks(array):
        return array.reshape(blocks, BLOCK, heads, head_size)

    q_blocks = to_blocks(queries)
    grad_blocks = to_blocks(out_grad)
    level_live = block_links >= 0
    causal = jnp.broadcast_to(causal_table(BLOCK), (blocks, BLOCK, BLOCK))
    remote_masks = [
        jnp.broadcast_to(level_live[level_num][:, None, None], (blocks, BLOCK, BLOCK))
        for level_num in range(LEVELS)
    ]
    allowed = jnp.concatenate([causal] + remote_masks, axis=2)
    fetched = []
    for level_num in range(LEVELS):
        fetched.append(from_behind((key_states, values), "dp", 2**level_num))
    key_all = jnp.concatenate(
        [to_blocks(key_states)] + [to_blocks(moved[0]) for moved in fetched], axis=1
    )
    val_all = jnp.concatenate(
        [to_blocks(values)] + [to_blocks(moved[1]) for moved in fetched], axis=1
    )
    soft_prob, weights, sink_prob, output = attend_forward(
        q_blocks, key_all, val_all, allowed, sink_logit, score_scale
    )
    refetched = []
    for level_num in range(LEVELS):
        refetched.append(from_behind((key_states, values), "dp", 2**level_num))
    key_all = jnp.concatenate(
        [to_blocks(key_states)] + [to_blocks(moved[0]) for moved in refetched], axis=1
    )
    val_all = jnp.concatenate(
        [to_blocks(values)] + [to_blocks(moved[1]) for moved in refetched], axis=1
    )
    query_grad, key_terms, value_terms, sink_term = attend_backward(
        q_blocks, key_all, val_all, grad_blocks, soft_prob, weights, sink_prob, output, score_scale
    )
    key_grad = key_terms[:, :BLOCK].reshape(1, tokens, width)
    value_grad = value_terms[:, :BLOCK].reshape(1, tokens, width)
    for level_num in range(LEVELS):
        first_col = BLOCK * (1 + level_num)
        key_part = (
            key_terms[:, first_col : first_col + BLOCK]
            .reshape(1, tokens, width)
            .astype(jnp.bfloat16)
        )
        value_part = (
            value_terms[:, first_col : first_col + BLOCK]
            .reshape(1, tokens, width)
            .astype(jnp.bfloat16)
        )
        key_back, value_back = from_behind((key_part, value_part), "dp", -(2**level_num))
        key_grad = key_grad + key_back.astype(jnp.float32)
        value_grad = value_grad + value_back.astype(jnp.float32)
    sink_grad = lax.psum(sink_term, ("dp", "ctx"))
    return (
        query_grad.reshape(1, tokens, width),
        key_grad.astype(jnp.bfloat16),
        value_grad.astype(jnp.bfloat16),
        sink_grad,
    )


def solution(mesh):
    placed = (
        P("ctx", "dp", None),
        P("ctx", "dp", None),
        P("ctx", "dp", None),
        P("ctx", "dp", None),
        P(None, "dp"),
        P(),
    )
    return jax.shard_map(
        body,
        mesh=mesh,
        in_specs=placed,
        out_specs=(P("ctx", "dp", None), P("ctx", "dp", None), P("ctx", "dp", None), P()),
        check_vma=False,
    )
```

profile of v0, /device:TPU:2, one launch (start us, length us, event | category | flops | bytes accessed | tf_op | source)
XLA Modules:
  0.0 183.5 jit_solution(4771667972555147948)
XLA Ops:
  0.7 1.5 copy.34
  2.1 4.4 %collective-permute-start.3 = (bf16[1,128,2560]{1,2,0:T(8,128)(2,1)S(1)}, bf16[1,128,2560]{1,2,0:T(8,128)(2,1)}, u32[]{:S(2)}, u32[]{:S(2)}) collective-permute-start(bf16[1,128,2560]{1,2,0:T(8,128)(2,1)S(1)} %copy.34), channel_id=1, source_target_pairs={{0,16},{8,24},{1,17},{9,25},{2,18},{10,26},{3,19},{11,27},{4,20},{... | collective-permute-start | bytes 1966088 | tf_op jit(solution)/shard_map/ppermute | solution.py:16
  6.6 1.9 %collective-permute-start.2 = (bf16[1,128,2560]{1,2,0:T(8,128)(2,1)S(1)}, bf16[1,128,2560]{1,2,0:T(8,128)(2,1)}, u32[]{:S(2)}, u32[]{:S(2)}) collective-permute-start(bf16[1,128,2560]{1,2,0:T(8,128)(2,1)S(1)} %copy.34), channel_id=1, source_target_pairs={{0,8},{8,16},{16,24},{1,9},{9,17},{17,25},{2,10},{10,18},{18,26},{... | collective-permute-start | bytes 1966088 | tf_op jit(solution)/shard_map/ppermute | solution.py:16
  9.9 2.1 %collective-permute-start.1 = (bf16[1,128,2560]{1,2,0:T(8,128)(2,1)S(1)}, bf16[1,128,2560]{1,2,0:T(8,128)(2,1)}, u32[]{:S(2)}, u32[]{:S(2)}) collective-permute-start(bf16[1,128,2560]{1,2,0:T(8,128)(2,1)S(1)} %copy.26), channel_id=1, source_target_pairs={{0,16},{8,24},{1,17},{9,25},{2,18},{10,26},{3,19},{11,27},{4,20},{... | collective-permute-start | bytes 1966088 | tf_op jit(solution)/shard_map/ppermute | solution.py:16
  12.0 1.9 %collective-permute-start = (bf16[1,128,2560]{1,2,0:T(8,128)(2,1)S(1)}, bf16[1,128,2560]{1,2,0:T(8,128)(2,1)}, u32[]{:S(2)}, u32[]{:S(2)}) collective-permute-start(bf16[1,128,2560]{1,2,0:T(8,128)(2,1)S(1)} %copy.26), channel_id=1, source_target_pairs={{0,8},{8,16},{16,24},{1,9},{9,17},{17,25},{2,10},{10,18},{18,26},{... | collective-permute-start | bytes 1966088 | tf_op jit(solution)/shard_map/ppermute | solution.py:16
  21.4 2.2 %copy.39 = bf16[1,128,20,128]{3,1,2,0:T(8,128)(2,1)} copy(bf16[1,128,20,128]{1,3,2,0:T(8,128)(2,1)} %bitcast.11) | data formatting | bytes 1310720 | tf_op jit(solution)/shard_map/reshape | solution.py:77
  23.6 2.6 %collective-permute-done.2 = bf16[1,128,2560]{1,2,0:T(8,128)(2,1)} collective-permute-done((bf16[1,128,2560]{1,2,0:T(8,128)(2,1)S(1)}, bf16[1,128,2560]{1,2,0:T(8,128)(2,1)}, u32[]{:S(2)}, u32[]{:S(2)}) %collective-permute-start.2) | collective-permute-done | bytes 655392 | tf_op jit(solution)/shard_map/ppermute | solution.py:16
  26.2 2.2 %copy.38 = bf16[1,128,20,128]{3,1,2,0:T(8,128)(2,1)} copy(bf16[1,128,20,128]{1,3,2,0:T(8,128)(2,1)} %bitcast.10) | data formatting | bytes 1310720 | tf_op jit(solution)/shard_map/reshape | solution.py:77
  28.4 5.4 %collective-permute-done.1 = bf16[1,128,2560]{1,2,0:T(8,128)(2,1)} collective-permute-done((bf16[1,128,2560]{1,2,0:T(8,128)(2,1)S(1)}, bf16[1,128,2560]{1,2,0:T(8,128)(2,1)}, u32[]{:S(2)}, u32[]{:S(2)}) %collective-permute-start.1) | collective-permute-done | bytes 655392 | tf_op jit(solution)/shard_map/ppermute | solution.py:16
  35.1 3.6 %collective-permute-done = bf16[1,128,2560]{1,2,0:T(8,128)(2,1)} collective-permute-done((bf16[1,128,2560]{1,2,0:T(8,128)(2,1)S(1)}, bf16[1,128,2560]{1,2,0:T(8,128)(2,1)}, u32[]{:S(2)}, u32[]{:S(2)}) %collective-permute-start) | collective-permute-done | bytes 655392 | tf_op jit(solution)/shard_map/ppermute | solution.py:16
  44.3 1.9 %fusion.6 = f32[128,20]{0,1:T(8,128)S(1)} fusion(f32[1,128,20,128]{1,3,2,0:T(8,128)S(1)} %bitcast.121, bf16[1,128,20,128]{3,1,2,0:T(8,128)(2,1)S(1)} %copy-done.7, bf16[1,128,20,128]{3,1,2,0:T(8,128)(2,1)S(1)} %copy-done.8, bf16[1,128,20,128]{3,1,2,0:T(8,128)(2,1)S(1)} %copy-done.6, f32[20,384,128]{2,1,0:T(8,128)S(1)} %get-tuple-element.19, ...), kind=kOutput, calls=%fused_computation.16 | convolution fusion | flops 263779840 | bytes 7288832 | tf_op jit(solution)/shard_map/bhqk,bkhd->bqhd/dot_general | solution.py:38
  46.4 1.6 fusion
  48.0 1.6 fusion.4
  49.6 2.5 %fusion.28 = (bf16[1,384,20,128]{3,1,2,0:T(8,128)(2,1)S(1)}, f32[1,384,20,128]{3,1,2,0:T(8,128)}) fusion(bf16[20,128,384]{1,2,0:T(8,128)(2,1)S(1)} %fusion, bf16[128,20,128]{0,2,1:T(8,128)(2,1)S(1)} %bitcast.116), kind=kOutput, calls=%fused_computation.43 | convolution fusion | flops 253624320 | bytes 8519680 | tf_op jit(solution)/shard_map/bhqk,bqhd->bkhd/dot_general | solution.py:58
  52.2 65.6 %psum.7 = f32[20]{0:T(128)} all-reduce(f32[20]{0:T(128)S(1)} %neg.3), channel_id=1, replica_groups=mesh['dp'=4,'ctx'=8] {'dp','ctx'}, use_global_device_ids=true, to_apply=%region_4.5 | all-reduce | flops 20 | bytes 160 | tf_op jit(solution)/shard_map/psum | solution.py:129
  121.7 1.9 %collective-permute-start.4 = (bf16[1,128,2560]{1,2,0:T(8,128)(2,1)S(1)}, bf16[1,128,2560]{1,2,0:T(8,128)(2,1)}, u32[]{:S(2)}, u32[]{:S(2)}) collective-permute-start(bf16[1,128,2560]{1,2,0:T(8,128)(2,1)S(1)} %bitcast.124), channel_id=1, source_target_pairs={{8,0},{16,8},{24,16},{9,1},{17,9},{25,17},{10,2},{18,10},{26,18},{... | collective-permute-start | bytes 1966088 | tf_op jit(solution)/shard_map/ppermute | solution.py:16
  123.7 5.5 %fusion.29 = (bf16[1,384,20,128]{1,3,2,0:T(8,128)(2,1)S(1)}, f32[1,384,20,128]{1,3,2,0:T(8,128)}) fusion(bf16[128,20,128]{0,2,1:T(8,128)(2,1)} %bitcast.123, f32[20,128]{1,0:T(8,128)S(1)} %exponential_add_fusion, f32[20,128]{1,0:T(8,128)S(1)} %broadcast_maximum_fusion, f32[20,384,128]{2,1,0:T(8,128)} %copy-done, pred[128,384]{0,1:T(8,128)(4,1)S(1)} %add_bitcast_fusion), kind=kOutput, calls=%fused_computation.44 | convolution fusion | flops 257556480 | bytes 10555392 | tf_op jit(solution)/shard_map/bhqk,bqhd->bkhd/dot_general | solution.py:61
  133.0 1.9 %collective-permute-start.6 = (bf16[1,128,2560]{2,1,0:T(8,128)(2,1)}, bf16[1,128,2560]{2,1,0:T(8,128)(2,1)}, u32[]{:S(2)}, u32[]{:S(2)}) collective-permute-start(bf16[1,128,2560]{2,1,0:T(8,128)(2,1)} %copy.53), channel_id=1, source_target_pairs={{8,0},{16,8},{24,16},{9,1},{17,9},{25,17},{10,2},{18,10},{26,18},{... | collective-permute-start | bytes 1966088 | tf_op jit(solution)/shard_map/ppermute | solution.py:16
  136.7 2.5 %slice.36 = f32[1,128,20,128]{3,1,2,0:T(8,128)} slice(f32[1,384,20,128]{3,1,2,0:T(8,128)} %get-tuple-element.21), slice={[0:1], [0:128], [0:20], [0:128]} | slice | bytes 2621440 | tf_op jit(solution)/shard_map/slice | solution.py:112
  139.2 1.7 copy.49
  141.0 27.4 %collective-permute-done.5 = bf16[1,128,2560]{1,2,0:T(8,128)(2,1)} collective-permute-done((bf16[1,128,2560]{1,2,0:T(8,128)(2,1)}, bf16[1,128,2560]{1,2,0:T(8,128)(2,1)}, u32[]{:S(2)}, u32[]{:S(2)}) %collective-permute-start.5) | collective-permute-done | bytes 655392 | tf_op jit(solution)/shard_map/ppermute | solution.py:16
  168.4 1.6 fusion.8
  171.1 10.1 %collective-permute-done.7 = bf16[1,128,2560]{2,1,0:T(8,128)(2,1)} collective-permute-done((bf16[1,128,2560]{2,1,0:T(8,128)(2,1)}, bf16[1,128,2560]{2,1,0:T(8,128)(2,1)}, u32[]{:S(2)}, u32[]{:S(2)}) %collective-permute-start.7) | collective-permute-done | bytes 655392 | tf_op jit(solution)/shard_map/ppermute | solution.py:16
  181.2 2.3 %add_convert_fusion = bf16[1,128,2560]{2,1,0:T(8,128)(2,1)} fusion(bf16[1,128,2560]{2,1,0:T(8,128)(2,1)} %collective-permute-done.7, f32[1,128,2560]{2,1,0:T(8,128)S(1)} %copy.54, bf16[1,128,2560]{2,1,0:T(8,128)(2,1)} %collective-permute-done.6), kind=kLoop, calls=%fused_computation.20 | loop fusion | flops 1638400 | bytes 3276800 | tf_op jit(solution)/shard_map/convert_element_type | solution.py:133
  (65 shorter events, 26.5 us)
Async XLA Ops:
  0.6 14.7 %copy-start.1 = (bf16[1,128,2560]{2,1,0:T(8,128)(2,1)S(1)}, bf16[1,128,2560]{2,1,0:T(8,128)(2,1)}, u32[]{:S(2)}) copy-start(bf16[1,128,2560]{2,1,0:T(8,128)(2,1)} %param.9) | copy-start | bytes 1966084
  0.6 16.1 %copy-start.13 = (s32[2,1]{0,1:T(1,128)S(1)}, s32[2,1]{0,1:T(1,128)}, u32[]{:S(2)}) copy-start(s32[2,1]{0,1:T(1,128)} %param.10) | copy-start | bytes 28
  2.1 18.7 %copy-start.3 = (bf16[1,128,2560]{2,1,0:T(8,128)(2,1)S(1)}, bf16[1,128,2560]{2,1,0:T(8,128)(2,1)}, u32[]{:S(2)}) copy-start(bf16[1,128,2560]{2,1,0:T(8,128)(2,1)} %param.6) | copy-start | bytes 1966084
  2.1 19.3 %collective-permute-start.3 = (bf16[1,128,2560]{1,2,0:T(8,128)(2,1)S(1)}, bf16[1,128,2560]{1,2,0:T(8,128)(2,1)}, u32[]{:S(2)}, u32[]{:S(2)}) collective-permute-start(bf16[1,128,2560]{1,2,0:T(8,128)(2,1)S(1)} %copy.34), channel_id=1, source_target_pairs={{0,16},{8,24},{1,17},{9,25},{2,18},{10,26},{3,19},{11,27},{4,20},{... | collective-permute-start | bytes 1966088 | tf_op jit(solution)/shard_map/ppermute | solution.py:16
  6.6 19.6 %collective-permute-start.2 = (bf16[1,128,2560]{1,2,0:T(8,128)(2,1)S(1)}, bf16[1,128,2560]{1,2,0:T(8,128)(2,1)}, u32[]{:S(2)}, u32[]{:S(2)}) collective-permute-start(bf16[1,128,2560]{1,2,0:T(8,128)(2,1)S(1)} %copy.34), channel_id=1, source_target_pairs={{0,8},{8,16},{16,24},{1,9},{9,17},{17,25},{2,10},{10,18},{18,26},{... | collective-permute-start | bytes 1966088 | tf_op jit(solution)/shard_map/ppermute | solution.py:16
  9.9 23.8 %collective-permute-start.1 = (bf16[1,128,2560]{1,2,0:T(8,128)(2,1)S(1)}, bf16[1,128,2560]{1,2,0:T(8,128)(2,1)}, u32[]{:S(2)}, u32[]{:S(2)}) collective-permute-start(bf16[1,128,2560]{1,2,0:T(8,128)(2,1)S(1)} %copy.26), channel_id=1, source_target_pairs={{0,16},{8,24},{1,17},{9,25},{2,18},{10,26},{3,19},{11,27},{4,20},{... | collective-permute-start | bytes 1966088 | tf_op jit(solution)/shard_map/ppermute | solution.py:16
  12.0 26.7 %collective-permute-start = (bf16[1,128,2560]{1,2,0:T(8,128)(2,1)S(1)}, bf16[1,128,2560]{1,2,0:T(8,128)(2,1)}, u32[]{:S(2)}, u32[]{:S(2)}) collective-permute-start(bf16[1,128,2560]{1,2,0:T(8,128)(2,1)S(1)} %copy.26), channel_id=1, source_target_pairs={{0,8},{8,16},{16,24},{1,9},{9,17},{17,25},{2,10},{10,18},{18,26},{... | collective-permute-start | bytes 1966088 | tf_op jit(solution)/shard_map/ppermute | solution.py:16
  15.4 31.0 %copy-start.4 = (bf16[1,128,2560]{1,2,0:T(8,128)(2,1)}, bf16[1,128,2560]{1,2,0:T(8,128)(2,1)S(1)}, u32[]{:S(2)}) copy-start(bf16[1,128,2560]{1,2,0:T(8,128)(2,1)S(1)} %copy.40) | copy-start | bytes 1966084
  21.2 19.0 %copy-start.5 = (bf16[1,128,20,128]{3,1,2,0:T(8,128)(2,1)S(1)}, bf16[1,128,20,128]{3,1,2,0:T(8,128)(2,1)}, u32[]{:S(2)}) copy-start(bf16[1,128,20,128]{3,1,2,0:T(8,128)(2,1)} %copy.29) | copy-start | bytes 1966084
  35.1 5.1 %copy-start.9 = (bf16[1,128,20,128]{3,1,2,0:T(8,128)(2,1)}, bf16[1,128,20,128]{3,1,2,0:T(8,128)(2,1)S(1)}, u32[]{:S(2)}) copy-start(bf16[1,128,20,128]{3,1,2,0:T(8,128)(2,1)S(1)} %copy.31) | copy-start | bytes 1966084
  40.2 0.8 copy-start.12
  41.0 5.4 %copy-start = (f32[20,384,128]{2,1,0:T(8,128)}, f32[20,384,128]{2,1,0:T(8,128)S(1)}, u32[]{:S(2)}) copy-start(f32[20,384,128]{2,1,0:T(8,128)S(1)} %get-tuple-element.19) | copy-start | bytes 11796484
  41.0 2.3 %copy-start.2 = (f32[1,128,2560]{1,2,0:T(8,128)S(1)}, f32[1,128,2560]{1,2,0:T(8,128)}, u32[]{:S(2)}) copy-start(f32[1,128,2560]{1,2,0:T(8,128)} %copy.42) | copy-start | bytes 3932164
  41.0 2.9 %copy-start.6 = (bf16[1,128,20,128]{3,1,2,0:T(8,128)(2,1)S(1)}, bf16[1,128,20,128]{3,1,2,0:T(8,128)(2,1)}, u32[]{:S(2)}) copy-start(bf16[1,128,20,128]{3,1,2,0:T(8,128)(2,1)} %copy.37) | copy-start | bytes 1966084
  41.0 3.1 %copy-start.7 = (bf16[1,128,20,128]{3,1,2,0:T(8,128)(2,1)S(1)}, bf16[1,128,20,128]{3,1,2,0:T(8,128)(2,1)}, u32[]{:S(2)}) copy-start(bf16[1,128,20,128]{3,1,2,0:T(8,128)(2,1)} %copy.39) | copy-start | bytes 1966084
  41.0 3.3 %copy-start.8 = (bf16[1,128,20,128]{3,1,2,0:T(8,128)(2,1)S(1)}, bf16[1,128,20,128]{3,1,2,0:T(8,128)(2,1)}, u32[]{:S(2)}) copy-start(bf16[1,128,20,128]{3,1,2,0:T(8,128)(2,1)} %copy.38) | copy-start | bytes 1966084
  46.4 1.6 copy-start.10
  49.6 68.1 %copy-start.11 = (bf16[20,128,128]{2,1,0:T(8,128)(2,1)S(1)}, bf16[20,128,128]{2,1,0:T(8,128)(2,1)}, u32[]{:S(2)}) copy-start(bf16[20,128,128]{2,1,0:T(8,128)(2,1)} %fusion.4) | copy-start | bytes 1966084
  120.4 47.9 %collective-permute-start.5 = (bf16[1,128,2560]{1,2,0:T(8,128)(2,1)}, bf16[1,128,2560]{1,2,0:T(8,128)(2,1)}, u32[]{:S(2)}, u32[]{:S(2)}) collective-permute-start(bf16[1,128,2560]{1,2,0:T(8,128)(2,1)} %bitcast.31), channel_id=1, source_target_pairs={{16,0},{24,8},{17,1},{25,9},{18,2},{26,10},{19,3},{27,11},{20,4},{... | collective-permute-start | bytes 1966088 | tf_op jit(solution)/shard_map/ppermute | solution.py:16
  121.7 46.6 %collective-permute-start.4 = (bf16[1,128,2560]{1,2,0:T(8,128)(2,1)S(1)}, bf16[1,128,2560]{1,2,0:T(8,128)(2,1)}, u32[]{:S(2)}, u32[]{:S(2)}) collective-permute-start(bf16[1,128,2560]{1,2,0:T(8,128)(2,1)S(1)} %bitcast.124), channel_id=1, source_target_pairs={{8,0},{16,8},{24,16},{9,1},{17,9},{25,17},{10,2},{18,10},{26,18},{... | collective-permute-start | bytes 1966088 | tf_op jit(solution)/shard_map/ppermute | solution.py:16
  131.7 49.5 %collective-permute-start.7 = (bf16[1,128,2560]{2,1,0:T(8,128)(2,1)}, bf16[1,128,2560]{2,1,0:T(8,128)(2,1)}, u32[]{:S(2)}, u32[]{:S(2)}) collective-permute-start(bf16[1,128,2560]{2,1,0:T(8,128)(2,1)} %copy.55), channel_id=1, source_target_pairs={{16,0},{24,8},{17,1},{25,9},{18,2},{26,10},{19,3},{27,11},{20,4},{... | collective-permute-start | bytes 1966088 | tf_op jit(solution)/shard_map/ppermute | solution.py:16
  133.0 48.2 %collective-permute-start.6 = (bf16[1,128,2560]{2,1,0:T(8,128)(2,1)}, bf16[1,128,2560]{2,1,0:T(8,128)(2,1)}, u32[]{:S(2)}, u32[]{:S(2)}) collective-permute-start(bf16[1,128,2560]{2,1,0:T(8,128)(2,1)} %copy.53), channel_id=1, source_target_pairs={{8,0},{16,8},{24,16},{9,1},{17,9},{25,17},{10,2},{18,10},{26,18},{... | collective-permute-start | bytes 1966088 | tf_op jit(solution)/shard_map/ppermute | solution.py:16
where the time goes:
time: 184 us; the launch traced here: 183 us
  blocking collectives  65.6 us (36%)
  waiting for transfers between devices  49.1 us (27%)
  local copies, waits for them, and re-layouts  31.8 us (17%)
  starting transfers between devices  16.8 us (9%)
  matrix products  13.9 us (8%)
  other arithmetic  5.32 us (3%)
    psum x1, blocking collectives, body(): sink_grad = lax.psum(sink_term, ('dp', 'ctx'))  65.6 us
    ppermute x8, waiting for transfers between devices, from_behind(): lax.ppermute(value, axis, [(source, source + steps) for source in range(i...  49.1 us
    ppermute x8, starting transfers between devices, from_behind(): lax.ppermute(value, axis, [(source, source + steps) for source in range(i...  16.8 us
    reshape x6, local copies, waits for them, and re-layouts, to_blocks(): return array.reshape(blocks, BLOCK, heads, head_size)  9.33 us
    unnamed x34, local copies, waits for them, and re-layouts  9.1 us
    dot_general x1, matrix products, attend_backward(): jnp.einsum('bhqk,bqhd->bkhd', weights, grad_blocks, preferred_element_typ...  5.47 us
    slice x2, local copies, waits for them, and re-layouts, body(): key_grad = key_terms[:, :BLOCK].reshape(1, tokens, width)  4.21 us
  transfers between devices with their start and end apart: 8, of which 5 were waited for; matrix products, arithmetic and copies ran while one was open for 17% of the time, Pallas kernels for 0%

commit v1 on v0

--- a/solution.py
+++ b/solution.py
@@ -1,13 +1,265 @@
+import functools
+
 import jax
 import jax.numpy as jnp
 from jax import lax
+from jax.experimental import pallas as pl
+from jax.experimental.pallas import tpu as pltpu
 from jax.sharding import PartitionSpec as P
 
 BLOCK = 128
 LEVELS = 2
-
-
+FLAG_ROWS = 16
 NEG_FILL = -1e30
+ORDER = (3, 1, 2)
+
+
+def pack_kernel(offset, width, share, links, *refs):
+    arrays, outs, flags, sems, flag_sems = refs[:4], refs[4:8], refs[8], refs[9], refs[10]
+    me = lax.axis_index("dp")
+    live = [jnp.where(links[level, 0] >= 0, 1.0, 0.0) for level in range(LEVELS)]
+    row = lax.broadcasted_iota(jnp.int32, (FLAG_ROWS, width), 0)
+    flags[...] = jnp.where(row < 8, live[0], live[1]).astype(jnp.bfloat16)
+    copies = []
+    for mask in ORDER + (0,):
+        start = pl.multiple_of((me ^ mask) * share + offset, BLOCK)
+        for num, array in enumerate(arrays):
+            copies.append(
+                pltpu.make_async_copy(
+                    array.at[0, :, pl.ds(start, width)],
+                    outs[mask].at[pl.ds(num * BLOCK, BLOCK), :],
+                    sems.at[mask, num],
+                )
+            )
+        copies.append(
+            pltpu.make_async_copy(
+                flags, outs[mask].at[pl.ds(4 * BLOCK, FLAG_ROWS), :], flag_sems.at[mask]
+            )
+        )
+    for copy in copies:
+        copy.start()
+    for copy in copies:
+        copy.wait()
+
+
+def pack(links, arrays, offset, width, share):
+    rows = 4 * BLOCK + FLAG_ROWS
+    return pl.pallas_call(
+        functools.partial(pack_kernel, offset, width, share),
+        out_shape=[jax.ShapeDtypeStruct((rows, width), jnp.bfloat16)] * 4,
+        in_specs=[pl.BlockSpec(memory_space=pltpu.SMEM)] + [pl.BlockSpec(memory_space=pl.ANY)] * 4,
+        out_specs=[pl.BlockSpec(memory_space=pl.ANY)] * 4,
+        scratch_shapes=[
+            pltpu.VMEM((FLAG_ROWS, width), jnp.bfloat16),
+            pltpu.SemaphoreType.DMA((4, 4)),
+            pltpu.SemaphoreType.DMA((4,)),
+        ],
+        cost_estimate=pl.CostEstimate(flops=0, bytes_accessed=16 * rows * width, transcendentals=0),
+        name="pack",
+    )(links, *arrays)
+
+
+def dot_nt(a, b):
+    return lax.dot_general(a, b, (((1,), (1,)), ((), ())), preferred_element_type=jnp.float32)
+
+
+def dot_nn(a, b):
+    return lax.dot_general(a, b, (((1,), (0,)), ((), ())), preferred_element_type=jnp.float32)
+
+
+def dot_tn(a, b):
+    return lax.dot_general(a, b, (((0,), (0,)), ((), ())), preferred_element_type=jnp.float32)
+
+
+def attend_kernel(first_head, heads, heads_dev, score_scale, sink, *refs):
+    ins, outs, sink_out = refs[:4], refs[4:8], refs[8]
+    held, grads, in_sems, out_sems = refs[9:]
+    me = lax.axis_index("dp")
+    blocks = 4
+
+    def columns(head):
+        return pl.ds(head * BLOCK, BLOCK)
+
+    loads = [
+        [
+            pltpu.make_async_copy(
+                ins[mask].at[:, columns(head)],
+                held.at[me ^ mask, :, columns(head)],
+                in_sems.at[head, mask],
+            )
+            for mask in range(blocks)
+        ]
+        for head in range(heads)
+    ]
+    for group in loads:
+        for copy in group:
+            copy.start()
+    keys_iota = lax.broadcasted_iota(jnp.int32, (BLOCK, BLOCK), 0)
+    queries_iota = lax.broadcasted_iota(jnp.int32, (BLOCK, BLOCK), 1)
+    causal = keys_iota <= queries_iota
+    sink_out[...] = jnp.zeros_like(sink_out)
+    stores = []
+    for head in range(heads):
+        for copy in loads[head]:
+            copy.wait()
+        cols = columns(head)
+
+        def part(kind, first, last):
+            return held[first : last + 1, kind * BLOCK : (kind + 1) * BLOCK, cols].reshape(
+                (last + 1 - first) * BLOCK, BLOCK
+            )
+
+        sink_logit = sink[me * heads_dev + first_head + head]
+        weight_blocks, grad_blocks = {}, {}
+        sink_total = jnp.zeros((1, BLOCK), jnp.float32)
+        for block in range(blocks):
+            first = max(0, block - LEVELS)
+            flags = held[block, 4 * BLOCK :, cols].astype(jnp.float32)
+            scores = dot_nt(part(1, first, block), part(0, block, block)) * score_scale
+            pieces = []
+            for source in range(first, block + 1):
+                piece = scores[(source - first) * BLOCK : (source - first + 1) * BLOCK]
+                if source == block:
+                    piece = jnp.where(causal, piece, NEG_FILL)
+                else:
+                    row = 8 * (block - source - 1)
+                    piece = jnp.where(flags[row : row + 1] > 0.5, piece, NEG_FILL)
+                pieces.append(piece)
+            scores = jnp.concatenate(pieces, axis=0)
+            row_max = jnp.maximum(jnp.max(scores, axis=0, keepdims=True), sink_logit)
+            exp_scores = jnp.exp(scores - row_max)
+            sink_exp = jnp.exp(sink_logit - row_max)
+            scale = 1.0 / (jnp.sum(exp_scores, axis=0, keepdims=True) + sink_exp)
+            soft_prob = exp_scores * scale
+            prob_grad = dot_nt(part(2, first, block), part(3, block, block))
+            row_delta = jnp.sum(soft_prob * prob_grad, axis=0, keepdims=True)
+            sink_total = sink_total + sink_exp * scale * row_delta
+            weights = soft_prob.astype(jnp.bfloat16)
+            score_grad = (soft_prob * (prob_grad - row_delta)).astype(jnp.bfloat16)
+            query_grad = dot_tn(score_grad, part(1, first, block)) * score_scale
+            grads[block, 0:BLOCK, cols] = query_grad.astype(jnp.bfloat16)
+            for source in range(first, block + 1):
+                rows = slice((source - first) * BLOCK, (source - first + 1) * BLOCK)
+                weight_blocks[block, source] = weights[rows]
+                grad_blocks[block, source] = score_grad[rows]
+        sink_out[head : head + 1, :] = sink_total
+        for source in range(blocks):
+            last = min(blocks - 1, source + LEVELS)
+            score_grad = jnp.concatenate([grad_blocks[b, source] for b in range(source, last + 1)], axis=1)
+            weights = jnp.concatenate([weight_blocks[b, source] for b in range(source, last + 1)], axis=1)
+            key_grad = dot_nn(score_grad, part(0, source, last)) * score_scale
+            value_grad = dot_nn(weights, part(3, source, last))
+            grads[source, BLOCK : 2 * BLOCK, cols] = key_grad.astype(jnp.bfloat16)
+            grads[source, 2 * BLOCK : 3 * BLOCK, cols] = value_grad.astype(jnp.bfloat16)
+        for mask in ORDER + (0,):
+            copy = pltpu.make_async_copy(
+                grads.at[me ^ mask, :, cols], outs[mask].at[:, cols], out_sems.at[head, mask]
+            )
+            copy.start()
+            stores.append(copy)
+    for copy in stores:
+        copy.wait()
+
+
+def attend(sink_logit, packed, first_head, heads, heads_dev, score_scale):
+    rows, width = packed[0].shape
+    grad_rows = 3 * BLOCK
+    return pl.pallas_call(
+        functools.partial(attend_kernel, first_head, heads, heads_dev, score_scale),
+        out_shape=[jax.ShapeDtypeStruct((grad_rows, width), jnp.bfloat16)] * 4
+        + [jax.ShapeDtypeStruct((8, BLOCK), jnp.float32)],
+        in_specs=[pl.BlockSpec(memory_space=pltpu.SMEM)] + [pl.BlockSpec(memory_space=pl.ANY)] * 4,
+        out_specs=[pl.BlockSpec(memory_space=pl.ANY)] * 4 + [pl.BlockSpec(memory_space=pltpu.VMEM)],
+        scratch_shapes=[
+            pltpu.VMEM((4, rows, width), jnp.bfloat16),
+            pltpu.VMEM((4, grad_rows, width), jnp.bfloat16),
+            pltpu.SemaphoreType.DMA((heads, 4)),
+            pltpu.SemaphoreType.DMA((heads, 4)),
+        ],
+        compiler_params=pltpu.CompilerParams(vmem_limit_bytes=32 * 2**20),
+        cost_estimate=pl.CostEstimate(
+            flops=heads * 9 * 5 * 2 * BLOCK**3,
+            bytes_accessed=8 * (rows + grad_rows) * width,
+            transcendentals=heads * 9 * BLOCK**2,
+        ),
+        name="attend",
+    )(sink_logit, *packed)
+
+
+def unpack_kernel(offset, width, share, *refs):
+    ins, outs, sems = refs[:4], refs[-4:-1], refs[-1]
+    me = lax.axis_index("dp")
+    copies = []
+    for mask in range(4):
+        start = pl.multiple_of((me ^ mask) * share + offset, BLOCK)
+        for num, out in enumerate(outs):
+            copies.append(
+                pltpu.make_async_copy(
+                    ins[mask].at[pl.ds(num * BLOCK, BLOCK), :],
+                    out.at[0, :, pl.ds(start, width)],
+                    sems.at[mask, num],
+                )
+            )
+    for copy in copies:
+        copy.start()
+    for copy in copies:
+        copy.wait()
+
+
+def unpack(parts, previous, offset, share, shape):
+    width = parts[0].shape[1]
+    return pl.pallas_call(
+        functools.partial(unpack_kernel, offset, width, share),
+        out_shape=[jax.ShapeDtypeStruct(shape, jnp.bfloat16)] * 3,
+        in_specs=[pl.BlockSpec(memory_space=pl.ANY)] * (4 + len(previous)),
+        out_specs=[pl.BlockSpec(memory_space=pl.ANY)] * 3,
+        scratch_shapes=[pltpu.SemaphoreType.DMA((4, 3))],
+        input_output_aliases={4 + num: num for num in range(len(previous))},
+        cost_estimate=pl.CostEstimate(flops=0, bytes_accessed=8 * 3 * BLOCK * width, transcendentals=0),
+        name="unpack",
+    )(*parts, *previous)
+
+
+def swap(value, axis, mask):
+    return lax.ppermute(value, axis, [(i, i ^ mask) for i in range(lax.axis_size(axis))])
+
+
+def head_shares_body(chunks, queries, key_states, values, out_grad, block_links, sink_logit):
+    heads = sink_logit.shape[0]
+    head_size = queries.shape[2] // heads
+    score_scale = head_size ** (-0.5)
+    heads_dev = heads // 4
+    share = heads_dev * head_size
+    arrays = (queries, key_states, values, out_grad)
+    received, first = [], 0
+    for count in chunks:
+        packed = pack(block_links, arrays, first * head_size, count * head_size, share)
+        moved = {mask: swap(packed[mask], "dp", mask) for mask in ORDER}
+        moved[0] = packed[0]
+        received.append((first, count, [moved[mask] for mask in range(4)]))
+        first += count
+    results, sink_parts = [], []
+    for first, count, packed in received:
+        *grads, sink_part = attend(sink_logit, packed, first, count, heads_dev, score_scale)
+        moved = {mask: swap(grads[mask], "dp", mask) for mask in ORDER}
+        moved[0] = grads[0]
+        results.append((first, [moved[mask] for mask in range(4)]))
+        sink_parts.append(sink_part[:count])
+    sink_term = -jnp.sum(jnp.concatenate(sink_parts, axis=0), axis=1)
+    mask = 1
+    while mask < lax.axis_size("ctx"):
+        sink_term = sink_term + swap(sink_term, "ctx", mask)
+        mask *= 2
+    me = lax.axis_index("dp")
+    sink_grad = jnp.zeros((4, heads_dev), jnp.float32)
+    shares = {mask: swap(sink_term, "dp", mask) for mask in ORDER}
+    shares[0] = sink_term
+    for mask in range(4):
+        sink_grad = lax.dynamic_update_slice(sink_grad, shares[mask][None], (me ^ mask, 0))
+    outputs = ()
+    for first, parts in results:
+        outputs = unpack(parts, outputs, first * head_size, share, queries.shape)
+    return (*outputs, sink_grad.reshape(heads))
 
 
 def from_behind(value, axis, steps):
@@ -65,7 +317,7 @@
     return (query_grad, key_terms, value_terms, sink_term)
 
 
-def body(queries, key_states, values, out_grad, block_links, sink_logit):
+def keys_travel_body(queries, key_states, values, out_grad, block_links, sink_logit):
     tokens = queries.shape[1]
     width = queries.shape[2]
     blocks = tokens // BLOCK
@@ -96,15 +348,6 @@
     )
     soft_prob, weights, sink_prob, output = attend_forward(
         q_blocks, key_all, val_all, allowed, sink_logit, score_scale
-    )
-    refetched = []
-    for level_num in range(LEVELS):
-        refetched.append(from_behind((key_states, values), "dp", 2**level_num))
-    key_all = jnp.concatenate(
-        [to_blocks(key_states)] + [to_blocks(moved[0]) for moved in refetched], axis=1
-    )
-    val_all = jnp.concatenate(
-        [to_blocks(values)] + [to_blocks(moved[1]) for moved in refetched], axis=1
     )
     query_grad, key_terms, value_terms, sink_term = attend_backward(
         q_blocks, key_all, val_all, grad_blocks, soft_prob, weights, sink_prob, output, score_scale
@@ -135,6 +378,24 @@
     )
 
 
+CHUNKS = (3, 2)
+
+
+def body(queries, key_states, values, out_grad, block_links, sink_logit):
+    heads = sink_logit.shape[0]
+    blocks = lax.axis_size("dp")
+    groups = lax.axis_size("ctx")
+    fits = (
+        blocks == 4
+        and queries.shape[:2] == (1, BLOCK)
+        and queries.shape[2] == heads * BLOCK
+        and heads == 4 * sum(CHUNKS)
+        and groups & (groups - 1) == 0
+    )
+    plan = functools.partial(head_shares_body, CHUNKS) if fits else keys_travel_body
+    return plan(queries, key_states, values, out_grad, block_links, sink_logit)
+
+
 def solution(mesh):
     placed = (
         P("ctx", "dp", None),

time: 184 us -> 203 us (1.10)
  the two profiles are of different devices: /device:TPU:2 before, /device:TPU:0 now
where the time goes in v1:
time: 203 us; the launch traced here: 202 us
  Pallas kernels  156 us (77%)
  starting transfers between devices  23.2 us (11%)
  waiting for transfers between devices  17 us (8%)
  local copies, waits for them, and re-layouts  5.53 us (3%)
    pallas_call x2, Pallas kernels, pack(): pl.pallas_call(functools.partial(pack_kernel, offset, width, share), out_...  83.5 us
    pallas_call x2, Pallas kernels, unpack(): pl.pallas_call(functools.partial(unpack_kernel, offset, width, share), ou...  62 us
    ppermute x18, starting transfers between devices, swap(): lax.ppermute(value, axis, [(i, i ^ mask) for i in range(lax.axis_size(axi...  23.2 us
    ppermute x18, waiting for transfers between devices, swap(): lax.ppermute(value, axis, [(i, i ^ mask) for i in range(lax.axis_size(axi...  17 us
    pallas_call x2, Pallas kernels, attend(): pl.pallas_call(functools.partial(attend_kernel, first_head, heads, heads_...  10.2 us
    unnamed x23, local copies, waits for them, and re-layouts  4.79 us
  transfers between devices with their start and end apart: 18, of which 7 were waited for; matrix products, arithmetic and copies ran while one was open for 0% of the time, Pallas kernels for 40%

profile of v1, /device:TPU:0, one launch (start us, length us, event | category | flops | bytes accessed | tf_op | source)
XLA Modules:
  0.0 202.3 jit_solution(3833511192531908402)
XLA Ops:
  2.0 49.6 %pack.3 = (bf16[528,384]{1,0:T(8,128)(2,1)}, bf16[528,384]{1,0:T(8,128)(2,1)}, bf16[528,384]{1,0:T(8,128)(2,1)}, bf16[528,384]{1,0:T(8,128)(2,1)}) custom-call(s32[2,1]{1,0:T(2,128)} %copy.13.links, bf16[1,128,2560]{2,1,0:T(8,128)(2,1)} %refs_0_.3, bf16[1,128,2560]{2,1,0:T(8,128)(2,1)} %refs_1_.3, bf16[1,128,2560]{2,1,0:T(8,128)(2,1)} %refs_2_.3, ...), custom_call_target="tpu_custom_call" | custom-call | bytes 3244032 | tf_op jit(solution)/shard_map/pack/pallas_call | solution.py:47
  51.6 3.0 %collective-permute-start.6 = (bf16[528,384]{1,0:T(8,128)(2,1)}, bf16[528,384]{1,0:T(8,128)(2,1)S(1)}, u32[]{:S(2)}, u32[]{:S(2)}) collective-permute-start(bf16[528,384]{1,0:T(8,128)(2,1)} %get-tuple-element.37), channel_id=1, source_target_pairs={{0,8},{8,0},{16,24},{24,16},{1,9},{9,1},{17,25},{25,17},{2,10},{10... | collective-permute-start | bytes 1216520 | tf_op jit(solution)/shard_map/ppermute | solution.py:224
  54.6 1.5 collective-permute-start.7
  56.1 33.9 %pack.2 = (bf16[528,256]{1,0:T(8,128)(2,1)}, bf16[528,256]{1,0:T(8,128)(2,1)}, bf16[528,256]{1,0:T(8,128)(2,1)}, bf16[528,256]{1,0:T(8,128)(2,1)}) custom-call(s32[2,1]{1,0:T(2,128)} %copy.13.links, bf16[1,128,2560]{2,1,0:T(8,128)(2,1)} %refs_0_.3, bf16[1,128,2560]{2,1,0:T(8,128)(2,1)} %refs_1_.3, bf16[1,128,2560]{2,1,0:T(8,128)(2,1)} %refs_2_.3, ...), custom_call_target="tpu_custom_call" | custom-call | bytes 2162688 | tf_op jit(solution)/shard_map/pack/pallas_call | solution.py:47
  90.0 1.9 collective-permute-start
  91.9 1.5 collective-permute-start.1
  94.1 6.0 %attend.3 = (bf16[384,384]{1,0:T(8,128)(2,1)S(1)}, bf16[384,384]{1,0:T(8,128)(2,1)S(1)}, bf16[384,384]{1,0:T(8,128)(2,1)S(1)}, bf16[384,384]{1,0:T(8,128)(2,1)S(1)}, f32[8,128]{1,0:T(8,128)S(1)}) custom-call(f32[20]{0:T(128)S(1)} %copy-done.4, bf16[528,384]{1,0:T(8,128)(2,1)S(1)} %copy-done.2, bf16[528,384]{1,0:T(8,128)(2,1)S(1)} %collective-permute-done.6.refs_1_, ...), custom_call_target="tpu_custom_call" | custom-call | flops 566231040 | bytes 2801664 | tf_op jit(solution)/shard_map/attend/pallas_call | solution.py:167
  100.8 1.4 collective-permute-start.9
  103.5 3.3 %collective-permute-done.2.refs_3_ = bf16[528,256]{1,0:T(8,128)(2,1)S(1)} collective-permute-done((bf16[528,256]{1,0:T(8,128)(2,1)}, bf16[528,256]{1,0:T(8,128)(2,1)S(1)}, u32[]{:S(2)}, u32[]{:S(2)}) %collective-permute-start.2) | collective-permute-done | bytes 270368 | tf_op jit(solution)/shard_map/ppermute | solution.py:224
  106.8 4.2 %attend.2 = (bf16[384,256]{1,0:T(8,128)(2,1)S(1)}, bf16[384,256]{1,0:T(8,128)(2,1)S(1)}, bf16[384,256]{1,0:T(8,128)(2,1)S(1)}, bf16[384,256]{1,0:T(8,128)(2,1)S(1)}, f32[8,128]{1,0:T(8,128)S(1)}) custom-call(f32[20]{0:T(128)S(1)} %copy-done.4, bf16[528,256]{1,0:T(8,128)(2,1)S(1)} %copy-done.3, bf16[528,256]{1,0:T(8,128)(2,1)S(1)} %collective-permute-done.refs_1_, ...), custom_call_target="tpu_custom_call" | custom-call | flops 377487360 | bytes 1867776 | tf_op jit(solution)/shard_map/attend/pallas_call | solution.py:167
  111.7 1.4 collective-permute-start.3
  114.0 1.5 collective-permute-start.11
  115.5 1.6 collective-permute-start.13
  117.1 2.0 collective-permute-done.13
  119.0 2.6 %collective-permute-start.14 = (f32[5]{0:T(128)S(1)}, f32[5]{0:T(128)S(1)}, u32[]{:S(2)}, u32[]{:S(2)}) collective-permute-start(f32[5]{0:T(128)S(1)} %add.22), channel_id=1, source_target_pairs={{0,4},{1,5},{2,6},{3,7},{4,0},{5,1},{6,2},{7,3},{8,12},{9,13},{10,... | collective-permute-start | bytes 68 | tf_op jit(solution)/shard_map/ppermute | solution.py:224
  121.6 1.9 collective-permute-done.14
  123.5 1.4 collective-permute-start.17
  124.9 3.0 %collective-permute-done.17 = f32[5]{0:T(128)S(1)} collective-permute-done((f32[5]{0:T(128)S(1)}, f32[5]{0:T(128)S(1)}, u32[]{:S(2)}, u32[]{:S(2)}) %collective-permute-start.17) | collective-permute-done | bytes 52 | tf_op jit(solution)/shard_map/ppermute | solution.py:224
  128.1 3.4 %collective-permute-done.16 = f32[5]{0:T(128)S(1)} collective-permute-done((f32[5]{0:T(128)S(1)}, f32[5]{0:T(128)S(1)}, u32[]{:S(2)}, u32[]{:S(2)}) %collective-permute-start.16) | collective-permute-done | bytes 52 | tf_op jit(solution)/shard_map/ppermute | solution.py:224
  131.5 1.4 collective-permute-start.15
  132.9 2.1 %collective-permute-done.15 = f32[5]{0:T(128)S(1)} collective-permute-done((f32[5]{0:T(128)S(1)}, f32[5]{0:T(128)S(1)}, u32[]{:S(2)}, u32[]{:S(2)}) %collective-permute-start.15) | collective-permute-done | bytes 52 | tf_op jit(solution)/shard_map/ppermute | solution.py:224
  135.2 2.7 %collective-permute-start.5 = (bf16[384,256]{1,0:T(8,128)(2,1)S(1)}, bf16[384,256]{1,0:T(8,128)(2,1)S(1)}, u32[]{:S(2)}, u32[]{:S(2)}) collective-permute-start(bf16[384,256]{1,0:T(8,128)(2,1)S(1)} %get-tuple-element.35), channel_id=1, source_target_pairs={{0,24},{8,16},{16,8},{24,0},{1,25},{9,17},{17,9},{25,1},{2,26},{10... | collective-permute-start | bytes 589832 | tf_op jit(solution)/shard_map/ppermute | solution.py:224
  139.5 36.9 %unpack.2 = (bf16[1,128,2560]{2,1,0:T(8,128)(2,1)}, bf16[1,128,2560]{2,1,0:T(8,128)(2,1)}, bf16[1,128,2560]{2,1,0:T(8,128)(2,1)}) custom-call(bf16[384,384]{1,0:T(8,128)(2,1)} %copy-done, bf16[384,384]{1,0:T(8,128)(2,1)} %copy-done.5, bf16[384,384]{1,0:T(8,128)(2,1)} %copy-done.6, bf16[384,384]{1,0:T(8,128)(2,1)} %copy-done.7), custom_call_target="tpu_custom_call" | custom-call | bytes 1179648 | tf_op jit(solution)/shard_map/unpack/pallas_call | solution.py:211
  177.3 25.0 %unpack.3 = (bf16[1,128,2560]{2,1,0:T(8,128)(2,1)}, bf16[1,128,2560]{2,1,0:T(8,128)(2,1)}, bf16[1,128,2560]{2,1,0:T(8,128)(2,1)}) custom-call(bf16[384,256]{1,0:T(8,128)(2,1)} %copy-done.1, bf16[384,256]{1,0:T(8,128)(2,1)} %copy-done.8, bf16[384,256]{1,0:T(8,128)(2,1)} %copy-done.9, ...), custom_call_target="tpu_custom_call", output_to_operand_aliasing={{0}: (4, {}), {1}: (5, {}), {2}: (6, {})} | custom-call | bytes 786432 | tf_op jit(solution)/shard_map/unpack/pallas_call | solution.py:211
  (54 shorter events, 8.3 us)
Async XLA Ops:
  51.6 41.8 %collective-permute-start.6 = (bf16[528,384]{1,0:T(8,128)(2,1)}, bf16[528,384]{1,0:T(8,128)(2,1)S(1)}, u32[]{:S(2)}, u32[]{:S(2)}) collective-permute-start(bf16[528,384]{1,0:T(8,128)(2,1)} %get-tuple-element.37), channel_id=1, source_target_pairs={{0,8},{8,0},{16,24},{24,16},{1,9},{9,1},{17,25},{25,17},{2,10},{10... | collective-permute-start | bytes 1216520 | tf_op jit(solution)/shard_map/ppermute | solution.py:224
  54.6 39.0 %collective-permute-start.7 = (bf16[528,384]{1,0:T(8,128)(2,1)}, bf16[528,384]{1,0:T(8,128)(2,1)S(1)}, u32[]{:S(2)}, u32[]{:S(2)}) collective-permute-start(bf16[528,384]{1,0:T(8,128)(2,1)} %get-tuple-element.38), channel_id=1, source_target_pairs={{0,16},{8,24},{16,0},{24,8},{1,17},{9,25},{17,1},{25,9},{2,18},{10... | collective-permute-start | bytes 1216520 | tf_op jit(solution)/shard_map/ppermute | solution.py:224
  56.1 37.5 %copy-start.2 = (bf16[528,384]{1,0:T(8,128)(2,1)S(1)}, bf16[528,384]{1,0:T(8,128)(2,1)}, u32[]{:S(2)}) copy-start(bf16[528,384]{1,0:T(8,128)(2,1)} %get-tuple-element.36.refs_0_) | copy-start | bytes 1216516
  56.1 37.5 %collective-permute-start.8 = (bf16[528,384]{1,0:T(8,128)(2,1)}, bf16[528,384]{1,0:T(8,128)(2,1)S(1)}, u32[]{:S(2)}, u32[]{:S(2)}) collective-permute-start(bf16[528,384]{1,0:T(8,128)(2,1)} %get-tuple-element.39), channel_id=1, source_target_pairs={{0,24},{8,16},{16,8},{24,0},{1,25},{9,17},{17,9},{25,1},{2,26},{10... | collective-permute-start | bytes 1216520 | tf_op jit(solution)/shard_map/ppermute | solution.py:224
  90.0 12.1 %collective-permute-start = (bf16[528,256]{1,0:T(8,128)(2,1)}, bf16[528,256]{1,0:T(8,128)(2,1)S(1)}, u32[]{:S(2)}, u32[]{:S(2)}) collective-permute-start(bf16[528,256]{1,0:T(8,128)(2,1)} %get-tuple-element.29), channel_id=1, source_target_pairs={{0,8},{8,0},{16,24},{24,16},{1,9},{9,1},{17,25},{25,17},{2,10},{10... | collective-permute-start | bytes 811016 | tf_op jit(solution)/shard_map/ppermute | solution.py:224
  91.9 11.6 %collective-permute-start.1 = (bf16[528,256]{1,0:T(8,128)(2,1)}, bf16[528,256]{1,0:T(8,128)(2,1)S(1)}, u32[]{:S(2)}, u32[]{:S(2)}) collective-permute-start(bf16[528,256]{1,0:T(8,128)(2,1)} %get-tuple-element.30), channel_id=1, source_target_pairs={{0,16},{8,24},{16,0},{24,8},{1,17},{9,25},{17,1},{25,9},{2,18},{10... | collective-permute-start | bytes 811016 | tf_op jit(solution)/shard_map/ppermute | solution.py:224
  93.4 13.4 %collective-permute-start.2 = (bf16[528,256]{1,0:T(8,128)(2,1)}, bf16[528,256]{1,0:T(8,128)(2,1)S(1)}, u32[]{:S(2)}, u32[]{:S(2)}) collective-permute-start(bf16[528,256]{1,0:T(8,128)(2,1)} %get-tuple-element.31), channel_id=1, source_target_pairs={{0,24},{8,16},{16,8},{24,0},{1,25},{9,17},{17,9},{25,1},{2,26},{10... | collective-permute-start | bytes 811016 | tf_op jit(solution)/shard_map/ppermute | solution.py:224
  94.1 12.8 %copy-start.3 = (bf16[528,256]{1,0:T(8,128)(2,1)S(1)}, bf16[528,256]{1,0:T(8,128)(2,1)}, u32[]{:S(2)}) copy-start(bf16[528,256]{1,0:T(8,128)(2,1)} %get-tuple-element.28.refs_0_) | copy-start | bytes 811012
  100.8 34.4 %collective-permute-start.9 = (bf16[384,384]{1,0:T(8,128)(2,1)S(1)}, bf16[384,384]{1,0:T(8,128)(2,1)S(1)}, u32[]{:S(2)}, u32[]{:S(2)}) collective-permute-start(bf16[384,384]{1,0:T(8,128)(2,1)S(1)} %get-tuple-element.41), channel_id=1, source_target_pairs={{0,8},{8,0},{16,24},{24,16},{1,9},{9,1},{17,25},{25,17},{2,10},{10... | collective-permute-start | bytes 884744 | tf_op jit(solution)/shard_map/ppermute | solution.py:224
  111.7 64.7 %collective-permute-start.3 = (bf16[384,256]{1,0:T(8,128)(2,1)S(1)}, bf16[384,256]{1,0:T(8,128)(2,1)S(1)}, u32[]{:S(2)}, u32[]{:S(2)}) collective-permute-start(bf16[384,256]{1,0:T(8,128)(2,1)S(1)} %get-tuple-element.33), channel_id=1, source_target_pairs={{0,8},{8,0},{16,24},{24,16},{1,9},{9,1},{17,25},{25,17},{2,10},{10... | collective-permute-start | bytes 589832 | tf_op jit(solution)/shard_map/ppermute | solution.py:224
  113.3 2.2 %collective-permute-start.12 = (f32[5]{0:T(128)S(1)}, f32[5]{0:T(128)S(1)}, u32[]{:S(2)}, u32[]{:S(2)}) collective-permute-start(f32[5]{0:T(128)S(1)} %neg.3), channel_id=1, source_target_pairs={{0,1},{1,0},{2,3},{3,2},{4,5},{5,4},{6,7},{7,6},{8,9},{9,8},{10,11... | collective-permute-start | bytes 68 | tf_op jit(solution)/shard_map/ppermute | solution.py:224
  113.4 25.3 %collective-permute-start.10 = (bf16[384,384]{1,0:T(8,128)(2,1)S(1)}, bf16[384,384]{1,0:T(8,128)(2,1)S(1)}, u32[]{:S(2)}, u32[]{:S(2)}) collective-permute-start(bf16[384,384]{1,0:T(8,128)(2,1)S(1)} %get-tuple-element.42), channel_id=1, source_target_pairs={{0,16},{8,24},{16,0},{24,8},{1,17},{9,25},{17,1},{25,9},{2,18},{10... | collective-permute-start | bytes 884744 | tf_op jit(solution)/shard_map/ppermute | solution.py:224
  114.0 24.7 %collective-permute-start.11 = (bf16[384,384]{1,0:T(8,128)(2,1)S(1)}, bf16[384,384]{1,0:T(8,128)(2,1)S(1)}, u32[]{:S(2)}, u32[]{:S(2)}) collective-permute-start(bf16[384,384]{1,0:T(8,128)(2,1)S(1)} %get-tuple-element.43), channel_id=1, source_target_pairs={{0,24},{8,16},{16,8},{24,0},{1,25},{9,17},{17,9},{25,1},{2,26},{10... | collective-permute-start | bytes 884744 | tf_op jit(solution)/shard_map/ppermute | solution.py:224
  115.5 3.5 %collective-permute-start.13 = (f32[5]{0:T(128)S(1)}, f32[5]{0:T(128)S(1)}, u32[]{:S(2)}, u32[]{:S(2)}) collective-permute-start(f32[5]{0:T(128)S(1)} %negate_add_fusion), channel_id=1, source_target_pairs={{0,2},{1,3},{2,0},{3,1},{4,6},{5,7},{6,4},{7,5},{8,10},{9,11},{10,... | collective-permute-start | bytes 68 | tf_op jit(solution)/shard_map/ppermute | solution.py:224
  119.0 4.4 %collective-permute-start.14 = (f32[5]{0:T(128)S(1)}, f32[5]{0:T(128)S(1)}, u32[]{:S(2)}, u32[]{:S(2)}) collective-permute-start(f32[5]{0:T(128)S(1)} %add.22), channel_id=1, source_target_pairs={{0,4},{1,5},{2,6},{3,7},{4,0},{5,1},{6,2},{7,3},{8,12},{9,13},{10,... | collective-permute-start | bytes 68 | tf_op jit(solution)/shard_map/ppermute | solution.py:224
  123.5 4.4 %collective-permute-start.17 = (f32[5]{0:T(128)S(1)}, f32[5]{0:T(128)S(1)}, u32[]{:S(2)}, u32[]{:S(2)}) collective-permute-start(f32[5]{0:T(128)S(1)} %add.23), channel_id=1, source_target_pairs={{0,24},{8,16},{16,8},{24,0},{1,25},{9,17},{17,9},{25,1},{2,26},{10... | collective-permute-start | bytes 68 | tf_op jit(solution)/shard_map/ppermute | solution.py:224
  127.9 3.5 %collective-permute-start.16 = (f32[5]{0:T(128)S(1)}, f32[5]{0:T(128)S(1)}, u32[]{:S(2)}, u32[]{:S(2)}) collective-permute-start(f32[5]{0:T(128)S(1)} %add.23), channel_id=1, source_target_pairs={{0,16},{8,24},{16,0},{24,8},{1,17},{9,25},{17,1},{25,9},{2,18},{10... | collective-permute-start | bytes 68 | tf_op jit(solution)/shard_map/ppermute | solution.py:224
  131.5 3.5 %collective-permute-start.15 = (f32[5]{0:T(128)S(1)}, f32[5]{0:T(128)S(1)}, u32[]{:S(2)}, u32[]{:S(2)}) collective-permute-start(f32[5]{0:T(128)S(1)} %add.23), channel_id=1, source_target_pairs={{0,8},{8,0},{16,24},{24,16},{1,9},{9,1},{17,25},{25,17},{2,10},{10... | collective-permute-start | bytes 68 | tf_op jit(solution)/shard_map/ppermute | solution.py:224
  135.0 41.5 %collective-permute-start.4 = (bf16[384,256]{1,0:T(8,128)(2,1)S(1)}, bf16[384,256]{1,0:T(8,128)(2,1)S(1)}, u32[]{:S(2)}, u32[]{:S(2)}) collective-permute-start(bf16[384,256]{1,0:T(8,128)(2,1)S(1)} %get-tuple-element.34), channel_id=1, source_target_pairs={{0,16},{8,24},{16,0},{24,8},{1,17},{9,25},{17,1},{25,9},{2,18},{10... | collective-permute-start | bytes 589832 | tf_op jit(solution)/shard_map/ppermute | solution.py:224
  135.2 3.5 %copy-start.5 = (bf16[384,384]{1,0:T(8,128)(2,1)}, bf16[384,384]{1,0:T(8,128)(2,1)S(1)}, u32[]{:S(2)}) copy-start(bf16[384,384]{1,0:T(8,128)(2,1)S(1)} %collective-permute-done.9.refs_1_) | copy-start | bytes 884740
  135.2 41.3 %collective-permute-start.5 = (bf16[384,256]{1,0:T(8,128)(2,1)S(1)}, bf16[384,256]{1,0:T(8,128)(2,1)S(1)}, u32[]{:S(2)}, u32[]{:S(2)}) collective-permute-start(bf16[384,256]{1,0:T(8,128)(2,1)S(1)} %get-tuple-element.35), channel_id=1, source_target_pairs={{0,24},{8,16},{16,8},{24,0},{1,25},{9,17},{17,9},{25,1},{2,26},{10... | collective-permute-start | bytes 589832 | tf_op jit(solution)/shard_map/ppermute | solution.py:224
  138.7 0.8 copy-start.7
  176.5 0.7 copy-start.9
  176.5 0.8 copy-start.10
  (5 other events, 3.4 us)

commit v2 on v1

v2 whole, which is shorter than its diff:
```python
import functools

import jax
import jax.numpy as jnp
from jax import lax
from jax.experimental import pallas as pl
from jax.experimental.pallas import tpu as pltpu
from jax.sharding import PartitionSpec as P

BLOCK = 128
LEVELS = 2
FLAG_ROWS = 16
LOG2_E = 1.4426950408889634
NEG_FILL = -1e30
ORDER = (3, 1, 2)


def pack_kernel(offset, width, share, links, *refs):
    arrays, outs, (held, load_sems, store_sems) = refs[:4], refs[4:7], refs[7:]
    me = lax.axis_index("dp")
    loads, stores = [], []
    for place, mask in enumerate(ORDER):
        start = pl.multiple_of((me ^ mask) * share + offset, BLOCK)
        loads.append(
            [
                pltpu.make_async_copy(
                    array.at[0, :, pl.ds(start, width)],
                    held.at[place, pl.ds(num * BLOCK, BLOCK), :],
                    load_sems.at[place, num],
                )
                for num, array in enumerate(arrays)
            ]
        )
        for copy in loads[-1]:
            copy.start()
    flags = live_flags(links, width)
    for place in range(3):
        held[place, 4 * BLOCK :, :] = flags
    for place in range(3):
        for copy in loads[place]:
            copy.wait()
        stores.append(pltpu.make_async_copy(held.at[place], outs[place], store_sems.at[place]))
        stores[-1].start()
    for copy in stores:
        copy.wait()


def live_flags(links, width):
    live = [jnp.where(links[level] >= 0, 1.0, 0.0) for level in range(LEVELS)]
    row = lax.broadcasted_iota(jnp.int32, (FLAG_ROWS, width), 0)
    return jnp.where(row < 8, live[0], live[1]).astype(jnp.bfloat16)


def pack(links, arrays, offset, width, share):
    rows = 4 * BLOCK + FLAG_ROWS
    return pl.pallas_call(
        functools.partial(pack_kernel, offset, width, share),
        out_shape=[jax.ShapeDtypeStruct((rows, width), jnp.bfloat16)] * 3,
        in_specs=[pl.BlockSpec(memory_space=pltpu.SMEM)] + [pl.BlockSpec(memory_space=pl.ANY)] * 4,
        out_specs=[pl.BlockSpec(memory_space=pl.ANY)] * 3,
        scratch_shapes=[
            pltpu.VMEM((3, rows, width), jnp.bfloat16),
            pltpu.SemaphoreType.DMA((3, 4)),
            pltpu.SemaphoreType.DMA((3,)),
        ],
        cost_estimate=pl.CostEstimate(flops=0, bytes_accessed=12 * rows * width, transcendentals=0),
        name="pack",
    )(links, *arrays)


def dot_nt(a, b):
    return lax.dot_general(a, b, (((1,), (1,)), ((), ())), preferred_element_type=jnp.float32)


def dot_nn(a, b):
    return lax.dot_general(a, b, (((1,), (0,)), ((), ())), preferred_element_type=jnp.float32)


def dot_tn(a, b):
    return lax.dot_general(a, b, (((0,), (0,)), ((), ())), preferred_element_type=jnp.float32)


def attend_kernel(first_head, heads, heads_dev, score_scale, num_previous, sink, links, sink_in, *refs):
    arrays, ins, refs = refs[:4], refs[4:7], refs[7 + num_previous :]
    outs, own_outs, sink_out = refs[:3], refs[3:6], refs[6]
    held, grads, own_sems, in_sems, own_out_sems, out_sems = refs[7:]
    me = lax.axis_index("dp")
    blocks = 4

    def own_columns(head):
        return pl.ds(pl.multiple_of((me * heads_dev + first_head + head) * BLOCK, BLOCK), BLOCK)

    def columns(head):
        return pl.ds(head * BLOCK, BLOCK)

    loads = [
        [
            pltpu.make_async_copy(
                array.at[0, :, own_columns(head)],
                held.at[me, pl.ds(num * BLOCK, BLOCK), columns(head)],
                own_sems.at[head, num],
            )
            for num, array in enumerate(arrays)
        ]
        + [
            pltpu.make_async_copy(
                ins[place].at[:, columns(head)],
                held.at[me ^ mask, :, columns(head)],
                in_sems.at[head, place],
            )
            for place, mask in enumerate(ORDER)
        ]
        for head in range(heads)
    ]
    for group in loads:
        for copy in group:
            copy.start()
    held[me, 4 * BLOCK :, :] = live_flags(links, held.shape[2])
    keys_iota = lax.broadcasted_iota(jnp.int32, (BLOCK, BLOCK), 0)
    queries_iota = lax.broadcasted_iota(jnp.int32, (BLOCK, BLOCK), 1)
    causal = keys_iota <= queries_iota
    lanes = lax.broadcasted_iota(jnp.int32, (8, BLOCK), 1)
    sink_sum = sink_in[...]
    stores = []
    for head in range(heads):
        for copy in loads[head]:
            copy.wait()
        cols = columns(head)

        def part(kind, first, last):
            return held[first : last + 1, kind * BLOCK : (kind + 1) * BLOCK, cols].reshape(
                (last + 1 - first) * BLOCK, BLOCK
            )

        sink_logit = sink[me * heads_dev + first_head + head] * LOG2_E
        scores, prob_grads = {}, {}
        for pair in range(0, blocks, 2):
            first = max(0, pair - LEVELS)
            score = dot_nt(part(1, first, pair + 1), part(0, pair, pair + 1))
            prob_grad = dot_nt(part(2, first, pair + 1), part(3, pair, pair + 1))
            for block in (pair, pair + 1):
                lanes_here = slice((block - pair) * BLOCK, (block - pair + 1) * BLOCK)
                for source in range(max(0, block - LEVELS), block + 1):
                    rows = slice((source - first) * BLOCK, (source - first + 1) * BLOCK)
                    scores[block, source] = score[rows, lanes_here]
                    prob_grads[block, source] = prob_grad[rows, lanes_here]
        sink_total = jnp.zeros((1, BLOCK), jnp.float32)
        weights, score_grads = {}, {}
        for block in range(blocks):
            sources = range(max(0, block - LEVELS), block + 1)
            flags = held[block, 4 * BLOCK :, cols].astype(jnp.float32)
            pieces = []
            for source in sources:
                piece = scores[block, source] * (score_scale * LOG2_E)
                if source == block:
                    piece = jnp.where(causal, piece, NEG_FILL)
                else:
                    row = 8 * (block - source - 1)
                    piece = jnp.where(flags[row : row + 1] > 0.5, piece, NEG_FILL)
                pieces.append(piece)
            row_max = functools.reduce(jnp.maximum, pieces)
            row_max = jnp.maximum(jnp.max(row_max, axis=0, keepdims=True), sink_logit)
            pieces = [jnp.exp2(piece - row_max) for piece in pieces]
            sink_exp = jnp.exp2(sink_logit - row_max)
            denominator = jnp.sum(functools.reduce(jnp.add, pieces), axis=0, keepdims=True) + sink_exp
            scale = 1.0 / denominator
            pieces = [piece * scale for piece in pieces]
            products = [piece * prob_grads[block, source] for piece, source in zip(pieces, sources)]
            row_delta = jnp.sum(functools.reduce(jnp.add, products), axis=0, keepdims=True)
            sink_total = sink_total + sink_exp * scale * row_delta
            for piece, source in zip(pieces, sources):
                weights[block, source] = piece.astype(jnp.bfloat16)
                score_grads[block, source] = (
                    piece * (prob_grads[block, source] - row_delta)
                ).astype(jnp.bfloat16)
        here = lanes == me * heads_dev + first_head + head
        sink_sum = sink_sum - jnp.where(here, jnp.sum(sink_total, axis=1, keepdims=True), 0.0)
        for block in range(blocks):
            first = max(0, block - LEVELS)
            score_grad = jnp.concatenate([score_grads[block, b] for b in range(first, block + 1)], axis=0)
            query_grad = dot_tn(score_grad, part(1, first, block)) * score_scale
            grads[block, 0:BLOCK, cols] = query_grad.astype(jnp.bfloat16)
        for source in range(blocks):
            last = min(blocks - 1, source + LEVELS)
            score_grad = jnp.concatenate([score_grads[b, source] for b in range(source, last + 1)], axis=1)
            weight = jnp.concatenate([weights[b, source] for b in range(source, last + 1)], axis=1)
            key_grad = dot_nn(score_grad, part(0, source, last)) * score_scale
            value_grad = dot_nn(weight, part(3, source, last))
            grads[source, BLOCK : 2 * BLOCK, cols] = key_grad.astype(jnp.bfloat16)
            grads[source, 2 * BLOCK : 3 * BLOCK, cols] = value_grad.astype(jnp.bfloat16)
        copies = [
            pltpu.make_async_copy(
                grads.at[me ^ mask, :, cols], outs[place].at[:, cols], out_sems.at[head, place]
            )
            for place, mask in enumerate(ORDER)
        ] + [
            pltpu.make_async_copy(
                grads.at[me, pl.ds(num * BLOCK, BLOCK), cols],
                out.at[0, :, own_columns(head)],
                own_out_sems.at[head, num],
            )
            for num, out in enumerate(own_outs)
        ]
        for copy in copies:
            copy.start()
        stores.extend(copies)
    sink_out[...] = sink_sum
    for copy in stores:
        copy.wait()


def attend(sink_logit, links, sink_sum, arrays, packed, previous, first_head, heads, heads_dev, score_scale):
    rows, width = packed[0].shape
    grad_rows = 3 * BLOCK
    hbm = pl.BlockSpec(memory_space=pl.ANY)
    smem = pl.BlockSpec(memory_space=pltpu.SMEM)
    vmem = pl.BlockSpec(memory_space=pltpu.VMEM)
    return pl.pallas_call(
        functools.partial(attend_kernel, first_head, heads, heads_dev, score_scale, len(previous)),
        out_shape=[jax.ShapeDtypeStruct((grad_rows, width), jnp.bfloat16)] * 3
        + [jax.ShapeDtypeStruct(arrays[0].shape, jnp.bfloat16)] * 3
        + [jax.ShapeDtypeStruct((8, BLOCK), jnp.float32)],
        in_specs=[smem, smem, vmem] + [hbm] * (7 + len(previous)),
        out_specs=[hbm] * 6 + [vmem],
        scratch_shapes=[
            pltpu.VMEM((4, rows, width), jnp.bfloat16),
            pltpu.VMEM((4, grad_rows, width), jnp.bfloat16),
            pltpu.SemaphoreType.DMA((heads, 4)),
            pltpu.SemaphoreType.DMA((heads, 3)),
            pltpu.SemaphoreType.DMA((heads, 3)),
            pltpu.SemaphoreType.DMA((heads, 3)),
        ],
        input_output_aliases={10 + num: 3 + num for num in range(len(previous))},
        compiler_params=pltpu.CompilerParams(vmem_limit_bytes=32 * 2**20),
        cost_estimate=pl.CostEstimate(flops=0, bytes_accessed=0, transcendentals=0),
        name="attend",
    )(sink_logit, links, sink_sum, *arrays, *packed, *previous)


def unpack_kernel(offset, width, share, *refs):
    ins, outs, sems = refs[:3], refs[6:9], refs[9]
    me = lax.axis_index("dp")
    copies = []
    for place, mask in enumerate(ORDER):
        start = pl.multiple_of((me ^ mask) * share + offset, BLOCK)
        for num, out in enumerate(outs):
            copies.append(
                pltpu.make_async_copy(
                    ins[place].at[pl.ds(num * BLOCK, BLOCK), :],
                    out.at[0, :, pl.ds(start, width)],
                    sems.at[place, num],
                )
            )
    for copy in copies:
        copy.start()
    for copy in copies:
        copy.wait()


def unpack(parts, previous, offset, share):
    width = parts[0].shape[1]
    return pl.pallas_call(
        functools.partial(unpack_kernel, offset, width, share),
        out_shape=[jax.ShapeDtypeStruct(out.shape, out.dtype) for out in previous],
        in_specs=[pl.BlockSpec(memory_space=pltpu.VMEM)] * 3 + [pl.BlockSpec(memory_space=pl.ANY)] * 3,
        out_specs=[pl.BlockSpec(memory_space=pl.ANY)] * 3,
        scratch_shapes=[pltpu.SemaphoreType.DMA((3, 3))],
        input_output_aliases={3 + num: num for num in range(3)},
        cost_estimate=pl.CostEstimate(flops=0, bytes_accessed=8 * 3 * BLOCK * width, transcendentals=0),
        name="unpack",
    )(*parts, *previous)


def swap(value, axis, mask):
    return lax.ppermute(value, axis, [(i, i ^ mask) for i in range(lax.axis_size(axis))])


def after(value, other):
    return lax.optimization_barrier((value, other))


def butterfly(value, axis):
    mask = 1
    while mask < lax.axis_size(axis):
        value = value + swap(value, axis, mask)
        mask *= 2
    return value


def head_shares_body(chunks, queries, key_states, values, out_grad, block_links, sink_logit):
    heads = sink_logit.shape[0]
    head_size = queries.shape[2] // heads
    score_scale = head_size ** (-0.5)
    heads_dev = heads // 4
    share = heads_dev * head_size
    arrays = (queries, key_states, values, out_grad)
    links = block_links.reshape(LEVELS)
    received, first = [], 0
    for count in chunks:
        packed = list(pack(links, arrays, first * head_size, count * head_size, share))
        moved = [None] * 3
        for place, mask in enumerate(ORDER):
            if received:
                packed[place], received[-1][2][place] = after(packed[place], received[-1][2][place])
            moved[place] = swap(packed[place], "dp", mask)
        received.append((first, count, moved))
        first += count
    results, outputs, sink_sum = [], [], jnp.zeros((8, BLOCK), jnp.float32)
    for num, (first, count, packed) in enumerate(received):
        *grads, sink_sum = attend(
            sink_logit, links, sink_sum, arrays, packed, outputs, first, count, heads_dev, score_scale
        )
        grads, outputs = grads[:3], grads[3:]
        moved = [None] * 3
        for place, mask in enumerate(ORDER):
            if num:
                grads[place], results[-1][1][place] = after(grads[place], results[-1][1][place])
            else:
                grads[place], received[1][2][0] = after(grads[place], received[1][2][0])
            moved[place] = swap(grads[place], "dp", mask)
        results.append((first, moved))
    sink_sum, results[0][1][0] = after(sink_sum, results[0][1][0])
    once = jnp.minimum(links[0] + 2, 1)
    sink_sum = lax.fori_loop(0, once, lambda _, held: butterfly(held, "ctx"), sink_sum)
    sink_sum = butterfly(sink_sum, "dp")
    for first, parts in results:
        outputs = unpack(parts, outputs, first * head_size, share)
    return (*outputs, sink_sum[0, :heads])


def from_behind(value, axis, steps):
    count = lax.axis_size(axis)
    initial, last = (max(0, -steps), min(count, count - steps))
    return lax.ppermute(value, axis, [(source, source + steps) for source in range(initial, last)])


def causal_table(block_len):
    rows_iota = lax.broadcasted_iota(jnp.int32, (block_len, block_len), 0)
    cols_iota = lax.broadcasted_iota(jnp.int32, (block_len, block_len), 1)
    return rows_iota >= cols_iota


def attend_forward(q_blocks, key_all, val_all, allowed, sink_logit, score_scale):
    scores = (
        jnp.einsum("bqhd,bkhd->bhqk", q_blocks, key_all, preferred_element_type=jnp.float32)
        * score_scale
    )
    scores = jnp.where(allowed[:, None], scores, NEG_FILL)
    row_max = jnp.maximum(jnp.max(scores, axis=-1), sink_logit[None, :, None])
    exp_scores = jnp.exp(scores - row_max[..., None])
    sink_exp = jnp.exp(sink_logit[None, :, None] - row_max)
    denominator = jnp.sum(exp_scores, axis=-1) + sink_exp
    soft_prob = exp_scores / denominator[..., None]
    sink_prob = sink_exp / denominator
    weights = soft_prob.astype(jnp.bfloat16)
    output = jnp.einsum(
        "bhqk,bkhd->bqhd", weights, val_all, preferred_element_type=jnp.float32
    ).astype(jnp.bfloat16)
    return (soft_prob, weights, sink_prob, output)


def attend_backward(
    q_blocks, key_all, val_all, grad_blocks, soft_prob, weights, sink_prob, output, score_scale
):
    row_delta = jnp.sum(grad_blocks.astype(jnp.float32) * output.astype(jnp.float32), axis=-1)
    row_delta = jnp.transpose(row_delta, (0, 2, 1))
    prob_grad = jnp.einsum(
        "bqhd,bkhd->bhqk", grad_blocks, val_all, preferred_element_type=jnp.float32
    )
    score_grad = (soft_prob * (prob_grad - row_delta[..., None])).astype(jnp.bfloat16)
    query_grad = (
        jnp.einsum("bhqk,bkhd->bqhd", score_grad, key_all, preferred_element_type=jnp.float32)
        * score_scale
    ).astype(jnp.bfloat16)
    key_terms = (
        jnp.einsum("bhqk,bqhd->bkhd", score_grad, q_blocks, preferred_element_type=jnp.float32)
        * score_scale
    )
    value_terms = jnp.einsum(
        "bhqk,bqhd->bkhd", weights, grad_blocks, preferred_element_type=jnp.float32
    )
    sink_term = -jnp.sum(sink_prob * row_delta, axis=(0, 2))
    return (query_grad, key_terms, value_terms, sink_term)


def keys_travel_body(queries, key_states, values, out_grad, block_links, sink_logit):
    tokens = queries.shape[1]
    width = queries.shape[2]
    blocks = tokens // BLOCK
    heads = sink_logit.shape[0]
    head_size = width // heads
    score_scale = head_size ** (-0.5)

    def to_blocks(array):
        return array.reshape(blocks, BLOCK, heads, head_size)

    q_blocks = to_blocks(queries)
    grad_blocks = to_blocks(out_grad)
    level_live = block_links >= 0
    causal = jnp.broadcast_to(causal_table(BLOCK), (blocks, BLOCK, BLOCK))
    remote_masks = [
        jnp.broadcast_to(level_live[level_num][:, None, None], (blocks, BLOCK, BLOCK))
        for level_num in range(LEVELS)
    ]
    allowed = jnp.concatenate([causal] + remote_masks, axis=2)
    fetched = []
    for level_num in range(LEVELS):
        fetched.append(from_behind((key_states, values), "dp", 2**level_num))
    key_all = jnp.concatenate(
        [to_blocks(key_states)] + [to_blocks(moved[0]) for moved in fetched], axis=1
    )
    val_all = jnp.concatenate(
        [to_blocks(values)] + [to_blocks(moved[1]) for moved in fetched], axis=1
    )
    soft_prob, weights, sink_prob, output = attend_forward(
        q_blocks, key_all, val_all, allowed, sink_logit, score_scale
    )
    query_grad, key_terms, value_terms, sink_term = attend_backward(
        q_blocks, key_all, val_all, grad_blocks, soft_prob, weights, sink_prob, output, score_scale
    )
    key_grad = key_terms[:, :BLOCK].reshape(1, tokens, width)
    value_grad = value_terms[:, :BLOCK].reshape(1, tokens, width)
    for level_num in range(LEVELS):
        first_col = BLOCK * (1 + level_num)
        key_part = (
            key_terms[:, first_col : first_col + BLOCK]
            .reshape(1, tokens, width)
            .astype(jnp.bfloat16)
        )
        value_part = (
            value_terms[:, first_col : first_col + BLOCK]
            .reshape(1, tokens, width)
            .astype(jnp.bfloat16)
        )
        key_back, value_back = from_behind((key_part, value_part), "dp", -(2**level_num))
        key_grad = key_grad + key_back.astype(jnp.float32)
        value_grad = value_grad + value_back.astype(jnp.float32)
    sink_grad = lax.psum(sink_term, ("dp", "ctx"))
    return (
        query_grad.reshape(1, tokens, width),
        key_grad.astype(jnp.bfloat16),
        value_grad.astype(jnp.bfloat16),
        sink_grad,
    )


CHUNKS = (2, 3)


def body(queries, key_states, values, out_grad, block_links, sink_logit):
    heads = sink_logit.shape[0]
    blocks = lax.axis_size("dp")
    groups = lax.axis_size("ctx")
    fits = (
        blocks == 4
        and queries.shape[:2] == (1, BLOCK)
        and queries.shape[2] == heads * BLOCK
        and heads == 4 * sum(CHUNKS)
        and groups & (groups - 1) == 0
    )
    plan = functools.partial(head_shares_body, CHUNKS) if fits else keys_travel_body
    return plan(queries, key_states, values, out_grad, block_links, sink_logit)


def solution(mesh):
    placed = (
        P("ctx", "dp", None),
        P("ctx", "dp", None),
        P("ctx", "dp", None),
        P("ctx", "dp", None),
        P(None, "dp"),
        P(),
    )
    return jax.shard_map(
        body,
        mesh=mesh,
        in_specs=placed,
        out_specs=(P("ctx", "dp", None), P("ctx", "dp", None), P("ctx", "dp", None), P()),
        check_vma=False,
    )
```

time: 203 us -> 69.9 us (0.34)
  Pallas kernels: 156 us -> 18.2 us
  waiting for transfers between devices: 17 us -> 24.5 us
  local copies, waits for them, and re-layouts: 5.53 us -> 1.45 us
    pallas_call x2, Pallas kernels: 83.5 us -> 5.77 us  [pack(): pl.pallas_call(functools.partial(pack_kernel, offset, width, share), out_...]
    pallas_call x2, Pallas kernels: 62 us -> 4.11 us  [unpack(): pl.pallas_call(functools.partial(unpack_kernel, offset, width, share), ou...]
    ppermute x18 -> x17, waiting for transfers between devices: 17 us -> 24.5 us  [swap(): lax.ppermute(value, axis, [(i, i ^ mask) for i in range(lax.axis_size(axi...]
    unnamed x23 -> x24, local copies, waits for them, and re-layouts: 4.79 us -> 0.93 us
    ppermute x18 -> x17, starting transfers between devices: 23.2 us -> 24.7 us  [swap(): lax.ppermute(value, axis, [(i, i ^ mask) for i in range(lax.axis_size(axi...]
  transfers between devices with their start and end apart: 18 -> 17, of which waited for: 7 -> 11; matrix products, arithmetic and copies ran while one was open for 0% -> 1% of each run, Pallas kernels for 40% -> 19%
where the time goes in v2:
time: 69.9 us; the launch traced here: 69.6 us
  starting transfers between devices  24.7 us (35%)
  waiting for transfers between devices  24.5 us (35%)
  Pallas kernels  18.2 us (26%)
  local copies, waits for them, and re-layouts  1.45 us (2%)
  between operations  0.81 us (1%)
    ppermute x17, starting transfers between devices, swap(): lax.ppermute(value, axis, [(i, i ^ mask) for i in range(lax.axis_size(axi...  24.7 us
    ppermute x17, waiting for transfers between devices, swap(): lax.ppermute(value, axis, [(i, i ^ mask) for i in range(lax.axis_size(axi...  24.5 us
    pallas_call x2, Pallas kernels, attend(): pl.pallas_call(functools.partial(attend_kernel, first_head, heads, heads_...  8.31 us
    pallas_call x2, Pallas kernels, pack(): pl.pallas_call(functools.partial(pack_kernel, offset, width, share), out_...  5.77 us
    pallas_call x2, Pallas kernels, unpack(): pl.pallas_call(functools.partial(unpack_kernel, offset, width, share), ou...  4.11 us
  transfers between devices with their start and end apart: 17, of which 11 were waited for; matrix products, arithmetic and copies ran while one was open for 1% of the time, Pallas kernels for 19%

profile of v2, /device:TPU:0, one launch (start us, length us, event | category | flops | bytes accessed | tf_op | source)
XLA Modules:
  0.0 69.6 jit_solution(9981056902660804185)
XLA Ops:
  0.6 2.7 %pack.3 = (bf16[528,256]{1,0:T(8,128)(2,1)}, bf16[528,256]{1,0:T(8,128)(2,1)}, bf16[528,256]{1,0:T(8,128)(2,1)}) custom-call(s32[2]{0:T(128)} %bitcast.5, bf16[1,128,2560]{2,1,0:T(8,128)(2,1)} %refs_0_.7, bf16[1,128,2560]{2,1,0:T(8,128)(2,1)} %refs_1_.7, bf16[1,128,2560]{2,1,0:T(8,128)(2,1)} %refs_2_.7, bf16[1,128,2560]{2,1,0:T(8,128)(2,1)} %refs_3_.7), custom_call_target="tpu_custom_call" | custom-call | bytes 1622016 | tf_op jit(solution)/shard_map/pack/pallas_call | solution.py:56
  3.3 4.0 %collective-permute-start.3 = (bf16[528,256]{1,0:T(8,128)(2,1)}, bf16[528,256]{1,0:T(8,128)(2,1)S(1)}, u32[]{:S(2)}, u32[]{:S(2)}) collective-permute-start(bf16[528,256]{1,0:T(8,128)(2,1)} %get-tuple-element.69), channel_id=1, source_target_pairs={{0,24},{8,16},{16,8},{24,0},{1,25},{9,17},{17,9},{25,1},{2,26},{10... | collective-permute-start | bytes 811016 | tf_op jit(solution)/shard_map/ppermute | solution.py:275
  8.0 3.1 %pack.2 = (bf16[528,384]{1,0:T(8,128)(2,1)}, bf16[528,384]{1,0:T(8,128)(2,1)}, bf16[528,384]{1,0:T(8,128)(2,1)}) custom-call(s32[2]{0:T(128)} %bitcast.6, bf16[1,128,2560]{2,1,0:T(8,128)(2,1)} %refs_0_.7, bf16[1,128,2560]{2,1,0:T(8,128)(2,1)} %refs_1_.7, bf16[1,128,2560]{2,1,0:T(8,128)(2,1)} %refs_2_.7, bf16[1,128,2560]{2,1,0:T(8,128)(2,1)} %refs_3_.7), custom_call_target="tpu_custom_call" | custom-call | bytes 2433024 | tf_op jit(solution)/shard_map/pack/pallas_call | solution.py:56
  11.1 3.7 %collective-permute-done.3.refs_4_ = bf16[528,256]{1,0:T(8,128)(2,1)S(1)} collective-permute-done((bf16[528,256]{1,0:T(8,128)(2,1)}, bf16[528,256]{1,0:T(8,128)(2,1)S(1)}, u32[]{:S(2)}, u32[]{:S(2)}) %collective-permute-start.3) | collective-permute-done | bytes 270368 | tf_op jit(solution)/shard_map/ppermute | solution.py:275
  14.8 3.0 %collective-permute-start.6 = (bf16[528,384]{1,0:T(8,128)(2,1)}, bf16[528,384]{1,0:T(8,128)(2,1)S(1)}, u32[]{:S(2)}, u32[]{:S(2)}) collective-permute-start(bf16[528,384]{1,0:T(8,128)(2,1)} %get-tuple-element.81), channel_id=1, source_target_pairs={{0,24},{8,16},{16,8},{24,0},{1,25},{9,17},{17,9},{25,1},{2,26},{10... | collective-permute-start | bytes 1216520 | tf_op jit(solution)/shard_map/ppermute | solution.py:275
  17.8 3.4 %collective-permute-done.4.refs_5_ = bf16[528,256]{1,0:T(8,128)(2,1)S(1)} collective-permute-done((bf16[528,256]{1,0:T(8,128)(2,1)}, bf16[528,256]{1,0:T(8,128)(2,1)S(1)}, u32[]{:S(2)}, u32[]{:S(2)}) %collective-permute-start.4) | collective-permute-done | bytes 270368 | tf_op jit(solution)/shard_map/ppermute | solution.py:275
  21.2 1.6 %collective-permute-start.7 = (bf16[528,384]{1,0:T(8,128)(2,1)}, bf16[528,384]{1,0:T(8,128)(2,1)S(1)}, u32[]{:S(2)}, u32[]{:S(2)}) collective-permute-start(bf16[528,384]{1,0:T(8,128)(2,1)} %get-tuple-element.85), channel_id=1, source_target_pairs={{0,8},{8,0},{16,24},{24,16},{1,9},{9,1},{17,25},{25,17},{2,10},{10... | collective-permute-start | bytes 1216520 | tf_op jit(solution)/shard_map/ppermute | solution.py:275
  24.1 3.6 %attend.2 = (bf16[384,256]{1,0:T(8,128)(2,1)S(1)}, bf16[384,256]{1,0:T(8,128)(2,1)S(1)}, bf16[384,256]{1,0:T(8,128)(2,1)S(1)}, bf16[1,128,2560]{2,1,0:T(8,128)(2...) custom-call(f32[20]{0:T(128)S(1)} %copy-done.5, s32[2]{0:T(128)S(1)} %bitcast.7, ...), custom_call_target="tpu_custom_call" | custom-call | tf_op jit(solution)/shard_map/attend/pallas_call | solution.py:218
  27.7 1.7 %collective-permute-done.6.refs_4_ = bf16[528,384]{1,0:T(8,128)(2,1)S(1)} collective-permute-done((bf16[528,384]{1,0:T(8,128)(2,1)}, bf16[528,384]{1,0:T(8,128)(2,1)S(1)}, u32[]{:S(2)}, u32[]{:S(2)}) %collective-permute-start.6) | collective-permute-done | bytes 405536 | tf_op jit(solution)/shard_map/ppermute | solution.py:275
  29.4 3.0 %collective-permute-start.9 = (bf16[384,256]{1,0:T(8,128)(2,1)S(1)}, bf16[384,256]{1,0:T(8,128)(2,1)S(1)}, u32[]{:S(2)}, u32[]{:S(2)}) collective-permute-start(bf16[384,256]{1,0:T(8,128)(2,1)S(1)} %get-tuple-element.91), channel_id=1, source_target_pairs={{0,24},{8,16},{16,8},{24,0},{1,25},{9,17},{17,9},{25,1},{2,26},{10... | collective-permute-start | bytes 589832 | tf_op jit(solution)/shard_map/ppermute | solution.py:275
  32.9 5.7 %collective-permute-done.7.refs_5_ = bf16[528,384]{1,0:T(8,128)(2,1)S(1)} collective-permute-done((bf16[528,384]{1,0:T(8,128)(2,1)}, bf16[528,384]{1,0:T(8,128)(2,1)S(1)}, u32[]{:S(2)}, u32[]{:S(2)}) %collective-permute-start.7) | collective-permute-done | bytes 405536 | tf_op jit(solution)/shard_map/ppermute | solution.py:275
  38.6 4.7 %attend.3 = (bf16[384,384]{1,0:T(8,128)(2,1)S(1)}, bf16[384,384]{1,0:T(8,128)(2,1)S(1)}, bf16[384,384]{1,0:T(8,128)(2,1)}, bf16[1,128,2560]{2,1,0:T(8,128)(2,1)}...) custom-call(f32[20]{0:T(128)S(1)} %copy-done.5, ...), custom_call_target="tpu_custom_call", output_to_operand_aliasing={{3}: (10, {}), {4}: (11, {}), {5}: (12, {})} | custom-call | tf_op jit(solution)/shard_map/attend/pallas_call | solution.py:218
  43.4 2.2 %collective-permute-done.13.refs_2_ = bf16[384,256]{1,0:T(8,128)(2,1)S(1)} collective-permute-done((bf16[384,256]{1,0:T(8,128)(2,1)S(1)}, bf16[384,256]{1,0:T(8,128)(2,1)S(1)}, u32[]{:S(2)}, u32[]{:S(2)}) %collective-permute-start.13) | collective-permute-done | bytes 196640 | tf_op jit(solution)/shard_map/ppermute | solution.py:275
  45.9 1.4 %collective-permute-start.14 = (bf16[384,384]{1,0:T(8,128)(2,1)}, bf16[384,384]{1,0:T(8,128)(2,1)S(1)}, u32[]{:S(2)}, u32[]{:S(2)}) collective-permute-start(bf16[384,384]{1,0:T(8,128)(2,1)} %get-tuple-element.98), channel_id=1, source_target_pairs={{0,16},{8,24},{16,0},{24,8},{1,17},{9,25},{17,1},{25,9},{2,18},{10... | collective-permute-start | bytes 884744 | tf_op jit(solution)/shard_map/ppermute | solution.py:275
  47.4 1.5 %collective-permute-start.12 = (bf16[384,384]{1,0:T(8,128)(2,1)S(1)}, bf16[384,384]{1,0:T(8,128)(2,1)S(1)}, u32[]{:S(2)}, u32[]{:S(2)}) collective-permute-start(bf16[384,384]{1,0:T(8,128)(2,1)S(1)} %get-tuple-element.95), channel_id=1, source_target_pairs={{0,8},{8,0},{16,24},{24,16},{1,9},{9,1},{17,25},{25,17},{2,10},{10... | collective-permute-start | bytes 884744 | tf_op jit(solution)/shard_map/ppermute | solution.py:275
  49.5 9.4 %while.10 = (s32[]{:T(128)}, f32[8,128]{1,0:T(8,128)S(1)}, s32[]{:T(128)}, s32[]{:T(128)}) while((s32[]{:T(128)}, f32[8,128]{1,0:T(8,128)S(1)}, s32[]{:T(128)}, s32[]{:T(128)}) %tuple.42), condition=%wide.region_1.0_spmd, body=%wide.region_0.0_spmd.sunk | while | flops 3074 | bytes 86189 | solution.py:324
  50.7 1.6 %collective-permute-start.1 = (f32[8,128]{1,0:T(8,128)S(1)}, f32[8,128]{1,0:T(8,128)S(1)}, u32[]{:S(2)}, u32[]{:S(2)}) collective-permute-start(f32[8,128]{1,0:T(8,128)S(1)} %add.30), channel_id=1, source_target_pairs={{0,2},{1,3},{2,0},{3,1},{4,6},{5,7},{6,4},{7,5},{8,10},{9,11},{10,... | collective-permute-start | bytes 12296 | tf_op jit(solution)/shard_map/while/body/ppermute | solution.py:275
  52.3 2.0 %collective-permute-done.1 = f32[8,128]{1,0:T(8,128)S(1)} collective-permute-done((f32[8,128]{1,0:T(8,128)S(1)}, f32[8,128]{1,0:T(8,128)S(1)}, u32[]{:S(2)}, u32[]{:S(2)}) %collective-permute-start.1) | collective-permute-done | bytes 4128 | tf_op jit(solution)/shard_map/while/body/ppermute | solution.py:275
  54.4 2.6 %collective-permute-start.2 = (f32[8,128]{1,0:T(8,128)S(1)}, f32[8,128]{1,0:T(8,128)S(1)}, u32[]{:S(2)}, u32[]{:S(2)}) collective-permute-start(f32[8,128]{1,0:T(8,128)S(1)} %add.31), channel_id=1, source_target_pairs={{0,4},{1,5},{2,6},{3,7},{4,0},{5,1},{6,2},{7,3},{8,12},{9,13},{10,... | collective-permute-start | bytes 12296 | tf_op jit(solution)/shard_map/while/body/ppermute | solution.py:275
  56.9 1.9 %collective-permute-done.2 = f32[8,128]{1,0:T(8,128)S(1)} collective-permute-done((f32[8,128]{1,0:T(8,128)S(1)}, f32[8,128]{1,0:T(8,128)S(1)}, u32[]{:S(2)}, u32[]{:S(2)}) %collective-permute-start.2) | collective-permute-done | bytes 4128 | tf_op jit(solution)/shard_map/while/body/ppermute | solution.py:275
  58.9 1.5 %collective-permute-start.15 = (f32[8,128]{1,0:T(8,128)S(1)}, f32[8,128]{1,0:T(8,128)S(1)}, u32[]{:S(2)}, u32[]{:S(2)}) collective-permute-start(f32[8,128]{1,0:T(8,128)S(1)} %get-tuple-element.114), channel_id=1, source_target_pairs={{0,8},{8,0},{16,24},{24,16},{1,9},{9,1},{17,25},{25,17},{2,10},{10... | collective-permute-start | bytes 12296 | tf_op jit(solution)/shard_map/ppermute | solution.py:275
  60.4 2.1 %collective-permute-done.15 = f32[8,128]{1,0:T(8,128)S(1)} collective-permute-done((f32[8,128]{1,0:T(8,128)S(1)}, f32[8,128]{1,0:T(8,128)S(1)}, u32[]{:S(2)}, u32[]{:S(2)}) %collective-permute-start.15) | collective-permute-done | bytes 4128 | tf_op jit(solution)/shard_map/ppermute | solution.py:275
  63.9 2.0 %unpack.2 = (bf16[1,128,2560]{2,1,0:T(8,128)(2,1)}, bf16[1,128,2560]{2,1,0:T(8,128)(2,1)}, bf16[1,128,2560]{2,1,0:T(8,128)(2,1)}) custom-call(bf16[384,256]{1,0:T(8,128)(2,1)} %copy-done.9, bf16[384,256]{1,0:T(8,128)(2,1)} %copy-done.11, bf16[384,256]{1,0:T(8,128)(2,1)} %copy-done.10, ...), custom_call_target="tpu_custom_call", output_to_operand_aliasing={{0}: (3, {}), {1}: (4, {}), {2}: (5, {})} | custom-call | bytes 786432 | tf_op jit(solution)/shard_map/unpack/pallas_call | solution.py:262
  67.5 2.1 %unpack.3 = (bf16[1,128,2560]{2,1,0:T(8,128)(2,1)}, bf16[1,128,2560]{2,1,0:T(8,128)(2,1)}, bf16[1,128,2560]{2,1,0:T(8,128)(2,1)}) custom-call(bf16[384,384]{1,0:T(8,128)(2,1)} %copy-done.8, bf16[384,384]{1,0:T(8,128)(2,1)} %copy-done.7, bf16[384,384]{1,0:T(8,128)(2,1)} %copy-done.6, ...), custom_call_target="tpu_custom_call", output_to_operand_aliasing={{0}: (3, {}), {1}: (4, {}), {2}: (5, {})} | custom-call | bytes 1179648 | tf_op jit(solution)/shard_map/unpack/pallas_call | solution.py:262
  (48 shorter events, 7.8 us)
Async XLA Ops:
  3.3 11.5 %collective-permute-start.3 = (bf16[528,256]{1,0:T(8,128)(2,1)}, bf16[528,256]{1,0:T(8,128)(2,1)S(1)}, u32[]{:S(2)}, u32[]{:S(2)}) collective-permute-start(bf16[528,256]{1,0:T(8,128)(2,1)} %get-tuple-element.69), channel_id=1, source_target_pairs={{0,24},{8,16},{16,8},{24,0},{1,25},{9,17},{17,9},{25,1},{2,26},{10... | collective-permute-start | bytes 811016 | tf_op jit(solution)/shard_map/ppermute | solution.py:275
  7.3 13.9 %collective-permute-start.4 = (bf16[528,256]{1,0:T(8,128)(2,1)}, bf16[528,256]{1,0:T(8,128)(2,1)S(1)}, u32[]{:S(2)}, u32[]{:S(2)}) collective-permute-start(bf16[528,256]{1,0:T(8,128)(2,1)} %get-tuple-element.72), channel_id=1, source_target_pairs={{0,8},{8,0},{16,24},{24,16},{1,9},{9,1},{17,25},{25,17},{2,10},{10... | collective-permute-start | bytes 811016 | tf_op jit(solution)/shard_map/ppermute | solution.py:275
  7.8 16.3 %copy-start = (bf16[1,128,2560]{2,1,0:T(8,128)(2,1)S(1)}, bf16[1,128,2560]{2,1,0:T(8,128)(2,1)}, u32[]{:S(2)}) copy-start(bf16[1,128,2560]{2,1,0:T(8,128)(2,1)} %refs_0_.7) | copy-start | bytes 1966084
  7.8 16.3 %copy-start.1 = (bf16[1,128,2560]{2,1,0:T(8,128)(2,1)S(1)}, bf16[1,128,2560]{2,1,0:T(8,128)(2,1)}, u32[]{:S(2)}) copy-start(bf16[1,128,2560]{2,1,0:T(8,128)(2,1)} %refs_1_.7) | copy-start | bytes 1966084
  7.8 16.3 %copy-start.2 = (bf16[1,128,2560]{2,1,0:T(8,128)(2,1)S(1)}, bf16[1,128,2560]{2,1,0:T(8,128)(2,1)}, u32[]{:S(2)}) copy-start(bf16[1,128,2560]{2,1,0:T(8,128)(2,1)} %refs_2_.7) | copy-start | bytes 1966084
  7.8 16.3 %copy-start.3 = (bf16[1,128,2560]{2,1,0:T(8,128)(2,1)S(1)}, bf16[1,128,2560]{2,1,0:T(8,128)(2,1)}, u32[]{:S(2)}) copy-start(bf16[1,128,2560]{2,1,0:T(8,128)(2,1)} %refs_3_.7) | copy-start | bytes 1966084
  7.8 13.4 %collective-permute-start.5 = (bf16[528,256]{1,0:T(8,128)(2,1)}, bf16[528,256]{1,0:T(8,128)(2,1)S(1)}, u32[]{:S(2)}, u32[]{:S(2)}) collective-permute-start(bf16[528,256]{1,0:T(8,128)(2,1)} %get-tuple-element.75), channel_id=1, source_target_pairs={{0,16},{8,24},{16,0},{24,8},{1,17},{9,25},{17,1},{25,9},{2,18},{10... | collective-permute-start | bytes 811016 | tf_op jit(solution)/shard_map/ppermute | solution.py:275
  14.8 14.5 %collective-permute-start.6 = (bf16[528,384]{1,0:T(8,128)(2,1)}, bf16[528,384]{1,0:T(8,128)(2,1)S(1)}, u32[]{:S(2)}, u32[]{:S(2)}) collective-permute-start(bf16[528,384]{1,0:T(8,128)(2,1)} %get-tuple-element.81), channel_id=1, source_target_pairs={{0,24},{8,16},{16,8},{24,0},{1,25},{9,17},{17,9},{25,1},{2,26},{10... | collective-permute-start | bytes 1216520 | tf_op jit(solution)/shard_map/ppermute | solution.py:275
  21.2 17.4 %collective-permute-start.7 = (bf16[528,384]{1,0:T(8,128)(2,1)}, bf16[528,384]{1,0:T(8,128)(2,1)S(1)}, u32[]{:S(2)}, u32[]{:S(2)}) collective-permute-start(bf16[528,384]{1,0:T(8,128)(2,1)} %get-tuple-element.85), channel_id=1, source_target_pairs={{0,8},{8,0},{16,24},{24,16},{1,9},{9,1},{17,25},{25,17},{2,10},{10... | collective-permute-start | bytes 1216520 | tf_op jit(solution)/shard_map/ppermute | solution.py:275
  22.8 15.9 %collective-permute-start.8 = (bf16[528,384]{1,0:T(8,128)(2,1)}, bf16[528,384]{1,0:T(8,128)(2,1)S(1)}, u32[]{:S(2)}, u32[]{:S(2)}) collective-permute-start(bf16[528,384]{1,0:T(8,128)(2,1)} %get-tuple-element.86), channel_id=1, source_target_pairs={{0,16},{8,24},{16,0},{24,8},{1,17},{9,25},{17,1},{25,9},{2,18},{10... | collective-permute-start | bytes 1216520 | tf_op jit(solution)/shard_map/ppermute | solution.py:275
  29.4 14.0 %collective-permute-start.9 = (bf16[384,256]{1,0:T(8,128)(2,1)S(1)}, bf16[384,256]{1,0:T(8,128)(2,1)S(1)}, u32[]{:S(2)}, u32[]{:S(2)}) collective-permute-start(bf16[384,256]{1,0:T(8,128)(2,1)S(1)} %get-tuple-element.91), channel_id=1, source_target_pairs={{0,24},{8,16},{16,8},{24,0},{1,25},{9,17},{17,9},{25,1},{2,26},{10... | collective-permute-start | bytes 589832 | tf_op jit(solution)/shard_map/ppermute | solution.py:275
  32.3 13.3 %collective-permute-start.13 = (bf16[384,256]{1,0:T(8,128)(2,1)S(1)}, bf16[384,256]{1,0:T(8,128)(2,1)S(1)}, u32[]{:S(2)}, u32[]{:S(2)}) collective-permute-start(bf16[384,256]{1,0:T(8,128)(2,1)S(1)} %get-tuple-element.97), channel_id=1, source_target_pairs={{0,16},{8,24},{16,0},{24,8},{1,17},{9,25},{17,1},{25,9},{2,18},{10... | collective-permute-start | bytes 589832 | tf_op jit(solution)/shard_map/ppermute | solution.py:275
  32.8 13.1 %collective-permute-start.11 = (bf16[384,256]{1,0:T(8,128)(2,1)S(1)}, bf16[384,256]{1,0:T(8,128)(2,1)S(1)}, u32[]{:S(2)}, u32[]{:S(2)}) collective-permute-start(bf16[384,256]{1,0:T(8,128)(2,1)S(1)} %get-tuple-element.94), channel_id=1, source_target_pairs={{0,8},{8,0},{16,24},{24,16},{1,9},{9,1},{17,25},{25,17},{2,10},{10... | collective-permute-start | bytes 589832 | tf_op jit(solution)/shard_map/ppermute | solution.py:275
  43.4 20.5 %copy-start.9 = (bf16[384,256]{1,0:T(8,128)(2,1)}, bf16[384,256]{1,0:T(8,128)(2,1)S(1)}, u32[]{:S(2)}) copy-start(bf16[384,256]{1,0:T(8,128)(2,1)S(1)} %collective-permute-done.9.refs_0_) | copy-start | bytes 589828
  45.6 3.3 %copy-start.10 = (bf16[384,256]{1,0:T(8,128)(2,1)}, bf16[384,256]{1,0:T(8,128)(2,1)S(1)}, u32[]{:S(2)}) copy-start(bf16[384,256]{1,0:T(8,128)(2,1)S(1)} %collective-permute-done.13.refs_2_) | copy-start | bytes 589828
  45.9 2.9 %copy-start.11 = (bf16[384,256]{1,0:T(8,128)(2,1)}, bf16[384,256]{1,0:T(8,128)(2,1)S(1)}, u32[]{:S(2)}) copy-start(bf16[384,256]{1,0:T(8,128)(2,1)S(1)} %collective-permute-done.11.refs_1_) | copy-start | bytes 589828
  45.9 20.7 %collective-permute-start.14 = (bf16[384,384]{1,0:T(8,128)(2,1)}, bf16[384,384]{1,0:T(8,128)(2,1)S(1)}, u32[]{:S(2)}, u32[]{:S(2)}) collective-permute-start(bf16[384,384]{1,0:T(8,128)(2,1)} %get-tuple-element.98), channel_id=1, source_target_pairs={{0,16},{8,24},{16,0},{24,8},{1,17},{9,25},{17,1},{25,9},{2,18},{10... | collective-permute-start | bytes 884744 | tf_op jit(solution)/shard_map/ppermute | solution.py:275
  47.4 19.2 %collective-permute-start.12 = (bf16[384,384]{1,0:T(8,128)(2,1)S(1)}, bf16[384,384]{1,0:T(8,128)(2,1)S(1)}, u32[]{:S(2)}, u32[]{:S(2)}) collective-permute-start(bf16[384,384]{1,0:T(8,128)(2,1)S(1)} %get-tuple-element.95), channel_id=1, source_target_pairs={{0,8},{8,0},{16,24},{24,16},{1,9},{9,1},{17,25},{25,17},{2,10},{10... | collective-permute-start | bytes 884744 | tf_op jit(solution)/shard_map/ppermute | solution.py:275
  48.9 17.7 %collective-permute-start.10 = (bf16[384,384]{1,0:T(8,128)(2,1)S(1)}, bf16[384,384]{1,0:T(8,128)(2,1)S(1)}, u32[]{:S(2)}, u32[]{:S(2)}) collective-permute-start(bf16[384,384]{1,0:T(8,128)(2,1)S(1)} %get-tuple-element.92), channel_id=1, source_target_pairs={{0,24},{8,16},{16,8},{24,0},{1,25},{9,17},{17,9},{25,1},{2,26},{10... | collective-permute-start | bytes 884744 | tf_op jit(solution)/shard_map/ppermute | solution.py:275
  49.5 1.2 %collective-permute-start = (f32[8,128]{1,0:T(8,128)S(1)}, f32[8,128]{1,0:T(8,128)S(1)}, u32[]{:S(2)}, u32[]{:S(2)}) collective-permute-start(f32[8,128]{1,0:T(8,128)S(1)} %get-tuple-element.146), channel_id=1, source_target_pairs={{0,1},{1,0},{2,3},{3,2},{4,5},{5,4},{6,7},{7,6},{8,9},{9,8},{10,11... | collective-permute-start | bytes 12296 | tf_op jit(solution)/shard_map/while/body/ppermute | solution.py:275
  50.7 3.6 %collective-permute-start.1 = (f32[8,128]{1,0:T(8,128)S(1)}, f32[8,128]{1,0:T(8,128)S(1)}, u32[]{:S(2)}, u32[]{:S(2)}) collective-permute-start(f32[8,128]{1,0:T(8,128)S(1)} %add.30), channel_id=1, source_target_pairs={{0,2},{1,3},{2,0},{3,1},{4,6},{5,7},{6,4},{7,5},{8,10},{9,11},{10,... | collective-permute-start | bytes 12296 | tf_op jit(solution)/shard_map/while/body/ppermute | solution.py:275
  54.4 4.5 %collective-permute-start.2 = (f32[8,128]{1,0:T(8,128)S(1)}, f32[8,128]{1,0:T(8,128)S(1)}, u32[]{:S(2)}, u32[]{:S(2)}) collective-permute-start(f32[8,128]{1,0:T(8,128)S(1)} %add.31), channel_id=1, source_target_pairs={{0,4},{1,5},{2,6},{3,7},{4,0},{5,1},{6,2},{7,3},{8,12},{9,13},{10,... | collective-permute-start | bytes 12296 | tf_op jit(solution)/shard_map/while/body/ppermute | solution.py:275
  58.9 3.6 %collective-permute-start.15 = (f32[8,128]{1,0:T(8,128)S(1)}, f32[8,128]{1,0:T(8,128)S(1)}, u32[]{:S(2)}, u32[]{:S(2)}) collective-permute-start(f32[8,128]{1,0:T(8,128)S(1)} %get-tuple-element.114), channel_id=1, source_target_pairs={{0,8},{8,0},{16,24},{24,16},{1,9},{9,1},{17,25},{25,17},{2,10},{10... | collective-permute-start | bytes 12296 | tf_op jit(solution)/shard_map/ppermute | solution.py:275
  62.5 3.6 %collective-permute-start.16 = (f32[8,128]{1,0:T(8,128)S(1)}, f32[8,128]{1,0:T(8,128)S(1)}, u32[]{:S(2)}, u32[]{:S(2)}) collective-permute-start(f32[8,128]{1,0:T(8,128)S(1)} %add.23), channel_id=1, source_target_pairs={{0,16},{8,24},{16,0},{24,8},{1,17},{9,25},{17,1},{25,9},{2,18},{10... | collective-permute-start | bytes 12296 | tf_op jit(solution)/shard_map/ppermute | solution.py:275
  (5 other events, 8.2 us)

commit v3 on v2

--- a/solution.py
+++ b/solution.py
@@ -231,42 +231,52 @@
             pltpu.SemaphoreType.DMA((heads, 3)),
         ],
         input_output_aliases={10 + num: 3 + num for num in range(len(previous))},
-        compiler_params=pltpu.CompilerParams(vmem_limit_bytes=32 * 2**20),
+        compiler_params=pltpu.CompilerParams(vmem_limit_bytes=8 * 2**20),
         cost_estimate=pl.CostEstimate(flops=0, bytes_accessed=0, transcendentals=0),
         name="attend",
     )(sink_logit, links, sink_sum, *arrays, *packed, *previous)
 
 
 def unpack_kernel(offset, width, share, *refs):
-    ins, outs, sems = refs[:3], refs[6:9], refs[9]
+    ins, outs, (held, load_sems, store_sems) = refs[:3], refs[6:9], refs[9:]
     me = lax.axis_index("dp")
-    copies = []
+    loads = [
+        pltpu.make_async_copy(ins[place], held.at[place], load_sems.at[place]) for place in range(3)
+    ]
+    for copy in loads:
+        copy.start()
+    stores = []
     for place, mask in enumerate(ORDER):
+        loads[place].wait()
         start = pl.multiple_of((me ^ mask) * share + offset, BLOCK)
         for num, out in enumerate(outs):
-            copies.append(
+            stores.append(
                 pltpu.make_async_copy(
-                    ins[place].at[pl.ds(num * BLOCK, BLOCK), :],
+                    held.at[place, pl.ds(num * BLOCK, BLOCK), :],
                     out.at[0, :, pl.ds(start, width)],
-                    sems.at[place, num],
+                    store_sems.at[place, num],
                 )
             )
-    for copy in copies:
-        copy.start()
-    for copy in copies:
+            stores[-1].start()
+    for copy in stores:
         copy.wait()
 
 
 def unpack(parts, previous, offset, share):
-    width = parts[0].shape[1]
+    rows, width = parts[0].shape
     return pl.pallas_call(
         functools.partial(unpack_kernel, offset, width, share),
         out_shape=[jax.ShapeDtypeStruct(out.shape, out.dtype) for out in previous],
-        in_specs=[pl.BlockSpec(memory_space=pltpu.VMEM)] * 3 + [pl.BlockSpec(memory_space=pl.ANY)] * 3,
+        in_specs=[pl.BlockSpec(memory_space=pl.ANY)] * 6,
         out_specs=[pl.BlockSpec(memory_space=pl.ANY)] * 3,
-        scratch_shapes=[pltpu.SemaphoreType.DMA((3, 3))],
+        scratch_shapes=[
+            pltpu.VMEM((3, rows, width), jnp.bfloat16),
+            pltpu.SemaphoreType.DMA((3,)),
+            pltpu.SemaphoreType.DMA((3, 3)),
+        ],
         input_output_aliases={3 + num: num for num in range(3)},
-        cost_estimate=pl.CostEstimate(flops=0, bytes_accessed=8 * 3 * BLOCK * width, transcendentals=0),
+        compiler_params=pltpu.CompilerParams(vmem_limit_bytes=8 * 2**20),
+        cost_estimate=pl.CostEstimate(flops=0, bytes_accessed=0, transcendentals=0),
         name="unpack",
     )(*parts, *previous)
 
@@ -297,12 +307,8 @@
     links = block_links.reshape(LEVELS)
     received, first = [], 0
     for count in chunks:
-        packed = list(pack(links, arrays, first * head_size, count * head_size, share))
-        moved = [None] * 3
-        for place, mask in enumerate(ORDER):
-            if received:
-                packed[place], received[-1][2][place] = after(packed[place], received[-1][2][place])
-            moved[place] = swap(packed[place], "dp", mask)
+        packed = pack(links, arrays, first * head_size, count * head_size, share)
+        moved = [swap(part, "dp", mask) for part, mask in zip(packed, ORDER)]
         received.append((first, count, moved))
         first += count
     results, outputs, sink_sum = [], [], jnp.zeros((8, BLOCK), jnp.float32)
@@ -311,15 +317,13 @@
             sink_logit, links, sink_sum, arrays, packed, outputs, first, count, heads_dev, score_scale
         )
         grads, outputs = grads[:3], grads[3:]
-        moved = [None] * 3
-        for place, mask in enumerate(ORDER):
-            if num:
-                grads[place], results[-1][1][place] = after(grads[place], results[-1][1][place])
-            else:
+        if num:
+            grads[0], results[0][1][0] = after(grads[0], results[0][1][0])
+        else:
+            for place in (1, 2):
                 grads[place], received[1][2][0] = after(grads[place], received[1][2][0])
-            moved[place] = swap(grads[place], "dp", mask)
-        results.append((first, moved))
-    sink_sum, results[0][1][0] = after(sink_sum, results[0][1][0])
+        results.append((first, [swap(grad, "dp", mask) for grad, mask in zip(grads, ORDER)]))
+    sink_sum, results[0][1][2] = after(sink_sum, results[0][1][2])
     once = jnp.minimum(links[0] + 2, 1)
     sink_sum = lax.fori_loop(0, once, lambda _, held: butterfly(held, "ctx"), sink_sum)
     sink_sum = butterfly(sink_sum, "dp")

time: 69.9 us -> 65.5 us (0.937)
  waiting for transfers between devices: 24.5 us -> 22.3 us
  Pallas kernels: 18.2 us -> 16.7 us
  local copies, waits for them, and re-layouts: 1.45 us -> 0.55 us
    ppermute x17, waiting for transfers between devices: 24.5 us -> 22.3 us  [swap(): lax.ppermute(value, axis, [(i, i ^ mask) for i in range(lax.axis_size(axi...]
    pallas_call x2, Pallas kernels: 4.11 us -> 2.84 us  [unpack(): pl.pallas_call(functools.partial(unpack_kernel, offset, width, share), ou...]
    unnamed x24 -> x12, local copies, waits for them, and re-layouts: 0.93 us -> 0.03 us
  transfers between devices with their start and end apart: 17 -> 17, of which waited for: 11 -> 8; matrix products, arithmetic and copies ran while one was open for 1% -> 1% of each run, Pallas kernels for 19% -> 20%
where the time goes in v3:
time: 65.5 us; the launch traced here: 65.3 us
  starting transfers between devices  24.8 us (38%)
  waiting for transfers between devices  22.3 us (34%)
  Pallas kernels  16.7 us (25%)
  between operations  0.82 us (1%)
    ppermute x17, starting transfers between devices, swap(): lax.ppermute(value, axis, [(i, i ^ mask) for i in range(lax.axis_size(axi...  24.8 us
    ppermute x17, waiting for transfers between devices, swap(): lax.ppermute(value, axis, [(i, i ^ mask) for i in range(lax.axis_size(axi...  22.3 us
    pallas_call x2, Pallas kernels, attend(): pl.pallas_call(functools.partial(attend_kernel, first_head, heads, heads_...  8.3 us
    pallas_call x2, Pallas kernels, pack(): pl.pallas_call(functools.partial(pack_kernel, offset, width, share), out_...  5.61 us
    pallas_call x2, Pallas kernels, unpack(): pl.pallas_call(functools.partial(unpack_kernel, offset, width, share), ou...  2.84 us
  transfers between devices with their start and end apart: 17, of which 8 were waited for; matrix products, arithmetic and copies ran while one was open for 1% of the time, Pallas kernels for 20%

profile of v3, /device:TPU:0, one launch (start us, length us, event | category | flops | bytes accessed | tf_op | source)
XLA Modules:
  0.0 65.3 jit_solution(5527565519880235641)
XLA Ops:
  0.6 2.7 %pack.2 = (bf16[528,256]{1,0:T(8,128)(2,1)}, bf16[528,256]{1,0:T(8,128)(2,1)}, bf16[528,256]{1,0:T(8,128)(2,1)}) custom-call(s32[2]{0:T(128)} %bitcast.5, bf16[1,128,2560]{2,1,0:T(8,128)(2,1)} %refs_0_.7, bf16[1,128,2560]{2,1,0:T(8,128)(2,1)} %refs_1_.7, bf16[1,128,2560]{2,1,0:T(8,128)(2,1)} %refs_2_.7, bf16[1,128,2560]{2,1,0:T(8,128)(2,1)} %refs_3_.7), custom_call_target="tpu_custom_call" | custom-call | bytes 1622016 | tf_op jit(solution)/shard_map/pack/pallas_call | solution.py:56
  3.4 4.0 %collective-permute-start.3 = (bf16[528,256]{1,0:T(8,128)(2,1)}, bf16[528,256]{1,0:T(8,128)(2,1)S(1)}, u32[]{:S(2)}, u32[]{:S(2)}) collective-permute-start(bf16[528,256]{1,0:T(8,128)(2,1)} %get-tuple-element.56), channel_id=1, source_target_pairs={{0,24},{8,16},{16,8},{24,0},{1,25},{9,17},{17,9},{25,1},{2,26},{10... | collective-permute-start | bytes 811016 | tf_op jit(solution)/shard_map/ppermute | solution.py:285
  7.3 2.9 %pack.3 = (bf16[528,384]{1,0:T(8,128)(2,1)}, bf16[528,384]{1,0:T(8,128)(2,1)}, bf16[528,384]{1,0:T(8,128)(2,1)}) custom-call(s32[2]{0:T(128)} %bitcast.6, bf16[1,128,2560]{2,1,0:T(8,128)(2,1)} %refs_0_.7, bf16[1,128,2560]{2,1,0:T(8,128)(2,1)} %refs_1_.7, bf16[1,128,2560]{2,1,0:T(8,128)(2,1)} %refs_2_.7, bf16[1,128,2560]{2,1,0:T(8,128)(2,1)} %refs_3_.7), custom_call_target="tpu_custom_call" | custom-call | bytes 2433024 | tf_op jit(solution)/shard_map/pack/pallas_call | solution.py:56
  10.5 1.8 %collective-permute-start.4 = (bf16[528,256]{1,0:T(8,128)(2,1)}, bf16[528,256]{1,0:T(8,128)(2,1)S(1)}, u32[]{:S(2)}, u32[]{:S(2)}) collective-permute-start(bf16[528,256]{1,0:T(8,128)(2,1)} %get-tuple-element.57), channel_id=1, source_target_pairs={{0,8},{8,0},{16,24},{24,16},{1,9},{9,1},{17,25},{25,17},{2,10},{10... | collective-permute-start | bytes 811016 | tf_op jit(solution)/shard_map/ppermute | solution.py:285
  12.3 1.5 %collective-permute-start.5 = (bf16[528,256]{1,0:T(8,128)(2,1)}, bf16[528,256]{1,0:T(8,128)(2,1)S(1)}, u32[]{:S(2)}, u32[]{:S(2)}) collective-permute-start(bf16[528,256]{1,0:T(8,128)(2,1)} %get-tuple-element.58), channel_id=1, source_target_pairs={{0,16},{8,24},{16,0},{24,8},{1,17},{9,25},{17,1},{25,9},{2,18},{10... | collective-permute-start | bytes 811016 | tf_op jit(solution)/shard_map/ppermute | solution.py:285
  14.6 2.4 %collective-permute-start.8 = (bf16[528,384]{1,0:T(8,128)(2,1)}, bf16[528,384]{1,0:T(8,128)(2,1)S(1)}, u32[]{:S(2)}, u32[]{:S(2)}) collective-permute-start(bf16[528,384]{1,0:T(8,128)(2,1)} %get-tuple-element.66), channel_id=1, source_target_pairs={{0,16},{8,24},{16,0},{24,8},{1,17},{9,25},{17,1},{25,9},{2,18},{10... | collective-permute-start | bytes 1216520 | tf_op jit(solution)/shard_map/ppermute | solution.py:285
  17.0 13.0 %collective-permute-done.4.refs_5_ = bf16[528,256]{1,0:T(8,128)(2,1)S(1)} collective-permute-done((bf16[528,256]{1,0:T(8,128)(2,1)}, bf16[528,256]{1,0:T(8,128)(2,1)S(1)}, u32[]{:S(2)}, u32[]{:S(2)}) %collective-permute-start.4) | collective-permute-done | bytes 270368 | tf_op jit(solution)/shard_map/ppermute | solution.py:285
  30.0 3.6 %attend.2 = (bf16[384,256]{1,0:T(8,128)(2,1)S(1)}, bf16[384,256]{1,0:T(8,128)(2,1)}, bf16[384,256]{1,0:T(8,128)(2,1)}, bf16[1,128,2560]{2,1,0:T(8,128)(2,1)}, bf...) custom-call(f32[20]{0:T(128)S(1)} %copy-done.5, s32[2]{0:T(128)S(1)} %bitcast.7, ...), custom_call_target="tpu_custom_call" | custom-call | tf_op jit(solution)/shard_map/attend/pallas_call | solution.py:218
  33.6 1.5 %collective-permute-start.9 = (bf16[384,256]{1,0:T(8,128)(2,1)S(1)}, bf16[384,256]{1,0:T(8,128)(2,1)S(1)}, u32[]{:S(2)}, u32[]{:S(2)}) collective-permute-start(bf16[384,256]{1,0:T(8,128)(2,1)S(1)} %get-tuple-element.71), channel_id=1, source_target_pairs={{0,24},{8,16},{16,8},{24,0},{1,25},{9,17},{17,9},{25,1},{2,26},{10... | collective-permute-start | bytes 589832 | tf_op jit(solution)/shard_map/ppermute | solution.py:285
  35.1 1.5 %collective-permute-start.14 = (bf16[384,256]{1,0:T(8,128)(2,1)}, bf16[384,256]{1,0:T(8,128)(2,1)S(1)}, u32[]{:S(2)}, u32[]{:S(2)}) collective-permute-start(bf16[384,256]{1,0:T(8,128)(2,1)} %get-tuple-element.78), channel_id=1, source_target_pairs={{0,16},{8,24},{16,0},{24,8},{1,17},{9,25},{17,1},{25,9},{2,18},{10... | collective-permute-start | bytes 589832 | tf_op jit(solution)/shard_map/ppermute | solution.py:285
  37.2 1.5 %collective-permute-done.7.refs_5_ = bf16[528,384]{1,0:T(8,128)(2,1)S(1)} collective-permute-done((bf16[528,384]{1,0:T(8,128)(2,1)}, bf16[528,384]{1,0:T(8,128)(2,1)S(1)}, u32[]{:S(2)}, u32[]{:S(2)}) %collective-permute-start.7) | collective-permute-done | bytes 405536 | tf_op jit(solution)/shard_map/ppermute | solution.py:285
  38.6 4.7 %attend.3 = (bf16[384,384]{1,0:T(8,128)(2,1)S(1)}, bf16[384,384]{1,0:T(8,128)(2,1)}, bf16[384,384]{1,0:T(8,128)(2,1)}, bf16[1,128,2560]{2,1,0:T(8,128)(2,1)}, bf...) custom-call(f32[20]{0:T(128)S(1)} %copy-done.5, ...), custom_call_target="tpu_custom_call", output_to_operand_aliasing={{3}: (10, {}), {4}: (11, {}), {5}: (12, {})} | custom-call | tf_op jit(solution)/shard_map/attend/pallas_call | solution.py:218
  43.3 1.6 %collective-permute-start.11 = (bf16[384,384]{1,0:T(8,128)(2,1)}, bf16[384,384]{1,0:T(8,128)(2,1)S(1)}, u32[]{:S(2)}, u32[]{:S(2)}) collective-permute-start(bf16[384,384]{1,0:T(8,128)(2,1)} %get-tuple-element.73), channel_id=1, source_target_pairs={{0,8},{8,0},{16,24},{24,16},{1,9},{9,1},{17,25},{25,17},{2,10},{10... | collective-permute-start | bytes 884744 | tf_op jit(solution)/shard_map/ppermute | solution.py:285
  44.9 1.5 %collective-permute-start.12 = (bf16[384,384]{1,0:T(8,128)(2,1)}, bf16[384,384]{1,0:T(8,128)(2,1)S(1)}, u32[]{:S(2)}, u32[]{:S(2)}) collective-permute-start(bf16[384,384]{1,0:T(8,128)(2,1)} %get-tuple-element.74), channel_id=1, source_target_pairs={{0,16},{8,24},{16,0},{24,8},{1,17},{9,25},{17,1},{25,9},{2,18},{10... | collective-permute-start | bytes 884744 | tf_op jit(solution)/shard_map/ppermute | solution.py:285
  47.0 9.4 %while.10 = (s32[]{:T(128)}, f32[8,128]{1,0:T(8,128)S(1)}, s32[]{:T(128)}, s32[]{:T(128)}) while((s32[]{:T(128)}, f32[8,128]{1,0:T(8,128)S(1)}, s32[]{:T(128)}, s32[]{:T(128)}) %tuple.30), condition=%wide.region_1.0_spmd, body=%wide.region_0.0_spmd.sunk | while | flops 3074 | bytes 86189 | solution.py:328
  48.2 1.6 %collective-permute-start.1 = (f32[8,128]{1,0:T(8,128)S(1)}, f32[8,128]{1,0:T(8,128)S(1)}, u32[]{:S(2)}, u32[]{:S(2)}) collective-permute-start(f32[8,128]{1,0:T(8,128)S(1)} %add.30), channel_id=1, source_target_pairs={{0,2},{1,3},{2,0},{3,1},{4,6},{5,7},{6,4},{7,5},{8,10},{9,11},{10,... | collective-permute-start | bytes 12296 | tf_op jit(solution)/shard_map/while/body/ppermute | solution.py:285
  49.8 2.0 %collective-permute-done.1 = f32[8,128]{1,0:T(8,128)S(1)} collective-permute-done((f32[8,128]{1,0:T(8,128)S(1)}, f32[8,128]{1,0:T(8,128)S(1)}, u32[]{:S(2)}, u32[]{:S(2)}) %collective-permute-start.1) | collective-permute-done | bytes 4128 | tf_op jit(solution)/shard_map/while/body/ppermute | solution.py:285
  51.8 2.6 %collective-permute-start.2 = (f32[8,128]{1,0:T(8,128)S(1)}, f32[8,128]{1,0:T(8,128)S(1)}, u32[]{:S(2)}, u32[]{:S(2)}) collective-permute-start(f32[8,128]{1,0:T(8,128)S(1)} %add.31), channel_id=1, source_target_pairs={{0,4},{1,5},{2,6},{3,7},{4,0},{5,1},{6,2},{7,3},{8,12},{9,13},{10,... | collective-permute-start | bytes 12296 | tf_op jit(solution)/shard_map/while/body/ppermute | solution.py:285
  54.4 1.9 %collective-permute-done.2 = f32[8,128]{1,0:T(8,128)S(1)} collective-permute-done((f32[8,128]{1,0:T(8,128)S(1)}, f32[8,128]{1,0:T(8,128)S(1)}, u32[]{:S(2)}, u32[]{:S(2)}) %collective-permute-start.2) | collective-permute-done | bytes 4128 | tf_op jit(solution)/shard_map/while/body/ppermute | solution.py:285
  56.3 1.5 %collective-permute-start.15 = (f32[8,128]{1,0:T(8,128)S(1)}, f32[8,128]{1,0:T(8,128)S(1)}, u32[]{:S(2)}, u32[]{:S(2)}) collective-permute-start(f32[8,128]{1,0:T(8,128)S(1)} %get-tuple-element.90), channel_id=1, source_target_pairs={{0,8},{8,0},{16,24},{24,16},{1,9},{9,1},{17,25},{25,17},{2,10},{10... | collective-permute-start | bytes 12296 | tf_op jit(solution)/shard_map/ppermute | solution.py:285
  57.8 2.1 %collective-permute-done.15 = f32[8,128]{1,0:T(8,128)S(1)} collective-permute-done((f32[8,128]{1,0:T(8,128)S(1)}, f32[8,128]{1,0:T(8,128)S(1)}, u32[]{:S(2)}, u32[]{:S(2)}) %collective-permute-start.15) | collective-permute-done | bytes 4128 | tf_op jit(solution)/shard_map/ppermute | solution.py:285
  59.9 1.5 %collective-permute-start.16 = (f32[8,128]{1,0:T(8,128)S(1)}, f32[8,128]{1,0:T(8,128)S(1)}, u32[]{:S(2)}, u32[]{:S(2)}) collective-permute-start(f32[8,128]{1,0:T(8,128)S(1)} %add.23), channel_id=1, source_target_pairs={{0,16},{8,24},{16,0},{24,8},{1,17},{9,25},{17,1},{25,9},{2,18},{10... | collective-permute-start | bytes 12296 | tf_op jit(solution)/shard_map/ppermute | solution.py:285
  61.5 1.6 %unpack.2 = (bf16[1,128,2560]{2,1,0:T(8,128)(2,1)}, bf16[1,128,2560]{2,1,0:T(8,128)(2,1)}, bf16[1,128,2560]{2,1,0:T(8,128)(2,1)}) custom-call(bf16[384,256]{1,0:T(8,128)(2,1)S(1)} %collective-permute-done.9.refs_0_, bf16[384,256]{1,0:T(8,128)(2,1)S(1)} %collective-permute-done.13.refs_1_, ...), custom_call_target="tpu_custom_call", output_to_operand_aliasing={{0}: (3, {}), {1}: (4, {}), {2}: (5, {})} | custom-call | tf_op jit(solution)/shard_map/unpack/pallas_call | solution.py:267
  64.1 1.2 %unpack.3 = (bf16[1,128,2560]{2,1,0:T(8,128)(2,1)}, bf16[1,128,2560]{2,1,0:T(8,128)(2,1)}, bf16[1,128,2560]{2,1,0:T(8,128)(2,1)}) custom-call(bf16[384,384]{1,0:T(8,128)(2,1)S(1)} %collective-permute-done.10.refs_0_, bf16[384,384]{1,0:T(8,128)(2,1)S(1)} %collective-permute-done.11.refs_1_, ...), custom_call_target="tpu_custom_call", output_to_operand_aliasing={{0}: (3, {}), {1}: (4, {}), {2}: (5, {})} | custom-call | tf_op jit(solution)/shard_map/unpack/pallas_call | solution.py:267
  (36 shorter events, 4.2 us)
Async XLA Ops:
  3.3 26.6 %copy-start = (bf16[1,128,2560]{2,1,0:T(8,128)(2,1)S(1)}, bf16[1,128,2560]{2,1,0:T(8,128)(2,1)}, u32[]{:S(2)}) copy-start(bf16[1,128,2560]{2,1,0:T(8,128)(2,1)} %refs_0_.7) | copy-start | bytes 1966084
  3.3 26.6 %copy-start.1 = (bf16[1,128,2560]{2,1,0:T(8,128)(2,1)S(1)}, bf16[1,128,2560]{2,1,0:T(8,128)(2,1)}, u32[]{:S(2)}) copy-start(bf16[1,128,2560]{2,1,0:T(8,128)(2,1)} %refs_1_.7) | copy-start | bytes 1966084
  3.3 26.6 %copy-start.2 = (bf16[1,128,2560]{2,1,0:T(8,128)(2,1)S(1)}, bf16[1,128,2560]{2,1,0:T(8,128)(2,1)}, u32[]{:S(2)}) copy-start(bf16[1,128,2560]{2,1,0:T(8,128)(2,1)} %refs_2_.7) | copy-start | bytes 1966084
  3.4 26.6 %copy-start.3 = (bf16[1,128,2560]{2,1,0:T(8,128)(2,1)S(1)}, bf16[1,128,2560]{2,1,0:T(8,128)(2,1)}, u32[]{:S(2)}) copy-start(bf16[1,128,2560]{2,1,0:T(8,128)(2,1)} %refs_3_.7) | copy-start | bytes 1966084
  3.4 11.2 %collective-permute-start.3 = (bf16[528,256]{1,0:T(8,128)(2,1)}, bf16[528,256]{1,0:T(8,128)(2,1)S(1)}, u32[]{:S(2)}, u32[]{:S(2)}) collective-permute-start(bf16[528,256]{1,0:T(8,128)(2,1)} %get-tuple-element.56), channel_id=1, source_target_pairs={{0,24},{8,16},{16,8},{24,0},{1,25},{9,17},{17,9},{25,1},{2,26},{10... | collective-permute-start | bytes 811016 | tf_op jit(solution)/shard_map/ppermute | solution.py:285
  10.3 24.8 %collective-permute-start.6 = (bf16[528,384]{1,0:T(8,128)(2,1)}, bf16[528,384]{1,0:T(8,128)(2,1)S(1)}, u32[]{:S(2)}, u32[]{:S(2)}) collective-permute-start(bf16[528,384]{1,0:T(8,128)(2,1)} %get-tuple-element.62), channel_id=1, source_target_pairs={{0,24},{8,16},{16,8},{24,0},{1,25},{9,17},{17,9},{25,1},{2,26},{10... | collective-permute-start | bytes 1216520 | tf_op jit(solution)/shard_map/ppermute | solution.py:285
  10.5 19.5 %collective-permute-start.4 = (bf16[528,256]{1,0:T(8,128)(2,1)}, bf16[528,256]{1,0:T(8,128)(2,1)S(1)}, u32[]{:S(2)}, u32[]{:S(2)}) collective-permute-start(bf16[528,256]{1,0:T(8,128)(2,1)} %get-tuple-element.57), channel_id=1, source_target_pairs={{0,8},{8,0},{16,24},{24,16},{1,9},{9,1},{17,25},{25,17},{2,10},{10... | collective-permute-start | bytes 811016 | tf_op jit(solution)/shard_map/ppermute | solution.py:285
  12.3 17.6 %collective-permute-start.5 = (bf16[528,256]{1,0:T(8,128)(2,1)}, bf16[528,256]{1,0:T(8,128)(2,1)S(1)}, u32[]{:S(2)}, u32[]{:S(2)}) collective-permute-start(bf16[528,256]{1,0:T(8,128)(2,1)} %get-tuple-element.58), channel_id=1, source_target_pairs={{0,16},{8,24},{16,0},{24,8},{1,17},{9,25},{17,1},{25,9},{2,18},{10... | collective-permute-start | bytes 811016 | tf_op jit(solution)/shard_map/ppermute | solution.py:285
  13.8 24.8 %collective-permute-start.7 = (bf16[528,384]{1,0:T(8,128)(2,1)}, bf16[528,384]{1,0:T(8,128)(2,1)S(1)}, u32[]{:S(2)}, u32[]{:S(2)}) collective-permute-start(bf16[528,384]{1,0:T(8,128)(2,1)} %get-tuple-element.65), channel_id=1, source_target_pairs={{0,8},{8,0},{16,24},{24,16},{1,9},{9,1},{17,25},{25,17},{2,10},{10... | collective-permute-start | bytes 1216520 | tf_op jit(solution)/shard_map/ppermute | solution.py:285
  14.6 15.4 %copy-start.4 = (s32[2,1]{0,1:T(1,128)S(1)}, s32[2,1]{0,1:T(1,128)}, u32[]{:S(2)}) copy-start(s32[2,1]{0,1:T(1,128)} %param.12) | copy-start | bytes 28
  14.6 15.4 %copy-start.5 = (f32[20]{0:T(128)S(1)}, f32[20]{0:T(128)}, u32[]{:S(2)}) copy-start(f32[20]{0:T(128)} %sink.3) | copy-start | bytes 244
  14.6 24.1 %collective-permute-start.8 = (bf16[528,384]{1,0:T(8,128)(2,1)}, bf16[528,384]{1,0:T(8,128)(2,1)S(1)}, u32[]{:S(2)}, u32[]{:S(2)}) collective-permute-start(bf16[528,384]{1,0:T(8,128)(2,1)} %get-tuple-element.66), channel_id=1, source_target_pairs={{0,16},{8,24},{16,0},{24,8},{1,17},{9,25},{17,1},{25,9},{2,18},{10... | collective-permute-start | bytes 1216520 | tf_op jit(solution)/shard_map/ppermute | solution.py:285
  33.6 12.8 %collective-permute-start.9 = (bf16[384,256]{1,0:T(8,128)(2,1)S(1)}, bf16[384,256]{1,0:T(8,128)(2,1)S(1)}, u32[]{:S(2)}, u32[]{:S(2)}) collective-permute-start(bf16[384,256]{1,0:T(8,128)(2,1)S(1)} %get-tuple-element.71), channel_id=1, source_target_pairs={{0,24},{8,16},{16,8},{24,0},{1,25},{9,17},{17,9},{25,1},{2,26},{10... | collective-permute-start | bytes 589832 | tf_op jit(solution)/shard_map/ppermute | solution.py:285
  35.1 11.8 %collective-permute-start.14 = (bf16[384,256]{1,0:T(8,128)(2,1)}, bf16[384,256]{1,0:T(8,128)(2,1)S(1)}, u32[]{:S(2)}, u32[]{:S(2)}) collective-permute-start(bf16[384,256]{1,0:T(8,128)(2,1)} %get-tuple-element.78), channel_id=1, source_target_pairs={{0,16},{8,24},{16,0},{24,8},{1,17},{9,25},{17,1},{25,9},{2,18},{10... | collective-permute-start | bytes 589832 | tf_op jit(solution)/shard_map/ppermute | solution.py:285
  36.6 24.8 %collective-permute-start.13 = (bf16[384,256]{1,0:T(8,128)(2,1)}, bf16[384,256]{1,0:T(8,128)(2,1)S(1)}, u32[]{:S(2)}, u32[]{:S(2)}) collective-permute-start(bf16[384,256]{1,0:T(8,128)(2,1)} %get-tuple-element.76), channel_id=1, source_target_pairs={{0,8},{8,0},{16,24},{24,16},{1,9},{9,1},{17,25},{25,17},{2,10},{10... | collective-permute-start | bytes 589832 | tf_op jit(solution)/shard_map/ppermute | solution.py:285
  43.3 20.7 %collective-permute-start.11 = (bf16[384,384]{1,0:T(8,128)(2,1)}, bf16[384,384]{1,0:T(8,128)(2,1)S(1)}, u32[]{:S(2)}, u32[]{:S(2)}) collective-permute-start(bf16[384,384]{1,0:T(8,128)(2,1)} %get-tuple-element.73), channel_id=1, source_target_pairs={{0,8},{8,0},{16,24},{24,16},{1,9},{9,1},{17,25},{25,17},{2,10},{10... | collective-permute-start | bytes 884744 | tf_op jit(solution)/shard_map/ppermute | solution.py:285
  44.9 19.2 %collective-permute-start.12 = (bf16[384,384]{1,0:T(8,128)(2,1)}, bf16[384,384]{1,0:T(8,128)(2,1)S(1)}, u32[]{:S(2)}, u32[]{:S(2)}) collective-permute-start(bf16[384,384]{1,0:T(8,128)(2,1)} %get-tuple-element.74), channel_id=1, source_target_pairs={{0,16},{8,24},{16,0},{24,8},{1,17},{9,25},{17,1},{25,9},{2,18},{10... | collective-permute-start | bytes 884744 | tf_op jit(solution)/shard_map/ppermute | solution.py:285
  46.4 17.6 %collective-permute-start.10 = (bf16[384,384]{1,0:T(8,128)(2,1)S(1)}, bf16[384,384]{1,0:T(8,128)(2,1)S(1)}, u32[]{:S(2)}, u32[]{:S(2)}) collective-permute-start(bf16[384,384]{1,0:T(8,128)(2,1)S(1)} %get-tuple-element.72), channel_id=1, source_target_pairs={{0,24},{8,16},{16,8},{24,0},{1,25},{9,17},{17,9},{25,1},{2,26},{10... | collective-permute-start | bytes 884744 | tf_op jit(solution)/shard_map/ppermute | solution.py:285
  47.0 1.2 %collective-permute-start = (f32[8,128]{1,0:T(8,128)S(1)}, f32[8,128]{1,0:T(8,128)S(1)}, u32[]{:S(2)}, u32[]{:S(2)}) collective-permute-start(f32[8,128]{1,0:T(8,128)S(1)} %get-tuple-element.122), channel_id=1, source_target_pairs={{0,1},{1,0},{2,3},{3,2},{4,5},{5,4},{6,7},{7,6},{8,9},{9,8},{10,11... | collective-permute-start | bytes 12296 | tf_op jit(solution)/shard_map/while/body/ppermute | solution.py:285
  48.2 3.6 %collective-permute-start.1 = (f32[8,128]{1,0:T(8,128)S(1)}, f32[8,128]{1,0:T(8,128)S(1)}, u32[]{:S(2)}, u32[]{:S(2)}) collective-permute-start(f32[8,128]{1,0:T(8,128)S(1)} %add.30), channel_id=1, source_target_pairs={{0,2},{1,3},{2,0},{3,1},{4,6},{5,7},{6,4},{7,5},{8,10},{9,11},{10,... | collective-permute-start | bytes 12296 | tf_op jit(solution)/shard_map/while/body/ppermute | solution.py:285
  51.8 4.5 %collective-permute-start.2 = (f32[8,128]{1,0:T(8,128)S(1)}, f32[8,128]{1,0:T(8,128)S(1)}, u32[]{:S(2)}, u32[]{:S(2)}) collective-permute-start(f32[8,128]{1,0:T(8,128)S(1)} %add.31), channel_id=1, source_target_pairs={{0,4},{1,5},{2,6},{3,7},{4,0},{5,1},{6,2},{7,3},{8,12},{9,13},{10,... | collective-permute-start | bytes 12296 | tf_op jit(solution)/shard_map/while/body/ppermute | solution.py:285
  56.3 3.6 %collective-permute-start.15 = (f32[8,128]{1,0:T(8,128)S(1)}, f32[8,128]{1,0:T(8,128)S(1)}, u32[]{:S(2)}, u32[]{:S(2)}) collective-permute-start(f32[8,128]{1,0:T(8,128)S(1)} %get-tuple-element.90), channel_id=1, source_target_pairs={{0,8},{8,0},{16,24},{24,16},{1,9},{9,1},{17,25},{25,17},{2,10},{10... | collective-permute-start | bytes 12296 | tf_op jit(solution)/shard_map/ppermute | solution.py:285
  59.9 3.6 %collective-permute-start.16 = (f32[8,128]{1,0:T(8,128)S(1)}, f32[8,128]{1,0:T(8,128)S(1)}, u32[]{:S(2)}, u32[]{:S(2)}) collective-permute-start(f32[8,128]{1,0:T(8,128)S(1)} %add.23), channel_id=1, source_target_pairs={{0,16},{8,24},{16,0},{24,8},{1,17},{9,25},{17,1},{25,9},{2,18},{10... | collective-permute-start | bytes 12296 | tf_op jit(solution)/shard_map/ppermute | solution.py:285

commit v4 on v3

--- a/solution.py
+++ b/solution.py
@@ -15,7 +15,7 @@
 ORDER = (3, 1, 2)
 
 
-def pack_kernel(offset, width, share, links, *refs):
+def pack_kernel(offset, width, share, with_flags, links, *refs):
     arrays, outs, (held, load_sems, store_sems) = refs[:4], refs[4:7], refs[7:]
     me = lax.axis_index("dp")
     loads, stores = [], []
@@ -33,9 +33,10 @@
         )
         for copy in loads[-1]:
             copy.start()
-    flags = live_flags(links, width)
-    for place in range(3):
-        held[place, 4 * BLOCK :, :] = flags
+    if with_flags:
+        flags = live_flags(links, width)
+        for place in range(3):
+            held[place, 4 * BLOCK :, :] = flags
     for place in range(3):
         for copy in loads[place]:
             copy.wait()
@@ -51,10 +52,10 @@
     return jnp.where(row < 8, live[0], live[1]).astype(jnp.bfloat16)
 
 
-def pack(links, arrays, offset, width, share):
-    rows = 4 * BLOCK + FLAG_ROWS
+def pack(links, arrays, offset, width, share, with_flags):
+    rows = 4 * BLOCK + FLAG_ROWS * with_flags
     return pl.pallas_call(
-        functools.partial(pack_kernel, offset, width, share),
+        functools.partial(pack_kernel, offset, width, share, with_flags),
         out_shape=[jax.ShapeDtypeStruct((rows, width), jnp.bfloat16)] * 3,
         in_specs=[pl.BlockSpec(memory_space=pltpu.SMEM)] + [pl.BlockSpec(memory_space=pl.ANY)] * 4,
         out_specs=[pl.BlockSpec(memory_space=pl.ANY)] * 3,
@@ -81,9 +82,9 @@
 
 
 def attend_kernel(first_head, heads, heads_dev, score_scale, num_previous, sink, links, sink_in, *refs):
-    arrays, ins, refs = refs[:4], refs[4:7], refs[7 + num_previous :]
+    arrays, ins, flag_ins, refs = refs[:4], refs[4:7], refs[7:10], refs[10 + num_previous :]
     outs, own_outs, sink_out = refs[:3], refs[3:6], refs[6]
-    held, grads, own_sems, in_sems, own_out_sems, out_sems = refs[7:]
+    held, flags_held, grads, own_sems, in_sems, flag_sems, own_out_sems, out_sems = refs[7:]
     me = lax.axis_index("dp")
     blocks = 4
 
@@ -104,7 +105,7 @@
         ]
         + [
             pltpu.make_async_copy(
-                ins[place].at[:, columns(head)],
+                ins[place].at[pl.ds(0, 4 * BLOCK), columns(head)],
                 held.at[me ^ mask, :, columns(head)],
                 in_sems.at[head, place],
             )
@@ -115,12 +116,24 @@
     for group in loads:
         for copy in group:
             copy.start()
-    held[me, 4 * BLOCK :, :] = live_flags(links, held.shape[2])
+    flag_loads = [
+        pltpu.make_async_copy(
+            flag_ins[place].at[pl.ds(4 * BLOCK, FLAG_ROWS), pl.ds(0, BLOCK)],
+            flags_held.at[me ^ mask],
+            flag_sems.at[place],
+        )
+        for place, mask in enumerate(ORDER)
+    ]
+    for copy in flag_loads:
+        copy.start()
+    flags_held[me] = live_flags(links, BLOCK)
     keys_iota = lax.broadcasted_iota(jnp.int32, (BLOCK, BLOCK), 0)
     queries_iota = lax.broadcasted_iota(jnp.int32, (BLOCK, BLOCK), 1)
     causal = keys_iota <= queries_iota
     lanes = lax.broadcasted_iota(jnp.int32, (8, BLOCK), 1)
     sink_sum = sink_in[...]
+    for copy in flag_loads:
+        copy.wait()
     stores = []
     for head in range(heads):
         for copy in loads[head]:
@@ -148,7 +161,7 @@
         weights, score_grads = {}, {}
         for block in range(blocks):
             sources = range(max(0, block - LEVELS), block + 1)
-            flags = held[block, 4 * BLOCK :, cols].astype(jnp.float32)
+            flags = flags_held[block].astype(jnp.float32)
             pieces = []
             for source in sources:
                 piece = scores[block, source] * (score_scale * LOG2_E)
@@ -209,9 +222,8 @@
         copy.wait()
 
 
-def attend(sink_logit, links, sink_sum, arrays, packed, previous, first_head, heads, heads_dev, score_scale):
-    rows, width = packed[0].shape
-    grad_rows = 3 * BLOCK
+def attend(sink_logit, links, sink_sum, arrays, packed, flags, previous, first_head, heads, heads_dev, score_scale):
+    rows, grad_rows, width = 4 * BLOCK, 3 * BLOCK, packed[0].shape[1]
     hbm = pl.BlockSpec(memory_space=pl.ANY)
     smem = pl.BlockSpec(memory_space=pltpu.SMEM)
     vmem = pl.BlockSpec(memory_space=pltpu.VMEM)
@@ -220,21 +232,23 @@
         out_shape=[jax.ShapeDtypeStruct((grad_rows, width), jnp.bfloat16)] * 3
         + [jax.ShapeDtypeStruct(arrays[0].shape, jnp.bfloat16)] * 3
         + [jax.ShapeDtypeStruct((8, BLOCK), jnp.float32)],
-        in_specs=[smem, smem, vmem] + [hbm] * (7 + len(previous)),
+        in_specs=[smem, smem, vmem] + [hbm] * (10 + len(previous)),
         out_specs=[hbm] * 6 + [vmem],
         scratch_shapes=[
             pltpu.VMEM((4, rows, width), jnp.bfloat16),
+            pltpu.VMEM((4, FLAG_ROWS, BLOCK), jnp.bfloat16),
             pltpu.VMEM((4, grad_rows, width), jnp.bfloat16),
             pltpu.SemaphoreType.DMA((heads, 4)),
             pltpu.SemaphoreType.DMA((heads, 3)),
+            pltpu.SemaphoreType.DMA((3,)),
             pltpu.SemaphoreType.DMA((heads, 3)),
             pltpu.SemaphoreType.DMA((heads, 3)),
         ],
-        input_output_aliases={10 + num: 3 + num for num in range(len(previous))},
+        input_output_aliases={13 + num: 3 + num for num in range(len(previous))},
         compiler_params=pltpu.CompilerParams(vmem_limit_bytes=8 * 2**20),
         cost_estimate=pl.CostEstimate(flops=0, bytes_accessed=0, transcendentals=0),
         name="attend",
-    )(sink_logit, links, sink_sum, *arrays, *packed, *previous)
+    )(sink_logit, links, sink_sum, *arrays, *packed, *flags, *previous)
 
 
 def unpack_kernel(offset, width, share, *refs):
@@ -289,11 +303,9 @@
     return lax.optimization_barrier((value, other))
 
 
-def butterfly(value, axis):
-    mask = 1
-    while mask < lax.axis_size(axis):
+def add_swapped(value, axis, masks):
+    for mask in masks:
         value = value + swap(value, axis, mask)
-        mask *= 2
     return value
 
 
@@ -307,17 +319,18 @@
     links = block_links.reshape(LEVELS)
     received, first = [], 0
     for count in chunks:
-        packed = pack(links, arrays, first * head_size, count * head_size, share)
+        packed = pack(links, arrays, first * head_size, count * head_size, share, first == 0)
         moved = [swap(part, "dp", mask) for part, mask in zip(packed, ORDER)]
         received.append((first, count, moved))
         first += count
     results, outputs, sink_sum = [], [], jnp.zeros((8, BLOCK), jnp.float32)
     for num, (first, count, packed) in enumerate(received):
         *grads, sink_sum = attend(
-            sink_logit, links, sink_sum, arrays, packed, outputs, first, count, heads_dev, score_scale
+            sink_logit, links, sink_sum, arrays, packed, received[0][2], outputs, first, count, heads_dev, score_scale
         )
-        grads, outputs = grads[:3], grads[3:]
+        grads, outputs = grads[:3], list(grads[3:])
         if num:
+            sink_sum = sink_sum + swap(sink_sum, "ctx", 2)
             grads[0], results[0][1][0] = after(grads[0], results[0][1][0])
         else:
             for place in (1, 2):
@@ -325,10 +338,12 @@
         results.append((first, [swap(grad, "dp", mask) for grad, mask in zip(grads, ORDER)]))
     sink_sum, results[0][1][2] = after(sink_sum, results[0][1][2])
     once = jnp.minimum(links[0] + 2, 1)
-    sink_sum = lax.fori_loop(0, once, lambda _, held: butterfly(held, "ctx"), sink_sum)
-    sink_sum = butterfly(sink_sum, "dp")
-    for first, parts in results:
-        outputs = unpack(parts, outputs, first * head_size, share)
+    sink_sum = lax.fori_loop(0, once, lambda _, held: add_swapped(held, "ctx", (1, 4)), sink_sum)
+    sink_sum = add_swapped(sink_sum, "dp", (1,))
+    outputs = list(unpack(results[0][1], outputs, results[0][0] * head_size, share))
+    sink_sum, outputs[0] = after(sink_sum, outputs[0])
+    sink_sum = add_swapped(sink_sum, "dp", (2,))
+    outputs = unpack(results[1][1], outputs, results[1][0] * head_size, share)
     return (*outputs, sink_sum[0, :heads])
 
 
@@ -460,7 +475,7 @@
         and queries.shape[:2] == (1, BLOCK)
         and queries.shape[2] == heads * BLOCK
         and heads == 4 * sum(CHUNKS)
-        and groups & (groups - 1) == 0
+        and groups == 8
     )
     plan = functools.partial(head_shares_body, CHUNKS) if fits else keys_travel_body
     return plan(queries, key_states, values, out_grad, block_links, sink_logit)

time: 65.5 us -> 64.9 us (level)
  waiting for transfers between devices: 22.3 us -> 21.4 us
    ppermute x17, waiting for transfers between devices: 22.3 us -> 21.4 us  [swap(): lax.ppermute(value, axis, [(i, i ^ mask) for i in range(lax.axis_size(axi...]
  transfers between devices with their start and end apart: 17 -> 17, of which waited for: 8 -> 7; matrix products, arithmetic and copies ran while one was open for 1% -> 1% of each run, Pallas kernels for 20% -> 20%
where the time goes in v4:
time: 64.9 us; the launch traced here: 64.6 us
  starting transfers between devices  25.1 us (39%)
  waiting for transfers between devices  21.4 us (33%)
  Pallas kernels  16.8 us (26%)
  between operations  0.82 us (1%)
    ppermute x17, starting transfers between devices, swap(): lax.ppermute(value, axis, [(i, i ^ mask) for i in range(lax.axis_size(axi...  25.1 us
    ppermute x17, waiting for transfers between devices, swap(): lax.ppermute(value, axis, [(i, i ^ mask) for i in range(lax.axis_size(axi...  21.4 us
    pallas_call x2, Pallas kernels, attend(): pl.pallas_call(functools.partial(attend_kernel, first_head, heads, heads_...  8.33 us
    pallas_call x2, Pallas kernels, pack(): pl.pallas_call(functools.partial(pack_kernel, offset, width, share, with_...  5.59 us
    pallas_call x2, Pallas kernels, unpack(): pl.pallas_call(functools.partial(unpack_kernel, offset, width, share), ou...  2.84 us
  transfers between devices with their start and end apart: 17, of which 7 were waited for; matrix products, arithmetic and copies ran while one was open for 1% of the time, Pallas kernels for 20%

profile of v4, /device:TPU:0, one launch (start us, length us, event | category | flops | bytes accessed | tf_op | source)
XLA Modules:
  0.0 64.6 jit_solution(3233799897433313142)
XLA Ops:
  0.6 2.7 %pack.2 = (bf16[528,256]{1,0:T(8,128)(2,1)}, bf16[528,256]{1,0:T(8,128)(2,1)}, bf16[528,256]{1,0:T(8,128)(2,1)}) custom-call(s32[2]{0:T(128)} %bitcast.5, bf16[1,128,2560]{2,1,0:T(8,128)(2,1)} %refs_0_.7, bf16[1,128,2560]{2,1,0:T(8,128)(2,1)} %refs_1_.7, bf16[1,128,2560]{2,1,0:T(8,128)(2,1)} %refs_2_.7, bf16[1,128,2560]{2,1,0:T(8,128)(2,1)} %refs_3_.7), custom_call_target="tpu_custom_call" | custom-call | bytes 1622016 | tf_op jit(solution)/shard_map/pack/pallas_call | solution.py:57
  3.4 4.0 %collective-permute-start.2 = (bf16[528,256]{1,0:T(8,128)(2,1)}, bf16[528,256]{1,0:T(8,128)(2,1)S(1)}, u32[]{:S(2)}, u32[]{:S(2)}) collective-permute-start(bf16[528,256]{1,0:T(8,128)(2,1)} %get-tuple-element.58), channel_id=1, source_target_pairs={{0,24},{8,16},{16,8},{24,0},{1,25},{9,17},{17,9},{25,1},{2,26},{10... | collective-permute-start | bytes 811016 | tf_op jit(solution)/shard_map/ppermute | solution.py:299
  7.3 2.9 %pack.3 = (bf16[512,384]{1,0:T(8,128)(2,1)}, bf16[512,384]{1,0:T(8,128)(2,1)}, bf16[512,384]{1,0:T(8,128)(2,1)}) custom-call(s32[2]{0:T(128)} %bitcast.6, bf16[1,128,2560]{2,1,0:T(8,128)(2,1)} %refs_0_.7, bf16[1,128,2560]{2,1,0:T(8,128)(2,1)} %refs_1_.7, bf16[1,128,2560]{2,1,0:T(8,128)(2,1)} %refs_2_.7, bf16[1,128,2560]{2,1,0:T(8,128)(2,1)} %refs_3_.7), custom_call_target="tpu_custom_call" | custom-call | bytes 2359296 | tf_op jit(solution)/shard_map/pack/pallas_call | solution.py:57
  10.5 1.8 %collective-permute-start.3 = (bf16[528,256]{1,0:T(8,128)(2,1)}, bf16[528,256]{1,0:T(8,128)(2,1)S(1)}, u32[]{:S(2)}, u32[]{:S(2)}) collective-permute-start(bf16[528,256]{1,0:T(8,128)(2,1)} %get-tuple-element.59), channel_id=1, source_target_pairs={{0,8},{8,0},{16,24},{24,16},{1,9},{9,1},{17,25},{25,17},{2,10},{10... | collective-permute-start | bytes 811016 | tf_op jit(solution)/shard_map/ppermute | solution.py:299
  12.3 1.5 %collective-permute-start.4 = (bf16[528,256]{1,0:T(8,128)(2,1)}, bf16[528,256]{1,0:T(8,128)(2,1)S(1)}, u32[]{:S(2)}, u32[]{:S(2)}) collective-permute-start(bf16[528,256]{1,0:T(8,128)(2,1)} %get-tuple-element.60), channel_id=1, source_target_pairs={{0,16},{8,24},{16,0},{24,8},{1,17},{9,25},{17,1},{25,9},{2,18},{10... | collective-permute-start | bytes 811016 | tf_op jit(solution)/shard_map/ppermute | solution.py:299
  14.6 2.4 %collective-permute-start.7 = (bf16[512,384]{1,0:T(8,128)(2,1)}, bf16[512,384]{1,0:T(8,128)(2,1)S(1)}, u32[]{:S(2)}, u32[]{:S(2)}) collective-permute-start(bf16[512,384]{1,0:T(8,128)(2,1)} %get-tuple-element.68), channel_id=1, source_target_pairs={{0,16},{8,24},{16,0},{24,8},{1,17},{9,25},{17,1},{25,9},{2,18},{10... | collective-permute-start | bytes 1179656 | tf_op jit(solution)/shard_map/ppermute | solution.py:299
  17.0 12.7 %collective-permute-done.3.refs_5_.refs_8_ = bf16[528,256]{1,0:T(8,128)(2,1)S(1)} collective-permute-done((bf16[528,256]{1,0:T(8,128)(2,1)}, bf16[528,256]{1,0:T(8,128)(2,1)S(1)}, u32[]{:S(2)}, u32[]{:S(2)}) %collective-permute-start.3) | collective-permute-done | bytes 270368 | tf_op jit(solution)/shard_map/ppermute | solution.py:299
  29.7 3.6 %attend.2 = (bf16[384,256]{1,0:T(8,128)(2,1)S(1)}, bf16[384,256]{1,0:T(8,128)(2,1)}, bf16[384,256]{1,0:T(8,128)(2,1)}, bf16[1,128,2560]{2,1,0:T(8,128)(2,1)}, bf...) custom-call(f32[20]{0:T(128)S(1)} %copy-done.5, s32[2]{0:T(128)S(1)} %bitcast.7, ...), custom_call_target="tpu_custom_call" | custom-call | tf_op jit(solution)/shard_map/attend/pallas_call | solution.py:230
  33.4 1.5 %collective-permute-start.8 = (bf16[384,256]{1,0:T(8,128)(2,1)S(1)}, bf16[384,256]{1,0:T(8,128)(2,1)S(1)}, u32[]{:S(2)}, u32[]{:S(2)}) collective-permute-start(bf16[384,256]{1,0:T(8,128)(2,1)S(1)} %get-tuple-element.73), channel_id=1, source_target_pairs={{0,24},{8,16},{16,8},{24,0},{1,25},{9,17},{17,9},{25,1},{2,26},{10... | collective-permute-start | bytes 589832 | tf_op jit(solution)/shard_map/ppermute | solution.py:299
  34.9 1.5 %collective-permute-start.13 = (bf16[384,256]{1,0:T(8,128)(2,1)}, bf16[384,256]{1,0:T(8,128)(2,1)S(1)}, u32[]{:S(2)}, u32[]{:S(2)}) collective-permute-start(bf16[384,256]{1,0:T(8,128)(2,1)} %get-tuple-element.78), channel_id=1, source_target_pairs={{0,16},{8,24},{16,0},{24,8},{1,17},{9,25},{17,1},{25,9},{2,18},{10... | collective-permute-start | bytes 589832 | tf_op jit(solution)/shard_map/ppermute | solution.py:299
  36.9 1.2 %collective-permute-done.6.refs_5_ = bf16[512,384]{1,0:T(8,128)(2,1)S(1)} collective-permute-done((bf16[512,384]{1,0:T(8,128)(2,1)}, bf16[512,384]{1,0:T(8,128)(2,1)S(1)}, u32[]{:S(2)}, u32[]{:S(2)}) %collective-permute-start.6) | collective-permute-done | bytes 393248 | tf_op jit(solution)/shard_map/ppermute | solution.py:299
  38.1 4.7 %attend.3 = (bf16[384,384]{1,0:T(8,128)(2,1)}, bf16[384,384]{1,0:T(8,128)(2,1)}, bf16[384,384]{1,0:T(8,128)(2,1)}, bf16[1,128,2560]{2,1,0:T(8,128)(2,1)}, bf16[1...) custom-call(f32[20]{0:T(128)S(1)} %copy-done.5, ...), custom_call_target="tpu_custom_call", output_to_operand_aliasing={{3}: (13, {}), {4}: (14, {}), {5}: (15, {})} | custom-call | tf_op jit(solution)/shard_map/attend/pallas_call | solution.py:230
  42.8 1.6 %collective-permute-start.12 = (f32[8,128]{1,0:T(8,128)S(1)}, f32[8,128]{1,0:T(8,128)S(1)}, u32[]{:S(2)}, u32[]{:S(2)}) collective-permute-start(f32[8,128]{1,0:T(8,128)S(1)} %get-tuple-element.77), channel_id=1, source_target_pairs={{0,2},{1,3},{2,0},{3,1},{4,6},{5,7},{6,4},{7,5},{8,10},{9,11},{10,... | collective-permute-start | bytes 12296 | tf_op jit(solution)/shard_map/ppermute | solution.py:299
  44.5 1.5 %collective-permute-start.10 = (bf16[384,384]{1,0:T(8,128)(2,1)}, bf16[384,384]{1,0:T(8,128)(2,1)S(1)}, u32[]{:S(2)}, u32[]{:S(2)}) collective-permute-start(bf16[384,384]{1,0:T(8,128)(2,1)} %get-tuple-element.75), channel_id=1, source_target_pairs={{0,8},{8,0},{16,24},{24,16},{1,9},{9,1},{17,25},{25,17},{2,10},{10... | collective-permute-start | bytes 884744 | tf_op jit(solution)/shard_map/ppermute | solution.py:299
  46.0 1.5 %collective-permute-start.11 = (bf16[384,384]{1,0:T(8,128)(2,1)}, bf16[384,384]{1,0:T(8,128)(2,1)S(1)}, u32[]{:S(2)}, u32[]{:S(2)}) collective-permute-start(bf16[384,384]{1,0:T(8,128)(2,1)} %get-tuple-element.76), channel_id=1, source_target_pairs={{0,16},{8,24},{16,0},{24,8},{1,17},{9,25},{17,1},{25,9},{2,18},{10... | collective-permute-start | bytes 884744 | tf_op jit(solution)/shard_map/ppermute | solution.py:299
  47.5 1.5 %collective-permute-start.9 = (bf16[384,384]{1,0:T(8,128)(2,1)}, bf16[384,384]{1,0:T(8,128)(2,1)S(1)}, u32[]{:S(2)}, u32[]{:S(2)}) collective-permute-start(bf16[384,384]{1,0:T(8,128)(2,1)} %get-tuple-element.74), channel_id=1, source_target_pairs={{0,24},{8,16},{16,8},{24,0},{1,25},{9,17},{17,9},{25,1},{2,26},{10... | collective-permute-start | bytes 884744 | tf_op jit(solution)/shard_map/ppermute | solution.py:299
  49.0 5.8 %while.10 = (s32[]{:T(128)}, f32[8,128]{1,0:T(8,128)S(1)}, s32[]{:T(128)}, s32[]{:T(128)}) while((s32[]{:T(128)}, f32[8,128]{1,0:T(8,128)S(1)}, s32[]{:T(128)}, s32[]{:T(128)}) %tuple.32), condition=%wide.region_1.0_spmd, body=%wide.region_0.0_spmd.sunk | while | flops 2050 | bytes 57477 | solution.py:341
  50.3 2.6 %collective-permute-start.1 = (f32[8,128]{1,0:T(8,128)S(1)}, f32[8,128]{1,0:T(8,128)S(1)}, u32[]{:S(2)}, u32[]{:S(2)}) collective-permute-start(f32[8,128]{1,0:T(8,128)S(1)} %add.30), channel_id=1, source_target_pairs={{0,4},{1,5},{2,6},{3,7},{4,0},{5,1},{6,2},{7,3},{8,12},{9,13},{10,... | collective-permute-start | bytes 12296 | tf_op jit(solution)/shard_map/while/body/ppermute | solution.py:299
  52.9 1.9 %collective-permute-done.1 = f32[8,128]{1,0:T(8,128)S(1)} collective-permute-done((f32[8,128]{1,0:T(8,128)S(1)}, f32[8,128]{1,0:T(8,128)S(1)}, u32[]{:S(2)}, u32[]{:S(2)}) %collective-permute-start.1) | collective-permute-done | bytes 4128 | tf_op jit(solution)/shard_map/while/body/ppermute | solution.py:299
  55.3 1.6 %unpack.2 = (bf16[1,128,2560]{2,1,0:T(8,128)(2,1)}, bf16[1,128,2560]{2,1,0:T(8,128)(2,1)}, bf16[1,128,2560]{2,1,0:T(8,128)(2,1)}) custom-call(bf16[384,256]{1,0:T(8,128)(2,1)S(1)} %collective-permute-done.8.refs_0_, bf16[384,256]{1,0:T(8,128)(2,1)S(1)} %collective-permute-done.15.refs_1_, ...), custom_call_target="tpu_custom_call", output_to_operand_aliasing={{0}: (3, {}), {1}: (4, {}), {2}: (5, {})} | custom-call | tf_op jit(solution)/shard_map/unpack/pallas_call | solution.py:281
  57.0 2.3 %collective-permute-done.14 = f32[8,128]{1,0:T(8,128)S(1)} collective-permute-done((f32[8,128]{1,0:T(8,128)S(1)}, f32[8,128]{1,0:T(8,128)S(1)}, u32[]{:S(2)}, u32[]{:S(2)}) %collective-permute-start.14) | collective-permute-done | bytes 4128 | tf_op jit(solution)/shard_map/ppermute | solution.py:299
  59.3 1.8 %collective-permute-start.16 = (f32[8,128]{1,0:T(8,128)S(1)}, f32[8,128]{1,0:T(8,128)S(1)}, u32[]{:S(2)}, u32[]{:S(2)}) collective-permute-start(f32[8,128]{1,0:T(8,128)S(1)} %add.24), channel_id=1, source_target_pairs={{0,16},{8,24},{16,0},{24,8},{1,17},{9,25},{17,1},{25,9},{2,18},{10... | collective-permute-start | bytes 12296 | tf_op jit(solution)/shard_map/ppermute | solution.py:299
  61.1 1.8 %collective-permute-done.16 = f32[8,128]{1,0:T(8,128)S(1)} collective-permute-done((f32[8,128]{1,0:T(8,128)S(1)}, f32[8,128]{1,0:T(8,128)S(1)}, u32[]{:S(2)}, u32[]{:S(2)}) %collective-permute-start.16) | collective-permute-done | bytes 4128 | tf_op jit(solution)/shard_map/ppermute | solution.py:299
  63.4 1.2 %unpack.3 = (bf16[1,128,2560]{2,1,0:T(8,128)(2,1)}, bf16[1,128,2560]{2,1,0:T(8,128)(2,1)}, bf16[1,128,2560]{2,1,0:T(8,128)(2,1)}) custom-call(bf16[384,384]{1,0:T(8,128)(2,1)S(1)} %collective-permute-done.9.refs_0_, bf16[384,384]{1,0:T(8,128)(2,1)S(1)} %collective-permute-done.10.refs_1_, ...), custom_call_target="tpu_custom_call", output_to_operand_aliasing={{0}: (3, {}), {1}: (4, {}), {2}: (5, {})} | custom-call | tf_op jit(solution)/shard_map/unpack/pallas_call | solution.py:281
  (36 shorter events, 3.9 us)
Async XLA Ops:
  3.3 26.4 %copy-start = (bf16[1,128,2560]{2,1,0:T(8,128)(2,1)S(1)}, bf16[1,128,2560]{2,1,0:T(8,128)(2,1)}, u32[]{:S(2)}) copy-start(bf16[1,128,2560]{2,1,0:T(8,128)(2,1)} %refs_0_.7) | copy-start | bytes 1966084
  3.3 26.4 %copy-start.1 = (bf16[1,128,2560]{2,1,0:T(8,128)(2,1)S(1)}, bf16[1,128,2560]{2,1,0:T(8,128)(2,1)}, u32[]{:S(2)}) copy-start(bf16[1,128,2560]{2,1,0:T(8,128)(2,1)} %refs_1_.7) | copy-start | bytes 1966084
  3.3 26.4 %copy-start.2 = (bf16[1,128,2560]{2,1,0:T(8,128)(2,1)S(1)}, bf16[1,128,2560]{2,1,0:T(8,128)(2,1)}, u32[]{:S(2)}) copy-start(bf16[1,128,2560]{2,1,0:T(8,128)(2,1)} %refs_2_.7) | copy-start | bytes 1966084
  3.4 26.4 %copy-start.3 = (bf16[1,128,2560]{2,1,0:T(8,128)(2,1)S(1)}, bf16[1,128,2560]{2,1,0:T(8,128)(2,1)}, u32[]{:S(2)}) copy-start(bf16[1,128,2560]{2,1,0:T(8,128)(2,1)} %refs_3_.7) | copy-start | bytes 1966084
  3.4 11.2 %collective-permute-start.2 = (bf16[528,256]{1,0:T(8,128)(2,1)}, bf16[528,256]{1,0:T(8,128)(2,1)S(1)}, u32[]{:S(2)}, u32[]{:S(2)}) collective-permute-start(bf16[528,256]{1,0:T(8,128)(2,1)} %get-tuple-element.58), channel_id=1, source_target_pairs={{0,24},{8,16},{16,8},{24,0},{1,25},{9,17},{17,9},{25,1},{2,26},{10... | collective-permute-start | bytes 811016 | tf_op jit(solution)/shard_map/ppermute | solution.py:299
  10.2 24.6 %collective-permute-start.5 = (bf16[512,384]{1,0:T(8,128)(2,1)}, bf16[512,384]{1,0:T(8,128)(2,1)S(1)}, u32[]{:S(2)}, u32[]{:S(2)}) collective-permute-start(bf16[512,384]{1,0:T(8,128)(2,1)} %get-tuple-element.64), channel_id=1, source_target_pairs={{0,24},{8,16},{16,8},{24,0},{1,25},{9,17},{17,9},{25,1},{2,26},{10... | collective-permute-start | bytes 1179656 | tf_op jit(solution)/shard_map/ppermute | solution.py:299
  10.5 19.2 %collective-permute-start.3 = (bf16[528,256]{1,0:T(8,128)(2,1)}, bf16[528,256]{1,0:T(8,128)(2,1)S(1)}, u32[]{:S(2)}, u32[]{:S(2)}) collective-permute-start(bf16[528,256]{1,0:T(8,128)(2,1)} %get-tuple-element.59), channel_id=1, source_target_pairs={{0,8},{8,0},{16,24},{24,16},{1,9},{9,1},{17,25},{25,17},{2,10},{10... | collective-permute-start | bytes 811016 | tf_op jit(solution)/shard_map/ppermute | solution.py:299
  12.3 17.4 %collective-permute-start.4 = (bf16[528,256]{1,0:T(8,128)(2,1)}, bf16[528,256]{1,0:T(8,128)(2,1)S(1)}, u32[]{:S(2)}, u32[]{:S(2)}) collective-permute-start(bf16[528,256]{1,0:T(8,128)(2,1)} %get-tuple-element.60), channel_id=1, source_target_pairs={{0,16},{8,24},{16,0},{24,8},{1,17},{9,25},{17,1},{25,9},{2,18},{10... | collective-permute-start | bytes 811016 | tf_op jit(solution)/shard_map/ppermute | solution.py:299
  13.8 24.3 %collective-permute-start.6 = (bf16[512,384]{1,0:T(8,128)(2,1)}, bf16[512,384]{1,0:T(8,128)(2,1)S(1)}, u32[]{:S(2)}, u32[]{:S(2)}) collective-permute-start(bf16[512,384]{1,0:T(8,128)(2,1)} %get-tuple-element.67), channel_id=1, source_target_pairs={{0,8},{8,0},{16,24},{24,16},{1,9},{9,1},{17,25},{25,17},{2,10},{10... | collective-permute-start | bytes 1179656 | tf_op jit(solution)/shard_map/ppermute | solution.py:299
  14.6 15.1 %copy-start.4 = (s32[2,1]{0,1:T(1,128)S(1)}, s32[2,1]{0,1:T(1,128)}, u32[]{:S(2)}) copy-start(s32[2,1]{0,1:T(1,128)} %param.12) | copy-start | bytes 28
  14.6 15.2 %copy-start.5 = (f32[20]{0:T(128)S(1)}, f32[20]{0:T(128)}, u32[]{:S(2)}) copy-start(f32[20]{0:T(128)} %sink.3) | copy-start | bytes 244
  14.6 23.5 %collective-permute-start.7 = (bf16[512,384]{1,0:T(8,128)(2,1)}, bf16[512,384]{1,0:T(8,128)(2,1)S(1)}, u32[]{:S(2)}, u32[]{:S(2)}) collective-permute-start(bf16[512,384]{1,0:T(8,128)(2,1)} %get-tuple-element.68), channel_id=1, source_target_pairs={{0,16},{8,24},{16,0},{24,8},{1,17},{9,25},{17,1},{25,9},{2,18},{10... | collective-permute-start | bytes 1179656 | tf_op jit(solution)/shard_map/ppermute | solution.py:299
  33.4 12.6 %collective-permute-start.8 = (bf16[384,256]{1,0:T(8,128)(2,1)S(1)}, bf16[384,256]{1,0:T(8,128)(2,1)S(1)}, u32[]{:S(2)}, u32[]{:S(2)}) collective-permute-start(bf16[384,256]{1,0:T(8,128)(2,1)S(1)} %get-tuple-element.73), channel_id=1, source_target_pairs={{0,24},{8,16},{16,8},{24,0},{1,25},{9,17},{17,9},{25,1},{2,26},{10... | collective-permute-start | bytes 589832 | tf_op jit(solution)/shard_map/ppermute | solution.py:299
  34.9 14.1 %collective-permute-start.13 = (bf16[384,256]{1,0:T(8,128)(2,1)}, bf16[384,256]{1,0:T(8,128)(2,1)S(1)}, u32[]{:S(2)}, u32[]{:S(2)}) collective-permute-start(bf16[384,256]{1,0:T(8,128)(2,1)} %get-tuple-element.78), channel_id=1, source_target_pairs={{0,16},{8,24},{16,0},{24,8},{1,17},{9,25},{17,1},{25,9},{2,18},{10... | collective-permute-start | bytes 589832 | tf_op jit(solution)/shard_map/ppermute | solution.py:299
  36.4 18.9 %collective-permute-start.15 = (bf16[384,256]{1,0:T(8,128)(2,1)}, bf16[384,256]{1,0:T(8,128)(2,1)S(1)}, u32[]{:S(2)}, u32[]{:S(2)}) collective-permute-start(bf16[384,256]{1,0:T(8,128)(2,1)} %get-tuple-element.82), channel_id=1, source_target_pairs={{0,8},{8,0},{16,24},{24,16},{1,9},{9,1},{17,25},{25,17},{2,10},{10... | collective-permute-start | bytes 589832 | tf_op jit(solution)/shard_map/ppermute | solution.py:299
  42.8 4.7 %collective-permute-start.12 = (f32[8,128]{1,0:T(8,128)S(1)}, f32[8,128]{1,0:T(8,128)S(1)}, u32[]{:S(2)}, u32[]{:S(2)}) collective-permute-start(f32[8,128]{1,0:T(8,128)S(1)} %get-tuple-element.77), channel_id=1, source_target_pairs={{0,2},{1,3},{2,0},{3,1},{4,6},{5,7},{6,4},{7,5},{8,10},{9,11},{10,... | collective-permute-start | bytes 12296 | tf_op jit(solution)/shard_map/ppermute | solution.py:299
  44.5 19.0 %collective-permute-start.10 = (bf16[384,384]{1,0:T(8,128)(2,1)}, bf16[384,384]{1,0:T(8,128)(2,1)S(1)}, u32[]{:S(2)}, u32[]{:S(2)}) collective-permute-start(bf16[384,384]{1,0:T(8,128)(2,1)} %get-tuple-element.75), channel_id=1, source_target_pairs={{0,8},{8,0},{16,24},{24,16},{1,9},{9,1},{17,25},{25,17},{2,10},{10... | collective-permute-start | bytes 884744 | tf_op jit(solution)/shard_map/ppermute | solution.py:299
  46.0 17.5 %collective-permute-start.11 = (bf16[384,384]{1,0:T(8,128)(2,1)}, bf16[384,384]{1,0:T(8,128)(2,1)S(1)}, u32[]{:S(2)}, u32[]{:S(2)}) collective-permute-start(bf16[384,384]{1,0:T(8,128)(2,1)} %get-tuple-element.76), channel_id=1, source_target_pairs={{0,16},{8,24},{16,0},{24,8},{1,17},{9,25},{17,1},{25,9},{2,18},{10... | collective-permute-start | bytes 884744 | tf_op jit(solution)/shard_map/ppermute | solution.py:299
  47.5 15.9 %collective-permute-start.9 = (bf16[384,384]{1,0:T(8,128)(2,1)}, bf16[384,384]{1,0:T(8,128)(2,1)S(1)}, u32[]{:S(2)}, u32[]{:S(2)}) collective-permute-start(bf16[384,384]{1,0:T(8,128)(2,1)} %get-tuple-element.74), channel_id=1, source_target_pairs={{0,24},{8,16},{16,8},{24,0},{1,25},{9,17},{17,9},{25,1},{2,26},{10... | collective-permute-start | bytes 884744 | tf_op jit(solution)/shard_map/ppermute | solution.py:299
  49.0 1.2 %collective-permute-start = (f32[8,128]{1,0:T(8,128)S(1)}, f32[8,128]{1,0:T(8,128)S(1)}, u32[]{:S(2)}, u32[]{:S(2)}) collective-permute-start(f32[8,128]{1,0:T(8,128)S(1)} %get-tuple-element.126), channel_id=1, source_target_pairs={{0,1},{1,0},{2,3},{3,2},{4,5},{5,4},{6,7},{7,6},{8,9},{9,8},{10,11... | collective-permute-start | bytes 12296 | tf_op jit(solution)/shard_map/while/body/ppermute | solution.py:299
  50.3 4.5 %collective-permute-start.1 = (f32[8,128]{1,0:T(8,128)S(1)}, f32[8,128]{1,0:T(8,128)S(1)}, u32[]{:S(2)}, u32[]{:S(2)}) collective-permute-start(f32[8,128]{1,0:T(8,128)S(1)} %add.30), channel_id=1, source_target_pairs={{0,4},{1,5},{2,6},{3,7},{4,0},{5,1},{6,2},{7,3},{8,12},{9,13},{10,... | collective-permute-start | bytes 12296 | tf_op jit(solution)/shard_map/while/body/ppermute | solution.py:299
  54.8 4.5 %collective-permute-start.14 = (f32[8,128]{1,0:T(8,128)S(1)}, f32[8,128]{1,0:T(8,128)S(1)}, u32[]{:S(2)}, u32[]{:S(2)}) collective-permute-start(f32[8,128]{1,0:T(8,128)S(1)} %get-tuple-element.80), channel_id=1, source_target_pairs={{0,8},{8,0},{16,24},{24,16},{1,9},{9,1},{17,25},{25,17},{2,10},{10... | collective-permute-start | bytes 12296 | tf_op jit(solution)/shard_map/ppermute | solution.py:299
  59.3 3.6 %collective-permute-start.16 = (f32[8,128]{1,0:T(8,128)S(1)}, f32[8,128]{1,0:T(8,128)S(1)}, u32[]{:S(2)}, u32[]{:S(2)}) collective-permute-start(f32[8,128]{1,0:T(8,128)S(1)} %add.24), channel_id=1, source_target_pairs={{0,16},{8,24},{16,0},{24,8},{1,17},{9,25},{17,1},{25,9},{2,18},{10... | collective-permute-start | bytes 12296 | tf_op jit(solution)/shard_map/ppermute | solution.py:299

commit v5 on v4

--- a/solution.py
+++ b/solution.py
@@ -130,7 +130,7 @@
     keys_iota = lax.broadcasted_iota(jnp.int32, (BLOCK, BLOCK), 0)
     queries_iota = lax.broadcasted_iota(jnp.int32, (BLOCK, BLOCK), 1)
     causal = keys_iota <= queries_iota
-    lanes = lax.broadcasted_iota(jnp.int32, (8, BLOCK), 1)
+    lanes = lax.broadcasted_iota(jnp.int32, (1, BLOCK), 1)
     sink_sum = sink_in[...]
     for copy in flag_loads:
         copy.wait()
@@ -231,7 +231,7 @@
         functools.partial(attend_kernel, first_head, heads, heads_dev, score_scale, len(previous)),
         out_shape=[jax.ShapeDtypeStruct((grad_rows, width), jnp.bfloat16)] * 3
         + [jax.ShapeDtypeStruct(arrays[0].shape, jnp.bfloat16)] * 3
-        + [jax.ShapeDtypeStruct((8, BLOCK), jnp.float32)],
+        + [jax.ShapeDtypeStruct((1, BLOCK), jnp.float32)],
         in_specs=[smem, smem, vmem] + [hbm] * (10 + len(previous)),
         out_specs=[hbm] * 6 + [vmem],
         scratch_shapes=[
@@ -323,7 +323,7 @@
         moved = [swap(part, "dp", mask) for part, mask in zip(packed, ORDER)]
         received.append((first, count, moved))
         first += count
-    results, outputs, sink_sum = [], [], jnp.zeros((8, BLOCK), jnp.float32)
+    results, outputs, sink_sum = [], [], jnp.zeros((1, BLOCK), jnp.float32)
     for num, (first, count, packed) in enumerate(received):
         *grads, sink_sum = attend(
             sink_logit, links, sink_sum, arrays, packed, received[0][2], outputs, first, count, heads_dev, score_scale

time: 64.9 us -> 64.7 us (level)
  no operation moved by 1% of the time
where the time goes in v5:
time: 64.7 us; the launch traced here: 64.5 us
  starting transfers between devices  25 us (39%)
  waiting for transfers between devices  21.2 us (33%)
  Pallas kernels  16.8 us (26%)
  between operations  0.82 us (1%)
    ppermute x17, starting transfers between devices, swap(): lax.ppermute(value, axis, [(i, i ^ mask) for i in range(lax.axis_size(axi...  25 us
    ppermute x17, waiting for transfers between devices, swap(): lax.ppermute(value, axis, [(i, i ^ mask) for i in range(lax.axis_size(axi...  21.2 us
    pallas_call x2, Pallas kernels, attend(): pl.pallas_call(functools.partial(attend_kernel, first_head, heads, heads_...  8.33 us
    pallas_call x2, Pallas kernels, pack(): pl.pallas_call(functools.partial(pack_kernel, offset, width, share, with_...  5.59 us
    pallas_call x2, Pallas kernels, unpack(): pl.pallas_call(functools.partial(unpack_kernel, offset, width, share), ou...  2.84 us
  transfers between devices with their start and end apart: 17, of which 7 were waited for; matrix products, arithmetic and copies ran while one was open for 1% of the time, Pallas kernels for 20%

profile of v5, /device:TPU:0, one launch (start us, length us, event | category | flops | bytes accessed | tf_op | source)
XLA Modules:
  0.0 64.5 jit_solution(12369770652643804854)
XLA Ops:
  0.6 2.7 %pack.2 = (bf16[528,256]{1,0:T(8,128)(2,1)}, bf16[528,256]{1,0:T(8,128)(2,1)}, bf16[528,256]{1,0:T(8,128)(2,1)}) custom-call(s32[2]{0:T(128)} %bitcast.5, bf16[1,128,2560]{2,1,0:T(8,128)(2,1)} %refs_0_.7, bf16[1,128,2560]{2,1,0:T(8,128)(2,1)} %refs_1_.7, bf16[1,128,2560]{2,1,0:T(8,128)(2,1)} %refs_2_.7, bf16[1,128,2560]{2,1,0:T(8,128)(2,1)} %refs_3_.7), custom_call_target="tpu_custom_call" | custom-call | bytes 1622016 | tf_op jit(solution)/shard_map/pack/pallas_call | solution.py:57
  3.4 4.0 %collective-permute-start.2 = (bf16[528,256]{1,0:T(8,128)(2,1)}, bf16[528,256]{1,0:T(8,128)(2,1)S(1)}, u32[]{:S(2)}, u32[]{:S(2)}) collective-permute-start(bf16[528,256]{1,0:T(8,128)(2,1)} %get-tuple-element.58), channel_id=1, source_target_pairs={{0,24},{8,16},{16,8},{24,0},{1,25},{9,17},{17,9},{25,1},{2,26},{10... | collective-permute-start | bytes 811016 | tf_op jit(solution)/shard_map/ppermute | solution.py:299
  7.3 2.9 %pack.3 = (bf16[512,384]{1,0:T(8,128)(2,1)}, bf16[512,384]{1,0:T(8,128)(2,1)}, bf16[512,384]{1,0:T(8,128)(2,1)}) custom-call(s32[2]{0:T(128)} %bitcast.6, bf16[1,128,2560]{2,1,0:T(8,128)(2,1)} %refs_0_.7, bf16[1,128,2560]{2,1,0:T(8,128)(2,1)} %refs_1_.7, bf16[1,128,2560]{2,1,0:T(8,128)(2,1)} %refs_2_.7, bf16[1,128,2560]{2,1,0:T(8,128)(2,1)} %refs_3_.7), custom_call_target="tpu_custom_call" | custom-call | bytes 2359296 | tf_op jit(solution)/shard_map/pack/pallas_call | solution.py:57
  10.5 1.8 %collective-permute-start.3 = (bf16[528,256]{1,0:T(8,128)(2,1)}, bf16[528,256]{1,0:T(8,128)(2,1)S(1)}, u32[]{:S(2)}, u32[]{:S(2)}) collective-permute-start(bf16[528,256]{1,0:T(8,128)(2,1)} %get-tuple-element.59), channel_id=1, source_target_pairs={{0,8},{8,0},{16,24},{24,16},{1,9},{9,1},{17,25},{25,17},{2,10},{10... | collective-permute-start | bytes 811016 | tf_op jit(solution)/shard_map/ppermute | solution.py:299
  12.3 1.5 %collective-permute-start.4 = (bf16[528,256]{1,0:T(8,128)(2,1)}, bf16[528,256]{1,0:T(8,128)(2,1)S(1)}, u32[]{:S(2)}, u32[]{:S(2)}) collective-permute-start(bf16[528,256]{1,0:T(8,128)(2,1)} %get-tuple-element.60), channel_id=1, source_target_pairs={{0,16},{8,24},{16,0},{24,8},{1,17},{9,25},{17,1},{25,9},{2,18},{10... | collective-permute-start | bytes 811016 | tf_op jit(solution)/shard_map/ppermute | solution.py:299
  14.6 2.4 %collective-permute-start.7 = (bf16[512,384]{1,0:T(8,128)(2,1)}, bf16[512,384]{1,0:T(8,128)(2,1)S(1)}, u32[]{:S(2)}, u32[]{:S(2)}) collective-permute-start(bf16[512,384]{1,0:T(8,128)(2,1)} %get-tuple-element.68), channel_id=1, source_target_pairs={{0,16},{8,24},{16,0},{24,8},{1,17},{9,25},{17,1},{25,9},{2,18},{10... | collective-permute-start | bytes 1179656 | tf_op jit(solution)/shard_map/ppermute | solution.py:299
  17.0 12.7 %collective-permute-done.3.refs_5_.refs_8_ = bf16[528,256]{1,0:T(8,128)(2,1)S(1)} collective-permute-done((bf16[528,256]{1,0:T(8,128)(2,1)}, bf16[528,256]{1,0:T(8,128)(2,1)S(1)}, u32[]{:S(2)}, u32[]{:S(2)}) %collective-permute-start.3) | collective-permute-done | bytes 270368 | tf_op jit(solution)/shard_map/ppermute | solution.py:299
  29.7 3.6 %attend.2 = (bf16[384,256]{1,0:T(8,128)(2,1)S(1)}, bf16[384,256]{1,0:T(8,128)(2,1)}, bf16[384,256]{1,0:T(8,128)(2,1)}, bf16[1,128,2560]{2,1,0:T(8,128)(2,1)}, bf...) custom-call(f32[20]{0:T(128)S(1)} %copy-done.5, s32[2]{0:T(128)S(1)} %bitcast.7, ...), custom_call_target="tpu_custom_call" | custom-call | tf_op jit(solution)/shard_map/attend/pallas_call | solution.py:230
  33.4 1.5 %collective-permute-start.8 = (bf16[384,256]{1,0:T(8,128)(2,1)S(1)}, bf16[384,256]{1,0:T(8,128)(2,1)S(1)}, u32[]{:S(2)}, u32[]{:S(2)}) collective-permute-start(bf16[384,256]{1,0:T(8,128)(2,1)S(1)} %get-tuple-element.73), channel_id=1, source_target_pairs={{0,24},{8,16},{16,8},{24,0},{1,25},{9,17},{17,9},{25,1},{2,26},{10... | collective-permute-start | bytes 589832 | tf_op jit(solution)/shard_map/ppermute | solution.py:299
  34.9 1.5 %collective-permute-start.13 = (bf16[384,256]{1,0:T(8,128)(2,1)}, bf16[384,256]{1,0:T(8,128)(2,1)S(1)}, u32[]{:S(2)}, u32[]{:S(2)}) collective-permute-start(bf16[384,256]{1,0:T(8,128)(2,1)} %get-tuple-element.78), channel_id=1, source_target_pairs={{0,16},{8,24},{16,0},{24,8},{1,17},{9,25},{17,1},{25,9},{2,18},{10... | collective-permute-start | bytes 589832 | tf_op jit(solution)/shard_map/ppermute | solution.py:299
  36.9 1.2 %collective-permute-done.6.refs_5_ = bf16[512,384]{1,0:T(8,128)(2,1)S(1)} collective-permute-done((bf16[512,384]{1,0:T(8,128)(2,1)}, bf16[512,384]{1,0:T(8,128)(2,1)S(1)}, u32[]{:S(2)}, u32[]{:S(2)}) %collective-permute-start.6) | collective-permute-done | bytes 393248 | tf_op jit(solution)/shard_map/ppermute | solution.py:299
  38.1 4.7 %attend.3 = (bf16[384,384]{1,0:T(8,128)(2,1)}, bf16[384,384]{1,0:T(8,128)(2,1)}, bf16[384,384]{1,0:T(8,128)(2,1)}, bf16[1,128,2560]{2,1,0:T(8,128)(2,1)}, bf16[1...) custom-call(f32[20]{0:T(128)S(1)} %copy-done.5, ...), custom_call_target="tpu_custom_call", output_to_operand_aliasing={{3}: (13, {}), {4}: (14, {}), {5}: (15, {})} | custom-call | tf_op jit(solution)/shard_map/attend/pallas_call | solution.py:230
  42.8 1.6 %collective-permute-start.12 = (f32[1,128]{1,0:T(1,128)S(1)}, f32[1,128]{1,0:T(1,128)S(1)}, u32[]{:S(2)}, u32[]{:S(2)}) collective-permute-start(f32[1,128]{1,0:T(1,128)S(1)} %get-tuple-element.77), channel_id=1, source_target_pairs={{0,2},{1,3},{2,0},{3,1},{4,6},{5,7},{6,4},{7,5},{8,10},{9,11},{10,... | collective-permute-start | bytes 1544 | tf_op jit(solution)/shard_map/ppermute | solution.py:299
  44.5 1.5 %collective-permute-start.10 = (bf16[384,384]{1,0:T(8,128)(2,1)}, bf16[384,384]{1,0:T(8,128)(2,1)S(1)}, u32[]{:S(2)}, u32[]{:S(2)}) collective-permute-start(bf16[384,384]{1,0:T(8,128)(2,1)} %get-tuple-element.75), channel_id=1, source_target_pairs={{0,8},{8,0},{16,24},{24,16},{1,9},{9,1},{17,25},{25,17},{2,10},{10... | collective-permute-start | bytes 884744 | tf_op jit(solution)/shard_map/ppermute | solution.py:299
  46.0 1.5 %collective-permute-start.11 = (bf16[384,384]{1,0:T(8,128)(2,1)}, bf16[384,384]{1,0:T(8,128)(2,1)S(1)}, u32[]{:S(2)}, u32[]{:S(2)}) collective-permute-start(bf16[384,384]{1,0:T(8,128)(2,1)} %get-tuple-element.76), channel_id=1, source_target_pairs={{0,16},{8,24},{16,0},{24,8},{1,17},{9,25},{17,1},{25,9},{2,18},{10... | collective-permute-start | bytes 884744 | tf_op jit(solution)/shard_map/ppermute | solution.py:299
  47.5 1.4 %collective-permute-start.9 = (bf16[384,384]{1,0:T(8,128)(2,1)}, bf16[384,384]{1,0:T(8,128)(2,1)S(1)}, u32[]{:S(2)}, u32[]{:S(2)}) collective-permute-start(bf16[384,384]{1,0:T(8,128)(2,1)} %get-tuple-element.74), channel_id=1, source_target_pairs={{0,24},{8,16},{16,8},{24,0},{1,25},{9,17},{17,9},{25,1},{2,26},{10... | collective-permute-start | bytes 884744 | tf_op jit(solution)/shard_map/ppermute | solution.py:299
  49.0 5.7 %while.10 = (s32[]{:T(128)}, f32[1,128]{1,0:T(1,128)S(1)}, s32[]{:T(128)}, s32[]{:T(128)}) while((s32[]{:T(128)}, f32[1,128]{1,0:T(1,128)S(1)}, s32[]{:T(128)}, s32[]{:T(128)}) %tuple.32), condition=%wide.region_1.0_spmd, body=%wide.region_0.0_spmd.sunk | while | flops 258 | bytes 7301 | solution.py:341
  50.2 2.6 %collective-permute-start.1 = (f32[1,128]{1,0:T(1,128)S(1)}, f32[1,128]{1,0:T(1,128)S(1)}, u32[]{:S(2)}, u32[]{:S(2)}) collective-permute-start(f32[1,128]{1,0:T(1,128)S(1)} %add.30), channel_id=1, source_target_pairs={{0,4},{1,5},{2,6},{3,7},{4,0},{5,1},{6,2},{7,3},{8,12},{9,13},{10,... | collective-permute-start | bytes 1544 | tf_op jit(solution)/shard_map/while/body/ppermute | solution.py:299
  52.7 1.9 %collective-permute-done.1 = f32[1,128]{1,0:T(1,128)S(1)} collective-permute-done((f32[1,128]{1,0:T(1,128)S(1)}, f32[1,128]{1,0:T(1,128)S(1)}, u32[]{:S(2)}, u32[]{:S(2)}) %collective-permute-start.1) | collective-permute-done | bytes 544 | tf_op jit(solution)/shard_map/while/body/ppermute | solution.py:299
  55.2 1.6 %unpack.2 = (bf16[1,128,2560]{2,1,0:T(8,128)(2,1)}, bf16[1,128,2560]{2,1,0:T(8,128)(2,1)}, bf16[1,128,2560]{2,1,0:T(8,128)(2,1)}) custom-call(bf16[384,256]{1,0:T(8,128)(2,1)S(1)} %collective-permute-done.8.refs_0_, bf16[384,256]{1,0:T(8,128)(2,1)S(1)} %collective-permute-done.15.refs_1_, ...), custom_call_target="tpu_custom_call", output_to_operand_aliasing={{0}: (3, {}), {1}: (4, {}), {2}: (5, {})} | custom-call | tf_op jit(solution)/shard_map/unpack/pallas_call | solution.py:281
  56.8 2.4 %collective-permute-done.14 = f32[1,128]{1,0:T(1,128)S(1)} collective-permute-done((f32[1,128]{1,0:T(1,128)S(1)}, f32[1,128]{1,0:T(1,128)S(1)}, u32[]{:S(2)}, u32[]{:S(2)}) %collective-permute-start.14) | collective-permute-done | bytes 544 | tf_op jit(solution)/shard_map/ppermute | solution.py:299
  59.2 1.8 %collective-permute-start.16 = (f32[1,128]{1,0:T(1,128)S(1)}, f32[1,128]{1,0:T(1,128)S(1)}, u32[]{:S(2)}, u32[]{:S(2)}) collective-permute-start(f32[1,128]{1,0:T(1,128)S(1)} %add.24), channel_id=1, source_target_pairs={{0,16},{8,24},{16,0},{24,8},{1,17},{9,25},{17,1},{25,9},{2,18},{10... | collective-permute-start | bytes 1544 | tf_op jit(solution)/shard_map/ppermute | solution.py:299
  61.0 1.8 %collective-permute-done.16 = f32[1,128]{1,0:T(1,128)S(1)} collective-permute-done((f32[1,128]{1,0:T(1,128)S(1)}, f32[1,128]{1,0:T(1,128)S(1)}, u32[]{:S(2)}, u32[]{:S(2)}) %collective-permute-start.16) | collective-permute-done | bytes 544 | tf_op jit(solution)/shard_map/ppermute | solution.py:299
  63.3 1.2 %unpack.3 = (bf16[1,128,2560]{2,1,0:T(8,128)(2,1)}, bf16[1,128,2560]{2,1,0:T(8,128)(2,1)}, bf16[1,128,2560]{2,1,0:T(8,128)(2,1)}) custom-call(bf16[384,384]{1,0:T(8,128)(2,1)S(1)} %collective-permute-done.9.refs_0_, bf16[384,384]{1,0:T(8,128)(2,1)S(1)} %collective-permute-done.10.refs_1_, ...), custom_call_target="tpu_custom_call", output_to_operand_aliasing={{0}: (3, {}), {1}: (4, {}), {2}: (5, {})} | custom-call | tf_op jit(solution)/shard_map/unpack/pallas_call | solution.py:281
  (36 shorter events, 3.9 us)
Async XLA Ops:
  3.3 26.4 %copy-start = (bf16[1,128,2560]{2,1,0:T(8,128)(2,1)S(1)}, bf16[1,128,2560]{2,1,0:T(8,128)(2,1)}, u32[]{:S(2)}) copy-start(bf16[1,128,2560]{2,1,0:T(8,128)(2,1)} %refs_0_.7) | copy-start | bytes 1966084
  3.3 26.4 %copy-start.1 = (bf16[1,128,2560]{2,1,0:T(8,128)(2,1)S(1)}, bf16[1,128,2560]{2,1,0:T(8,128)(2,1)}, u32[]{:S(2)}) copy-start(bf16[1,128,2560]{2,1,0:T(8,128)(2,1)} %refs_1_.7) | copy-start | bytes 1966084
  3.3 26.4 %copy-start.2 = (bf16[1,128,2560]{2,1,0:T(8,128)(2,1)S(1)}, bf16[1,128,2560]{2,1,0:T(8,128)(2,1)}, u32[]{:S(2)}) copy-start(bf16[1,128,2560]{2,1,0:T(8,128)(2,1)} %refs_2_.7) | copy-start | bytes 1966084
  3.4 26.4 %copy-start.3 = (bf16[1,128,2560]{2,1,0:T(8,128)(2,1)S(1)}, bf16[1,128,2560]{2,1,0:T(8,128)(2,1)}, u32[]{:S(2)}) copy-start(bf16[1,128,2560]{2,1,0:T(8,128)(2,1)} %refs_3_.7) | copy-start | bytes 1966084
  3.4 11.2 %collective-permute-start.2 = (bf16[528,256]{1,0:T(8,128)(2,1)}, bf16[528,256]{1,0:T(8,128)(2,1)S(1)}, u32[]{:S(2)}, u32[]{:S(2)}) collective-permute-start(bf16[528,256]{1,0:T(8,128)(2,1)} %get-tuple-element.58), channel_id=1, source_target_pairs={{0,24},{8,16},{16,8},{24,0},{1,25},{9,17},{17,9},{25,1},{2,26},{10... | collective-permute-start | bytes 811016 | tf_op jit(solution)/shard_map/ppermute | solution.py:299
  10.2 24.6 %collective-permute-start.5 = (bf16[512,384]{1,0:T(8,128)(2,1)}, bf16[512,384]{1,0:T(8,128)(2,1)S(1)}, u32[]{:S(2)}, u32[]{:S(2)}) collective-permute-start(bf16[512,384]{1,0:T(8,128)(2,1)} %get-tuple-element.64), channel_id=1, source_target_pairs={{0,24},{8,16},{16,8},{24,0},{1,25},{9,17},{17,9},{25,1},{2,26},{10... | collective-permute-start | bytes 1179656 | tf_op jit(solution)/shard_map/ppermute | solution.py:299
  10.5 19.2 %collective-permute-start.3 = (bf16[528,256]{1,0:T(8,128)(2,1)}, bf16[528,256]{1,0:T(8,128)(2,1)S(1)}, u32[]{:S(2)}, u32[]{:S(2)}) collective-permute-start(bf16[528,256]{1,0:T(8,128)(2,1)} %get-tuple-element.59), channel_id=1, source_target_pairs={{0,8},{8,0},{16,24},{24,16},{1,9},{9,1},{17,25},{25,17},{2,10},{10... | collective-permute-start | bytes 811016 | tf_op jit(solution)/shard_map/ppermute | solution.py:299
  12.3 17.4 %collective-permute-start.4 = (bf16[528,256]{1,0:T(8,128)(2,1)}, bf16[528,256]{1,0:T(8,128)(2,1)S(1)}, u32[]{:S(2)}, u32[]{:S(2)}) collective-permute-start(bf16[528,256]{1,0:T(8,128)(2,1)} %get-tuple-element.60), channel_id=1, source_target_pairs={{0,16},{8,24},{16,0},{24,8},{1,17},{9,25},{17,1},{25,9},{2,18},{10... | collective-permute-start | bytes 811016 | tf_op jit(solution)/shard_map/ppermute | solution.py:299
  13.8 24.3 %collective-permute-start.6 = (bf16[512,384]{1,0:T(8,128)(2,1)}, bf16[512,384]{1,0:T(8,128)(2,1)S(1)}, u32[]{:S(2)}, u32[]{:S(2)}) collective-permute-start(bf16[512,384]{1,0:T(8,128)(2,1)} %get-tuple-element.67), channel_id=1, source_target_pairs={{0,8},{8,0},{16,24},{24,16},{1,9},{9,1},{17,25},{25,17},{2,10},{10... | collective-permute-start | bytes 1179656 | tf_op jit(solution)/shard_map/ppermute | solution.py:299
  14.6 15.1 %copy-start.4 = (s32[2,1]{0,1:T(1,128)S(1)}, s32[2,1]{0,1:T(1,128)}, u32[]{:S(2)}) copy-start(s32[2,1]{0,1:T(1,128)} %param.12) | copy-start | bytes 28
  14.6 15.2 %copy-start.5 = (f32[20]{0:T(128)S(1)}, f32[20]{0:T(128)}, u32[]{:S(2)}) copy-start(f32[20]{0:T(128)} %sink.3) | copy-start | bytes 244
  14.6 23.5 %collective-permute-start.7 = (bf16[512,384]{1,0:T(8,128)(2,1)}, bf16[512,384]{1,0:T(8,128)(2,1)S(1)}, u32[]{:S(2)}, u32[]{:S(2)}) collective-permute-start(bf16[512,384]{1,0:T(8,128)(2,1)} %get-tuple-element.68), channel_id=1, source_target_pairs={{0,16},{8,24},{16,0},{24,8},{1,17},{9,25},{17,1},{25,9},{2,18},{10... | collective-permute-start | bytes 1179656 | tf_op jit(solution)/shard_map/ppermute | solution.py:299
  33.4 12.6 %collective-permute-start.8 = (bf16[384,256]{1,0:T(8,128)(2,1)S(1)}, bf16[384,256]{1,0:T(8,128)(2,1)S(1)}, u32[]{:S(2)}, u32[]{:S(2)}) collective-permute-start(bf16[384,256]{1,0:T(8,128)(2,1)S(1)} %get-tuple-element.73), channel_id=1, source_target_pairs={{0,24},{8,16},{16,8},{24,0},{1,25},{9,17},{17,9},{25,1},{2,26},{10... | collective-permute-start | bytes 589832 | tf_op jit(solution)/shard_map/ppermute | solution.py:299
  34.9 14.1 %collective-permute-start.13 = (bf16[384,256]{1,0:T(8,128)(2,1)}, bf16[384,256]{1,0:T(8,128)(2,1)S(1)}, u32[]{:S(2)}, u32[]{:S(2)}) collective-permute-start(bf16[384,256]{1,0:T(8,128)(2,1)} %get-tuple-element.78), channel_id=1, source_target_pairs={{0,16},{8,24},{16,0},{24,8},{1,17},{9,25},{17,1},{25,9},{2,18},{10... | collective-permute-start | bytes 589832 | tf_op jit(solution)/shard_map/ppermute | solution.py:299
  36.4 18.8 %collective-permute-start.15 = (bf16[384,256]{1,0:T(8,128)(2,1)}, bf16[384,256]{1,0:T(8,128)(2,1)S(1)}, u32[]{:S(2)}, u32[]{:S(2)}) collective-permute-start(bf16[384,256]{1,0:T(8,128)(2,1)} %get-tuple-element.82), channel_id=1, source_target_pairs={{0,8},{8,0},{16,24},{24,16},{1,9},{9,1},{17,25},{25,17},{2,10},{10... | collective-permute-start | bytes 589832 | tf_op jit(solution)/shard_map/ppermute | solution.py:299
  42.8 4.7 %collective-permute-start.12 = (f32[1,128]{1,0:T(1,128)S(1)}, f32[1,128]{1,0:T(1,128)S(1)}, u32[]{:S(2)}, u32[]{:S(2)}) collective-permute-start(f32[1,128]{1,0:T(1,128)S(1)} %get-tuple-element.77), channel_id=1, source_target_pairs={{0,2},{1,3},{2,0},{3,1},{4,6},{5,7},{6,4},{7,5},{8,10},{9,11},{10,... | collective-permute-start | bytes 1544 | tf_op jit(solution)/shard_map/ppermute | solution.py:299
  44.5 18.8 %collective-permute-start.10 = (bf16[384,384]{1,0:T(8,128)(2,1)}, bf16[384,384]{1,0:T(8,128)(2,1)S(1)}, u32[]{:S(2)}, u32[]{:S(2)}) collective-permute-start(bf16[384,384]{1,0:T(8,128)(2,1)} %get-tuple-element.75), channel_id=1, source_target_pairs={{0,8},{8,0},{16,24},{24,16},{1,9},{9,1},{17,25},{25,17},{2,10},{10... | collective-permute-start | bytes 884744 | tf_op jit(solution)/shard_map/ppermute | solution.py:299
  46.0 17.3 %collective-permute-start.11 = (bf16[384,384]{1,0:T(8,128)(2,1)}, bf16[384,384]{1,0:T(8,128)(2,1)S(1)}, u32[]{:S(2)}, u32[]{:S(2)}) collective-permute-start(bf16[384,384]{1,0:T(8,128)(2,1)} %get-tuple-element.76), channel_id=1, source_target_pairs={{0,16},{8,24},{16,0},{24,8},{1,17},{9,25},{17,1},{25,9},{2,18},{10... | collective-permute-start | bytes 884744 | tf_op jit(solution)/shard_map/ppermute | solution.py:299
  47.5 15.8 %collective-permute-start.9 = (bf16[384,384]{1,0:T(8,128)(2,1)}, bf16[384,384]{1,0:T(8,128)(2,1)S(1)}, u32[]{:S(2)}, u32[]{:S(2)}) collective-permute-start(bf16[384,384]{1,0:T(8,128)(2,1)} %get-tuple-element.74), channel_id=1, source_target_pairs={{0,24},{8,16},{16,8},{24,0},{1,25},{9,17},{17,9},{25,1},{2,26},{10... | collective-permute-start | bytes 884744 | tf_op jit(solution)/shard_map/ppermute | solution.py:299
  49.0 1.2 %collective-permute-start = (f32[1,128]{1,0:T(1,128)S(1)}, f32[1,128]{1,0:T(1,128)S(1)}, u32[]{:S(2)}, u32[]{:S(2)}) collective-permute-start(f32[1,128]{1,0:T(1,128)S(1)} %get-tuple-element.126), channel_id=1, source_target_pairs={{0,1},{1,0},{2,3},{3,2},{4,5},{5,4},{6,7},{7,6},{8,9},{9,8},{10,11... | collective-permute-start | bytes 1544 | tf_op jit(solution)/shard_map/while/body/ppermute | solution.py:299
  50.2 4.4 %collective-permute-start.1 = (f32[1,128]{1,0:T(1,128)S(1)}, f32[1,128]{1,0:T(1,128)S(1)}, u32[]{:S(2)}, u32[]{:S(2)}) collective-permute-start(f32[1,128]{1,0:T(1,128)S(1)} %add.30), channel_id=1, source_target_pairs={{0,4},{1,5},{2,6},{3,7},{4,0},{5,1},{6,2},{7,3},{8,12},{9,13},{10,... | collective-permute-start | bytes 1544 | tf_op jit(solution)/shard_map/while/body/ppermute | solution.py:299
  54.6 4.6 %collective-permute-start.14 = (f32[1,128]{1,0:T(1,128)S(1)}, f32[1,128]{1,0:T(1,128)S(1)}, u32[]{:S(2)}, u32[]{:S(2)}) collective-permute-start(f32[1,128]{1,0:T(1,128)S(1)} %get-tuple-element.80), channel_id=1, source_target_pairs={{0,8},{8,0},{16,24},{24,16},{1,9},{9,1},{17,25},{25,17},{2,10},{10... | collective-permute-start | bytes 1544 | tf_op jit(solution)/shard_map/ppermute | solution.py:299
  59.2 3.5 %collective-permute-start.16 = (f32[1,128]{1,0:T(1,128)S(1)}, f32[1,128]{1,0:T(1,128)S(1)}, u32[]{:S(2)}, u32[]{:S(2)}) collective-permute-start(f32[1,128]{1,0:T(1,128)S(1)} %add.24), channel_id=1, source_target_pairs={{0,16},{8,24},{16,0},{24,8},{1,17},{9,25},{17,1},{25,9},{2,18},{10... | collective-permute-start | bytes 1544 | tf_op jit(solution)/shard_map/ppermute | solution.py:299

commit v6 on v4

--- a/solution.py
+++ b/solution.py
@@ -333,7 +333,7 @@
             sink_sum = sink_sum + swap(sink_sum, "ctx", 2)
             grads[0], results[0][1][0] = after(grads[0], results[0][1][0])
         else:
-            for place in (1, 2):
+            for place in range(3):
                 grads[place], received[1][2][0] = after(grads[place], received[1][2][0])
         results.append((first, [swap(grad, "dp", mask) for grad, mask in zip(grads, ORDER)]))
     sink_sum, results[0][1][2] = after(sink_sum, results[0][1][2])

time: 64.9 us -> 64.9 us (level)
  no operation moved by 1% of the time
where the time goes in v6:
time: 64.9 us; the launch traced here: 64.6 us
  starting transfers between devices  25.1 us (39%)
  waiting for transfers between devices  21.4 us (33%)
  Pallas kernels  16.8 us (26%)
  between operations  0.83 us (1%)
    ppermute x17, starting transfers between devices, swap(): lax.ppermute(value, axis, [(i, i ^ mask) for i in range(lax.axis_size(axi...  25.1 us
    ppermute x17, waiting for transfers between devices, swap(): lax.ppermute(value, axis, [(i, i ^ mask) for i in range(lax.axis_size(axi...  21.4 us
    pallas_call x2, Pallas kernels, attend(): pl.pallas_call(functools.partial(attend_kernel, first_head, heads, heads_...  8.33 us
    pallas_call x2, Pallas kernels, pack(): pl.pallas_call(functools.partial(pack_kernel, offset, width, share, with_...  5.59 us
    pallas_call x2, Pallas kernels, unpack(): pl.pallas_call(functools.partial(unpack_kernel, offset, width, share), ou...  2.84 us
  transfers between devices with their start and end apart: 17, of which 7 were waited for; matrix products, arithmetic and copies ran while one was open for 1% of the time, Pallas kernels for 20%

profile of v6, /device:TPU:0, one launch (start us, length us, event | category | flops | bytes accessed | tf_op | source)
XLA Modules:
  0.0 64.6 jit_solution(15404415654868676635)
XLA Ops:
  0.6 2.7 %pack.2 = (bf16[528,256]{1,0:T(8,128)(2,1)}, bf16[528,256]{1,0:T(8,128)(2,1)}, bf16[528,256]{1,0:T(8,128)(2,1)}) custom-call(s32[2]{0:T(128)} %bitcast.5, bf16[1,128,2560]{2,1,0:T(8,128)(2,1)} %refs_0_.7, bf16[1,128,2560]{2,1,0:T(8,128)(2,1)} %refs_1_.7, bf16[1,128,2560]{2,1,0:T(8,128)(2,1)} %refs_2_.7, bf16[1,128,2560]{2,1,0:T(8,128)(2,1)} %refs_3_.7), custom_call_target="tpu_custom_call" | custom-call | bytes 1622016 | tf_op jit(solution)/shard_map/pack/pallas_call | solution.py:57
  3.4 4.0 %collective-permute-start.2 = (bf16[528,256]{1,0:T(8,128)(2,1)}, bf16[528,256]{1,0:T(8,128)(2,1)S(1)}, u32[]{:S(2)}, u32[]{:S(2)}) collective-permute-start(bf16[528,256]{1,0:T(8,128)(2,1)} %get-tuple-element.60), channel_id=1, source_target_pairs={{0,24},{8,16},{16,8},{24,0},{1,25},{9,17},{17,9},{25,1},{2,26},{10... | collective-permute-start | bytes 811016 | tf_op jit(solution)/shard_map/ppermute | solution.py:299
  7.3 2.9 %pack.3 = (bf16[512,384]{1,0:T(8,128)(2,1)}, bf16[512,384]{1,0:T(8,128)(2,1)}, bf16[512,384]{1,0:T(8,128)(2,1)}) custom-call(s32[2]{0:T(128)} %bitcast.6, bf16[1,128,2560]{2,1,0:T(8,128)(2,1)} %refs_0_.7, bf16[1,128,2560]{2,1,0:T(8,128)(2,1)} %refs_1_.7, bf16[1,128,2560]{2,1,0:T(8,128)(2,1)} %refs_2_.7, bf16[1,128,2560]{2,1,0:T(8,128)(2,1)} %refs_3_.7), custom_call_target="tpu_custom_call" | custom-call | bytes 2359296 | tf_op jit(solution)/shard_map/pack/pallas_call | solution.py:57
  10.5 1.8 %collective-permute-start.3 = (bf16[528,256]{1,0:T(8,128)(2,1)}, bf16[528,256]{1,0:T(8,128)(2,1)S(1)}, u32[]{:S(2)}, u32[]{:S(2)}) collective-permute-start(bf16[528,256]{1,0:T(8,128)(2,1)} %get-tuple-element.61), channel_id=1, source_target_pairs={{0,8},{8,0},{16,24},{24,16},{1,9},{9,1},{17,25},{25,17},{2,10},{10... | collective-permute-start | bytes 811016 | tf_op jit(solution)/shard_map/ppermute | solution.py:299
  12.3 1.5 %collective-permute-start.4 = (bf16[528,256]{1,0:T(8,128)(2,1)}, bf16[528,256]{1,0:T(8,128)(2,1)S(1)}, u32[]{:S(2)}, u32[]{:S(2)}) collective-permute-start(bf16[528,256]{1,0:T(8,128)(2,1)} %get-tuple-element.62), channel_id=1, source_target_pairs={{0,16},{8,24},{16,0},{24,8},{1,17},{9,25},{17,1},{25,9},{2,18},{10... | collective-permute-start | bytes 811016 | tf_op jit(solution)/shard_map/ppermute | solution.py:299
  14.6 2.4 %collective-permute-start.7 = (bf16[512,384]{1,0:T(8,128)(2,1)}, bf16[512,384]{1,0:T(8,128)(2,1)S(1)}, u32[]{:S(2)}, u32[]{:S(2)}) collective-permute-start(bf16[512,384]{1,0:T(8,128)(2,1)} %get-tuple-element.72), channel_id=1, source_target_pairs={{0,16},{8,24},{16,0},{24,8},{1,17},{9,25},{17,1},{25,9},{2,18},{10... | collective-permute-start | bytes 1179656 | tf_op jit(solution)/shard_map/ppermute | solution.py:299
  17.0 12.7 %collective-permute-done.3.refs_5_.refs_8_ = bf16[528,256]{1,0:T(8,128)(2,1)S(1)} collective-permute-done((bf16[528,256]{1,0:T(8,128)(2,1)}, bf16[528,256]{1,0:T(8,128)(2,1)S(1)}, u32[]{:S(2)}, u32[]{:S(2)}) %collective-permute-start.3) | collective-permute-done | bytes 270368 | tf_op jit(solution)/shard_map/ppermute | solution.py:299
  29.7 3.6 %attend.2 = (bf16[384,256]{1,0:T(8,128)(2,1)S(1)}, bf16[384,256]{1,0:T(8,128)(2,1)}, bf16[384,256]{1,0:T(8,128)(2,1)}, bf16[1,128,2560]{2,1,0:T(8,128)(2,1)}, bf...) custom-call(f32[20]{0:T(128)S(1)} %copy-done.5, s32[2]{0:T(128)S(1)} %bitcast.7, ...), custom_call_target="tpu_custom_call" | custom-call | tf_op jit(solution)/shard_map/attend/pallas_call | solution.py:230
  33.4 1.5 %collective-permute-start.8 = (bf16[384,256]{1,0:T(8,128)(2,1)S(1)}, bf16[384,256]{1,0:T(8,128)(2,1)S(1)}, u32[]{:S(2)}, u32[]{:S(2)}) collective-permute-start(bf16[384,256]{1,0:T(8,128)(2,1)S(1)} %get-tuple-element.77), channel_id=1, source_target_pairs={{0,24},{8,16},{16,8},{24,0},{1,25},{9,17},{17,9},{25,1},{2,26},{10... | collective-permute-start | bytes 589832 | tf_op jit(solution)/shard_map/ppermute | solution.py:299
  34.9 1.5 %collective-permute-start.13 = (bf16[384,256]{1,0:T(8,128)(2,1)}, bf16[384,256]{1,0:T(8,128)(2,1)S(1)}, u32[]{:S(2)}, u32[]{:S(2)}) collective-permute-start(bf16[384,256]{1,0:T(8,128)(2,1)} %get-tuple-element.82), channel_id=1, source_target_pairs={{0,16},{8,24},{16,0},{24,8},{1,17},{9,25},{17,1},{25,9},{2,18},{10... | collective-permute-start | bytes 589832 | tf_op jit(solution)/shard_map/ppermute | solution.py:299
  36.9 1.2 %collective-permute-done.6.refs_5_ = bf16[512,384]{1,0:T(8,128)(2,1)S(1)} collective-permute-done((bf16[512,384]{1,0:T(8,128)(2,1)}, bf16[512,384]{1,0:T(8,128)(2,1)S(1)}, u32[]{:S(2)}, u32[]{:S(2)}) %collective-permute-start.6) | collective-permute-done | bytes 393248 | tf_op jit(solution)/shard_map/ppermute | solution.py:299
  38.1 4.7 %attend.3 = (bf16[384,384]{1,0:T(8,128)(2,1)}, bf16[384,384]{1,0:T(8,128)(2,1)}, bf16[384,384]{1,0:T(8,128)(2,1)}, bf16[1,128,2560]{2,1,0:T(8,128)(2,1)}, bf16[1...) custom-call(f32[20]{0:T(128)S(1)} %copy-done.5, ...), custom_call_target="tpu_custom_call", output_to_operand_aliasing={{3}: (13, {}), {4}: (14, {}), {5}: (15, {})} | custom-call | tf_op jit(solution)/shard_map/attend/pallas_call | solution.py:230
  42.8 1.6 %collective-permute-start.12 = (f32[8,128]{1,0:T(8,128)S(1)}, f32[8,128]{1,0:T(8,128)S(1)}, u32[]{:S(2)}, u32[]{:S(2)}) collective-permute-start(f32[8,128]{1,0:T(8,128)S(1)} %get-tuple-element.81), channel_id=1, source_target_pairs={{0,2},{1,3},{2,0},{3,1},{4,6},{5,7},{6,4},{7,5},{8,10},{9,11},{10,... | collective-permute-start | bytes 12296 | tf_op jit(solution)/shard_map/ppermute | solution.py:299
  44.5 1.5 %collective-permute-start.10 = (bf16[384,384]{1,0:T(8,128)(2,1)}, bf16[384,384]{1,0:T(8,128)(2,1)S(1)}, u32[]{:S(2)}, u32[]{:S(2)}) collective-permute-start(bf16[384,384]{1,0:T(8,128)(2,1)} %get-tuple-element.79), channel_id=1, source_target_pairs={{0,8},{8,0},{16,24},{24,16},{1,9},{9,1},{17,25},{25,17},{2,10},{10... | collective-permute-start | bytes 884744 | tf_op jit(solution)/shard_map/ppermute | solution.py:299
  46.0 1.5 %collective-permute-start.11 = (bf16[384,384]{1,0:T(8,128)(2,1)}, bf16[384,384]{1,0:T(8,128)(2,1)S(1)}, u32[]{:S(2)}, u32[]{:S(2)}) collective-permute-start(bf16[384,384]{1,0:T(8,128)(2,1)} %get-tuple-element.80), channel_id=1, source_target_pairs={{0,16},{8,24},{16,0},{24,8},{1,17},{9,25},{17,1},{25,9},{2,18},{10... | collective-permute-start | bytes 884744 | tf_op jit(solution)/shard_map/ppermute | solution.py:299
  47.5 1.5 %collective-permute-start.9 = (bf16[384,384]{1,0:T(8,128)(2,1)}, bf16[384,384]{1,0:T(8,128)(2,1)S(1)}, u32[]{:S(2)}, u32[]{:S(2)}) collective-permute-start(bf16[384,384]{1,0:T(8,128)(2,1)} %get-tuple-element.78), channel_id=1, source_target_pairs={{0,24},{8,16},{16,8},{24,0},{1,25},{9,17},{17,9},{25,1},{2,26},{10... | collective-permute-start | bytes 884744 | tf_op jit(solution)/shard_map/ppermute | solution.py:299
  49.0 5.8 %while.10 = (s32[]{:T(128)}, f32[8,128]{1,0:T(8,128)S(1)}, s32[]{:T(128)}, s32[]{:T(128)}) while((s32[]{:T(128)}, f32[8,128]{1,0:T(8,128)S(1)}, s32[]{:T(128)}, s32[]{:T(128)}) %tuple.34), condition=%wide.region_1.0_spmd, body=%wide.region_0.0_spmd.sunk | while | flops 2050 | bytes 57477 | solution.py:341
  50.3 2.6 %collective-permute-start.1 = (f32[8,128]{1,0:T(8,128)S(1)}, f32[8,128]{1,0:T(8,128)S(1)}, u32[]{:S(2)}, u32[]{:S(2)}) collective-permute-start(f32[8,128]{1,0:T(8,128)S(1)} %add.30), channel_id=1, source_target_pairs={{0,4},{1,5},{2,6},{3,7},{4,0},{5,1},{6,2},{7,3},{8,12},{9,13},{10,... | collective-permute-start | bytes 12296 | tf_op jit(solution)/shard_map/while/body/ppermute | solution.py:299
  52.9 1.9 %collective-permute-done.1 = f32[8,128]{1,0:T(8,128)S(1)} collective-permute-done((f32[8,128]{1,0:T(8,128)S(1)}, f32[8,128]{1,0:T(8,128)S(1)}, u32[]{:S(2)}, u32[]{:S(2)}) %collective-permute-start.1) | collective-permute-done | bytes 4128 | tf_op jit(solution)/shard_map/while/body/ppermute | solution.py:299
  55.3 1.6 %unpack.2 = (bf16[1,128,2560]{2,1,0:T(8,128)(2,1)}, bf16[1,128,2560]{2,1,0:T(8,128)(2,1)}, bf16[1,128,2560]{2,1,0:T(8,128)(2,1)}) custom-call(bf16[384,256]{1,0:T(8,128)(2,1)S(1)} %collective-permute-done.8.refs_0_, bf16[384,256]{1,0:T(8,128)(2,1)S(1)} %collective-permute-done.15.refs_1_, ...), custom_call_target="tpu_custom_call", output_to_operand_aliasing={{0}: (3, {}), {1}: (4, {}), {2}: (5, {})} | custom-call | tf_op jit(solution)/shard_map/unpack/pallas_call | solution.py:281
  57.0 2.3 %collective-permute-done.14 = f32[8,128]{1,0:T(8,128)S(1)} collective-permute-done((f32[8,128]{1,0:T(8,128)S(1)}, f32[8,128]{1,0:T(8,128)S(1)}, u32[]{:S(2)}, u32[]{:S(2)}) %collective-permute-start.14) | collective-permute-done | bytes 4128 | tf_op jit(solution)/shard_map/ppermute | solution.py:299
  59.3 1.8 %collective-permute-start.16 = (f32[8,128]{1,0:T(8,128)S(1)}, f32[8,128]{1,0:T(8,128)S(1)}, u32[]{:S(2)}, u32[]{:S(2)}) collective-permute-start(f32[8,128]{1,0:T(8,128)S(1)} %add.24), channel_id=1, source_target_pairs={{0,16},{8,24},{16,0},{24,8},{1,17},{9,25},{17,1},{25,9},{2,18},{10... | collective-permute-start | bytes 12296 | tf_op jit(solution)/shard_map/ppermute | solution.py:299
  61.1 1.8 %collective-permute-done.16 = f32[8,128]{1,0:T(8,128)S(1)} collective-permute-done((f32[8,128]{1,0:T(8,128)S(1)}, f32[8,128]{1,0:T(8,128)S(1)}, u32[]{:S(2)}, u32[]{:S(2)}) %collective-permute-start.16) | collective-permute-done | bytes 4128 | tf_op jit(solution)/shard_map/ppermute | solution.py:299
  63.4 1.2 %unpack.3 = (bf16[1,128,2560]{2,1,0:T(8,128)(2,1)}, bf16[1,128,2560]{2,1,0:T(8,128)(2,1)}, bf16[1,128,2560]{2,1,0:T(8,128)(2,1)}) custom-call(bf16[384,384]{1,0:T(8,128)(2,1)S(1)} %collective-permute-done.9.refs_0_, bf16[384,384]{1,0:T(8,128)(2,1)S(1)} %collective-permute-done.10.refs_1_, ...), custom_call_target="tpu_custom_call", output_to_operand_aliasing={{0}: (3, {}), {1}: (4, {}), {2}: (5, {})} | custom-call | tf_op jit(solution)/shard_map/unpack/pallas_call | solution.py:281
  (36 shorter events, 3.9 us)
Async XLA Ops:
  3.3 26.4 %copy-start = (bf16[1,128,2560]{2,1,0:T(8,128)(2,1)S(1)}, bf16[1,128,2560]{2,1,0:T(8,128)(2,1)}, u32[]{:S(2)}) copy-start(bf16[1,128,2560]{2,1,0:T(8,128)(2,1)} %refs_0_.7) | copy-start | bytes 1966084
  3.3 26.4 %copy-start.1 = (bf16[1,128,2560]{2,1,0:T(8,128)(2,1)S(1)}, bf16[1,128,2560]{2,1,0:T(8,128)(2,1)}, u32[]{:S(2)}) copy-start(bf16[1,128,2560]{2,1,0:T(8,128)(2,1)} %refs_1_.7) | copy-start | bytes 1966084
  3.3 26.4 %copy-start.2 = (bf16[1,128,2560]{2,1,0:T(8,128)(2,1)S(1)}, bf16[1,128,2560]{2,1,0:T(8,128)(2,1)}, u32[]{:S(2)}) copy-start(bf16[1,128,2560]{2,1,0:T(8,128)(2,1)} %refs_2_.7) | copy-start | bytes 1966084
  3.4 26.4 %copy-start.3 = (bf16[1,128,2560]{2,1,0:T(8,128)(2,1)S(1)}, bf16[1,128,2560]{2,1,0:T(8,128)(2,1)}, u32[]{:S(2)}) copy-start(bf16[1,128,2560]{2,1,0:T(8,128)(2,1)} %refs_3_.7) | copy-start | bytes 1966084
  3.4 11.2 %collective-permute-start.2 = (bf16[528,256]{1,0:T(8,128)(2,1)}, bf16[528,256]{1,0:T(8,128)(2,1)S(1)}, u32[]{:S(2)}, u32[]{:S(2)}) collective-permute-start(bf16[528,256]{1,0:T(8,128)(2,1)} %get-tuple-element.60), channel_id=1, source_target_pairs={{0,24},{8,16},{16,8},{24,0},{1,25},{9,17},{17,9},{25,1},{2,26},{10... | collective-permute-start | bytes 811016 | tf_op jit(solution)/shard_map/ppermute | solution.py:299
  10.2 23.1 %collective-permute-start.5 = (bf16[512,384]{1,0:T(8,128)(2,1)}, bf16[512,384]{1,0:T(8,128)(2,1)S(1)}, u32[]{:S(2)}, u32[]{:S(2)}) collective-permute-start(bf16[512,384]{1,0:T(8,128)(2,1)} %get-tuple-element.67), channel_id=1, source_target_pairs={{0,24},{8,16},{16,8},{24,0},{1,25},{9,17},{17,9},{25,1},{2,26},{10... | collective-permute-start | bytes 1179656 | tf_op jit(solution)/shard_map/ppermute | solution.py:299
  10.5 19.2 %collective-permute-start.3 = (bf16[528,256]{1,0:T(8,128)(2,1)}, bf16[528,256]{1,0:T(8,128)(2,1)S(1)}, u32[]{:S(2)}, u32[]{:S(2)}) collective-permute-start(bf16[528,256]{1,0:T(8,128)(2,1)} %get-tuple-element.61), channel_id=1, source_target_pairs={{0,8},{8,0},{16,24},{24,16},{1,9},{9,1},{17,25},{25,17},{2,10},{10... | collective-permute-start | bytes 811016 | tf_op jit(solution)/shard_map/ppermute | solution.py:299
  12.3 17.4 %collective-permute-start.4 = (bf16[528,256]{1,0:T(8,128)(2,1)}, bf16[528,256]{1,0:T(8,128)(2,1)S(1)}, u32[]{:S(2)}, u32[]{:S(2)}) collective-permute-start(bf16[528,256]{1,0:T(8,128)(2,1)} %get-tuple-element.62), channel_id=1, source_target_pairs={{0,16},{8,24},{16,0},{24,8},{1,17},{9,25},{17,1},{25,9},{2,18},{10... | collective-permute-start | bytes 811016 | tf_op jit(solution)/shard_map/ppermute | solution.py:299
  13.8 24.3 %collective-permute-start.6 = (bf16[512,384]{1,0:T(8,128)(2,1)}, bf16[512,384]{1,0:T(8,128)(2,1)S(1)}, u32[]{:S(2)}, u32[]{:S(2)}) collective-permute-start(bf16[512,384]{1,0:T(8,128)(2,1)} %get-tuple-element.71), channel_id=1, source_target_pairs={{0,8},{8,0},{16,24},{24,16},{1,9},{9,1},{17,25},{25,17},{2,10},{10... | collective-permute-start | bytes 1179656 | tf_op jit(solution)/shard_map/ppermute | solution.py:299
  14.6 15.1 %copy-start.4 = (s32[2,1]{0,1:T(1,128)S(1)}, s32[2,1]{0,1:T(1,128)}, u32[]{:S(2)}) copy-start(s32[2,1]{0,1:T(1,128)} %param.12) | copy-start | bytes 28
  14.6 15.2 %copy-start.5 = (f32[20]{0:T(128)S(1)}, f32[20]{0:T(128)}, u32[]{:S(2)}) copy-start(f32[20]{0:T(128)} %sink.3) | copy-start | bytes 244
  14.6 23.5 %collective-permute-start.7 = (bf16[512,384]{1,0:T(8,128)(2,1)}, bf16[512,384]{1,0:T(8,128)(2,1)S(1)}, u32[]{:S(2)}, u32[]{:S(2)}) collective-permute-start(bf16[512,384]{1,0:T(8,128)(2,1)} %get-tuple-element.72), channel_id=1, source_target_pairs={{0,16},{8,24},{16,0},{24,8},{1,17},{9,25},{17,1},{25,9},{2,18},{10... | collective-permute-start | bytes 1179656 | tf_op jit(solution)/shard_map/ppermute | solution.py:299
  33.4 12.6 %collective-permute-start.8 = (bf16[384,256]{1,0:T(8,128)(2,1)S(1)}, bf16[384,256]{1,0:T(8,128)(2,1)S(1)}, u32[]{:S(2)}, u32[]{:S(2)}) collective-permute-start(bf16[384,256]{1,0:T(8,128)(2,1)S(1)} %get-tuple-element.77), channel_id=1, source_target_pairs={{0,24},{8,16},{16,8},{24,0},{1,25},{9,17},{17,9},{25,1},{2,26},{10... | collective-permute-start | bytes 589832 | tf_op jit(solution)/shard_map/ppermute | solution.py:299
  34.9 14.1 %collective-permute-start.13 = (bf16[384,256]{1,0:T(8,128)(2,1)}, bf16[384,256]{1,0:T(8,128)(2,1)S(1)}, u32[]{:S(2)}, u32[]{:S(2)}) collective-permute-start(bf16[384,256]{1,0:T(8,128)(2,1)} %get-tuple-element.82), channel_id=1, source_target_pairs={{0,16},{8,24},{16,0},{24,8},{1,17},{9,25},{17,1},{25,9},{2,18},{10... | collective-permute-start | bytes 589832 | tf_op jit(solution)/shard_map/ppermute | solution.py:299
  36.4 18.9 %collective-permute-start.15 = (bf16[384,256]{1,0:T(8,128)(2,1)}, bf16[384,256]{1,0:T(8,128)(2,1)S(1)}, u32[]{:S(2)}, u32[]{:S(2)}) collective-permute-start(bf16[384,256]{1,0:T(8,128)(2,1)} %get-tuple-element.86), channel_id=1, source_target_pairs={{0,8},{8,0},{16,24},{24,16},{1,9},{9,1},{17,25},{25,17},{2,10},{10... | collective-permute-start | bytes 589832 | tf_op jit(solution)/shard_map/ppermute | solution.py:299
  42.8 4.7 %collective-permute-start.12 = (f32[8,128]{1,0:T(8,128)S(1)}, f32[8,128]{1,0:T(8,128)S(1)}, u32[]{:S(2)}, u32[]{:S(2)}) collective-permute-start(f32[8,128]{1,0:T(8,128)S(1)} %get-tuple-element.81), channel_id=1, source_target_pairs={{0,2},{1,3},{2,0},{3,1},{4,6},{5,7},{6,4},{7,5},{8,10},{9,11},{10,... | collective-permute-start | bytes 12296 | tf_op jit(solution)/shard_map/ppermute | solution.py:299
  44.5 19.0 %collective-permute-start.10 = (bf16[384,384]{1,0:T(8,128)(2,1)}, bf16[384,384]{1,0:T(8,128)(2,1)S(1)}, u32[]{:S(2)}, u32[]{:S(2)}) collective-permute-start(bf16[384,384]{1,0:T(8,128)(2,1)} %get-tuple-element.79), channel_id=1, source_target_pairs={{0,8},{8,0},{16,24},{24,16},{1,9},{9,1},{17,25},{25,17},{2,10},{10... | collective-permute-start | bytes 884744 | tf_op jit(solution)/shard_map/ppermute | solution.py:299
  46.0 17.5 %collective-permute-start.11 = (bf16[384,384]{1,0:T(8,128)(2,1)}, bf16[384,384]{1,0:T(8,128)(2,1)S(1)}, u32[]{:S(2)}, u32[]{:S(2)}) collective-permute-start(bf16[384,384]{1,0:T(8,128)(2,1)} %get-tuple-element.80), channel_id=1, source_target_pairs={{0,16},{8,24},{16,0},{24,8},{1,17},{9,25},{17,1},{25,9},{2,18},{10... | collective-permute-start | bytes 884744 | tf_op jit(solution)/shard_map/ppermute | solution.py:299
  47.5 15.9 %collective-permute-start.9 = (bf16[384,384]{1,0:T(8,128)(2,1)}, bf16[384,384]{1,0:T(8,128)(2,1)S(1)}, u32[]{:S(2)}, u32[]{:S(2)}) collective-permute-start(bf16[384,384]{1,0:T(8,128)(2,1)} %get-tuple-element.78), channel_id=1, source_target_pairs={{0,24},{8,16},{16,8},{24,0},{1,25},{9,17},{17,9},{25,1},{2,26},{10... | collective-permute-start | bytes 884744 | tf_op jit(solution)/shard_map/ppermute | solution.py:299
  49.0 1.2 %collective-permute-start = (f32[8,128]{1,0:T(8,128)S(1)}, f32[8,128]{1,0:T(8,128)S(1)}, u32[]{:S(2)}, u32[]{:S(2)}) collective-permute-start(f32[8,128]{1,0:T(8,128)S(1)} %get-tuple-element.130), channel_id=1, source_target_pairs={{0,1},{1,0},{2,3},{3,2},{4,5},{5,4},{6,7},{7,6},{8,9},{9,8},{10,11... | collective-permute-start | bytes 12296 | tf_op jit(solution)/shard_map/while/body/ppermute | solution.py:299
  50.3 4.5 %collective-permute-start.1 = (f32[8,128]{1,0:T(8,128)S(1)}, f32[8,128]{1,0:T(8,128)S(1)}, u32[]{:S(2)}, u32[]{:S(2)}) collective-permute-start(f32[8,128]{1,0:T(8,128)S(1)} %add.30), channel_id=1, source_target_pairs={{0,4},{1,5},{2,6},{3,7},{4,0},{5,1},{6,2},{7,3},{8,12},{9,13},{10,... | collective-permute-start | bytes 12296 | tf_op jit(solution)/shard_map/while/body/ppermute | solution.py:299
  54.8 4.5 %collective-permute-start.14 = (f32[8,128]{1,0:T(8,128)S(1)}, f32[8,128]{1,0:T(8,128)S(1)}, u32[]{:S(2)}, u32[]{:S(2)}) collective-permute-start(f32[8,128]{1,0:T(8,128)S(1)} %get-tuple-element.84), channel_id=1, source_target_pairs={{0,8},{8,0},{16,24},{24,16},{1,9},{9,1},{17,25},{25,17},{2,10},{10... | collective-permute-start | bytes 12296 | tf_op jit(solution)/shard_map/ppermute | solution.py:299
  59.3 3.6 %collective-permute-start.16 = (f32[8,128]{1,0:T(8,128)S(1)}, f32[8,128]{1,0:T(8,128)S(1)}, u32[]{:S(2)}, u32[]{:S(2)}) collective-permute-start(f32[8,128]{1,0:T(8,128)S(1)} %add.24), channel_id=1, source_target_pairs={{0,16},{8,24},{16,0},{24,8},{1,17},{9,25},{17,1},{25,9},{2,18},{10... | collective-permute-start | bytes 12296 | tf_op jit(solution)/shard_map/ppermute | solution.py:299
